TPU v7x, 32 devices: a whole 2x2x4 slice. The times are simulated.
32 devices in a mesh: ctx: 4 (over z), exp: 8 (over y, x, core).
Axes of the slice: x: 2, y: 2, z: 4, core: 2. Of those that a mesh axis runs over, the one named last changes fastest.
Arguments:
- tokens: bfloat16 [8, 2048, 1024], P('exp', 'ctx'), may hold values from -6 to 6
- w_query: bfloat16 [1024, 1024], P(('ctx', 'exp')), may hold values from -0.1875 to 0.1875
- w_key: bfloat16 [1024, 1024], P(('ctx', 'exp')), may hold values from -0.1875 to 0.1875
- w_value: bfloat16 [1024, 1024], P(('ctx', 'exp')), may hold values from -0.1875 to 0.1875
- w_out: bfloat16 [1024, 1024], P(('ctx', 'exp')), may hold values from -0.75 to 0.75
- w_router: bfloat16 [1024, 8], P(('ctx', 'exp')), may hold values from -0.125 to 0.125
- gain_attn: bfloat16 [1024], P(('ctx', 'exp')), may hold values from 0.5 to 1.5
- gain_mlp: bfloat16 [1024], P(('ctx', 'exp')), may hold values from 0.5 to 1.5
- pos_bias: bfloat16 [512], P(('ctx', 'exp')), may hold values from -5 to 5
- exp_gate: bfloat16 [8, 1024, 2816], P('exp', 'ctx'), may hold values from -0.1875 to 0.1875
- exp_up: bfloat16 [8, 1024, 2816], P('exp', 'ctx'), may hold values from -0.1875 to 0.1875
- exp_down: bfloat16 [8, 2816, 1024], P('exp', 'ctx'), may hold values from -0.109375 to 0.109375
- doc_lengths: int32 [8, 8], P('exp'), may hold values from 1 to 2048, as said below
- bucket_of: int32 [1024], replicated, may hold values from 0 to 31
- expert_ids: int32 [8, 2048, 2], P('exp', 'ctx'), may hold values from 0 to 7, all different within a row; in each aligned block of 512 rows (0 to 511, 512 to 1023, ..., all dimensions but the last counted through in order) at most 160 rows name the same one
- cotangent: bfloat16 [8, 2048, 1024], P('exp', 'ctx'), may hold values from -6 to 6
Outputs:
- output: bfloat16 [8, 2048, 1024], P('exp', 'ctx')
- input_grad: float32 [8, 2048, 1024], P('exp', 'ctx')
- grad_query: float32 [1024, 1024], P(('ctx', 'exp'))
- grad_key: float32 [1024, 1024], P(('ctx', 'exp'))
- grad_value: float32 [1024, 1024], P(('ctx', 'exp'))
- grad_out: float32 [1024, 1024], P(('ctx', 'exp'))
- grad_router: float32 [1024, 8], P(('ctx', 'exp'))
- grad_gain_attn: float32 [1024], P(('ctx', 'exp'))
- grad_gain_mlp: float32 [1024], P(('ctx', 'exp'))
- grad_pos_bias: float32 [512], P(('ctx', 'exp'))
- grad_gate: float32 [8, 1024, 2816], P('exp', 'ctx')
- grad_up: float32 [8, 1024, 2816], P('exp', 'ctx')
- grad_down: float32 [8, 2816, 1024], P('exp', 'ctx')
Inputs may be any that keep to these rules, and one draw needn't show every extreme that they name: `doc_lengths`: the 8 lengths of a sequence sum to 2048. `expert_ids`: a token names 2 different experts; among the 512 tokens of one aligned token block no expert is named more than 160 times.
All inputs are finite; a program needn't handle non-finite values.
Results may differ from a plain program's by a relative error of at most 0.017.
Values may be sent and summed in bfloat16 or wider, within the bound.
A program may use at most 320 MiB of HBM per device.

v0:
```python
import jax
import jax.numpy as jnp
from jax import lax
from jax.sharding import PartitionSpec as P

HEADS = 16
HEAD_DIM = 64
BUCKETS = 32
TOP = 2
WINDOW = 1024


EPSILON = 1e-06
PRECISION_MAX = lax.Precision.HIGHEST


def from_behind(block, axis, distance):
    devices = range(lax.axis_size(axis))
    route = [(i - distance, i) for i in devices if i - distance in devices]
    return lax.ppermute(block, axis, route)


def norm_rows(values, gain):
    return values * lax.rsqrt(jnp.mean(values * values, axis=-1, keepdims=True) + EPSILON) * gain


def glu_part(gate_pre, up_pre):
    return jax.nn.gelu(gate_pre, approximate=True) * up_pre


def contract_rows(left, right):
    return lax.dot_general(
        left, right, (((0,), (0,)), ((), ())), preferred_element_type=jnp.float32
    )


def contract_last(left, right):
    return lax.dot_general(
        left, right, (((1,), (1,)), ((), ())), preferred_element_type=jnp.float32
    )


def body(
    tokens,
    w_query,
    w_key,
    w_value,
    w_out,
    w_router,
    gain_attn,
    gain_mlp,
    pos_bias,
    exp_gate,
    exp_up,
    exp_down,
    doc_lengths,
    bucket_of,
    expert_ids,
    cotangent,
):

    def fetch_dense():
        return (
            lax.all_gather(w_query, ("ctx", "exp"), axis=0, tiled=True),
            lax.all_gather(w_key, ("ctx", "exp"), axis=0, tiled=True),
            lax.all_gather(w_value, ("ctx", "exp"), axis=0, tiled=True),
            lax.all_gather(w_out, ("ctx", "exp"), axis=0, tiled=True),
            lax.all_gather(w_router, ("ctx", "exp"), axis=0, tiled=True),
            lax.all_gather(gain_attn, ("ctx", "exp"), axis=0, tiled=True),
            lax.all_gather(gain_mlp, ("ctx", "exp"), axis=0, tiled=True),
            lax.all_gather(pos_bias, ("ctx", "exp"), axis=0, tiled=True),
        )

    def fetch_experts():
        return (
            lax.all_gather(exp_gate, "ctx", axis=1, tiled=True),
            lax.all_gather(exp_up, "ctx", axis=1, tiled=True),
            lax.all_gather(exp_down, "ctx", axis=1, tiled=True),
        )

    inputs = tokens[0].astype(jnp.float32)
    rows_dev = inputs.shape[0]
    width = inputs.shape[1]
    experts = w_router.shape[1]
    capacity = (5 * TOP * rows_dev + 4 * experts - 1) // (4 * experts)
    reach = (WINDOW + rows_dev - 2) // rows_dev
    scale = HEAD_DIM ** (-0.5)

    def heads_of(array):
        return array.reshape(rows_dev, HEADS, HEAD_DIM)

    dense = fetch_dense()
    ctx_index = lax.axis_index("ctx")
    bias_table = dense[7].reshape(HEADS, BUCKETS)
    ends = jnp.cumsum(doc_lengths[0])
    local_steps = jnp.arange(rows_dev, dtype=jnp.int32)
    query_pos = ctx_index * rows_dev + local_steps
    query_doc = jnp.sum((query_pos[:, None] >= ends[None, :]).astype(jnp.int32), axis=1)
    bucket_range = jnp.arange(BUCKETS, dtype=jnp.int32)

    def bucket_map(stride):
        key_pos = (ctx_index - stride) * rows_dev + local_steps
        key_doc = jnp.sum((key_pos[:, None] >= ends[None, :]).astype(jnp.int32), axis=1)
        distance = query_pos[:, None] - key_pos[None, :]
        inside = (distance >= 0) & (distance < WINDOW)
        allowed = (key_pos[None, :] >= 0) & inside & (query_doc[:, None] == key_doc[None, :])
        picked_bucket = jnp.take(bucket_of, jnp.clip(distance, 0, WINDOW - 1))
        onehot_map = ((picked_bucket[..., None] == bucket_range) & inside[..., None]).astype(
            jnp.bfloat16
        )
        return (allowed, onehot_map)

    def masked_bias(allowed, onehot_map):
        bias = jnp.einsum("hb,tsb->hts", bias_table, onehot_map, preferred_element_type=jnp.float32)
        return jnp.where(allowed[None], bias, -1e30)

    normalized_input = norm_rows(inputs, dense[5].astype(jnp.float32)).astype(jnp.bfloat16)
    queries = jnp.dot(normalized_input, dense[0], preferred_element_type=jnp.float32).astype(
        jnp.bfloat16
    )
    keys = jnp.dot(normalized_input, dense[1], preferred_element_type=jnp.float32).astype(
        jnp.bfloat16
    )
    values = jnp.dot(normalized_input, dense[2], preferred_element_type=jnp.float32).astype(
        jnp.bfloat16
    )
    query_heads = heads_of(queries)
    scaled_heads = query_heads * jnp.asarray(scale, jnp.bfloat16)

    def scores_of(bias_block, key_heads):
        return (
            jnp.einsum("thd,shd->hts", scaled_heads, key_heads, preferred_element_type=jnp.float32)
            + bias_block
        )

    blocks = [jnp.stack([keys, values])]
    carried = blocks[0]
    for stride in range(1, reach + 1):
        carried = from_behind(carried, "ctx", 1)
        blocks.append(carried)
    maps = [bucket_map(stride) for stride in range(len(blocks))]
    biases = [masked_bias(entry[0], entry[1]) for entry in maps]
    score_list = [
        scores_of(biases[stride], heads_of(blocks[stride][0])) for stride in range(len(blocks))
    ]
    running = jnp.max(score_list[0], axis=-1)
    for stride in range(1, len(blocks)):
        running = jnp.maximum(running, jnp.max(score_list[stride], axis=-1))
    expos = [jnp.exp(block_scores - running[..., None]) for block_scores in score_list]
    totals = jnp.sum(expos[0], axis=-1)
    for stride in range(1, len(blocks)):
        totals = totals + jnp.sum(expos[stride], axis=-1)
    logsum = running + jnp.log(totals)
    inverse = 1.0 / totals
    attention_output = jnp.zeros((rows_dev, HEADS, HEAD_DIM), jnp.float32)
    for stride in range(len(blocks)):
        probs = (expos[stride] * inverse[..., None]).astype(jnp.bfloat16)
        attention_output = attention_output + jnp.einsum(
            "hts,shd->thd", probs, heads_of(blocks[stride][1]), preferred_element_type=jnp.float32
        )
    attn_low = attention_output.reshape(rows_dev, width).astype(jnp.bfloat16)
    middle = inputs + jnp.dot(attn_low, dense[3], preferred_element_type=jnp.float32)
    normalized_expert_input = norm_rows(middle, dense[6].astype(jnp.float32)).astype(jnp.bfloat16)
    router_scores = jnp.dot(
        normalized_expert_input.astype(jnp.float32),
        dense[4].astype(jnp.float32),
        precision=PRECISION_MAX,
    )
    choices_dev = expert_ids[0]
    picked = (choices_dev[..., None] == jnp.arange(experts, dtype=jnp.int32)).astype(jnp.float32)
    chosen = jnp.sum(picked * router_scores[:, None, :], axis=-1)
    gates = jax.nn.softmax(chosen, axis=-1)
    flat_ids = choices_dev.reshape(-1)
    onehot_int = (flat_ids[:, None] == jnp.arange(experts, dtype=jnp.int32)[None, :]).astype(
        jnp.int32
    )
    slots = jnp.sum(jnp.cumsum(onehot_int, axis=0) * onehot_int, axis=1) - 1
    source_rows = jnp.repeat(normalized_expert_input, TOP, axis=0)
    outbound = (
        jnp.zeros((experts, capacity, width), jnp.bfloat16).at[flat_ids, slots].set(source_rows)
    )
    arrived = lax.all_to_all(outbound, "exp", split_axis=0, concat_axis=0, tiled=True)
    expert_rows = arrived.reshape(-1, width)
    gathered = fetch_experts()
    gate_w = gathered[0][0]
    up_w = gathered[1][0]
    down_w = gathered[2][0]
    gate_pre = jnp.dot(expert_rows, gate_w, preferred_element_type=jnp.float32)
    up_pre = jnp.dot(expert_rows, up_w, preferred_element_type=jnp.float32)
    hidden = glu_part(gate_pre, up_pre).astype(jnp.bfloat16)
    produced = (
        jnp.dot(hidden, down_w, preferred_element_type=jnp.float32)
        .astype(jnp.bfloat16)
        .reshape(experts, capacity, width)
    )
    returned = lax.all_to_all(produced, "exp", split_axis=0, concat_axis=0, tiled=True)
    expert_out = returned[flat_ids, slots].reshape(rows_dev, TOP, width).astype(jnp.float32)
    result = middle + jnp.sum(gates[..., None] * expert_out, axis=1)
    output = result.astype(jnp.bfloat16)[None]
    dense = fetch_dense()
    gathered = fetch_experts()
    gate_w = gathered[0][0]
    up_w = gathered[1][0]
    down_w = gathered[2][0]
    upstream = cotangent[0].astype(jnp.float32)
    gate_grad = jnp.sum(upstream[:, None, :] * expert_out, axis=-1)
    chosen_grad = gates * (gate_grad - jnp.sum(gates * gate_grad, axis=-1, keepdims=True))
    logits_grad = jnp.sum(picked * chosen_grad[..., None], axis=1)
    router_grad = jnp.dot(
        normalized_expert_input.astype(jnp.float32).T, logits_grad, precision=PRECISION_MAX
    )
    normed_mlp_grad = jnp.dot(logits_grad, dense[4].astype(jnp.float32).T, precision=PRECISION_MAX)
    sent_grad = (gates[..., None] * upstream[:, None, :]).astype(jnp.bfloat16).reshape(-1, width)
    grad_outbound = (
        jnp.zeros((experts, capacity, width), jnp.bfloat16).at[flat_ids, slots].set(sent_grad)
    )
    grad_arrived = lax.all_to_all(
        grad_outbound, "exp", split_axis=0, concat_axis=0, tiled=True
    ).reshape(-1, width)
    gate_pre = jnp.dot(expert_rows, gate_w, preferred_element_type=jnp.float32)
    up_pre = jnp.dot(expert_rows, up_w, preferred_element_type=jnp.float32)
    activated, glu_pull = jax.vjp(glu_part, gate_pre, up_pre)
    hidden = activated.astype(jnp.bfloat16)
    hidden_grad = contract_last(grad_arrived, down_w)
    down_grad = contract_rows(hidden, grad_arrived)
    gate_pre_grad, up_pre_grad = glu_pull(hidden_grad)
    gate_pre_grad = gate_pre_grad.astype(jnp.bfloat16)
    up_pre_grad = up_pre_grad.astype(jnp.bfloat16)
    gate_w_grad = contract_rows(expert_rows, gate_pre_grad)
    up_w_grad = contract_rows(expert_rows, up_pre_grad)
    rows_grad = contract_last(gate_pre_grad, gate_w) + contract_last(up_pre_grad, up_w)
    rows_back = lax.all_to_all(
        rows_grad.reshape(experts, capacity, width).astype(jnp.bfloat16),
        "exp",
        split_axis=0,
        concat_axis=0,
        tiled=True,
    ).astype(jnp.float32)
    normed_mlp_grad = normed_mlp_grad + jnp.sum(
        rows_back[flat_ids, slots].reshape(rows_dev, TOP, width), axis=1
    )
    expert_grads = (
        lax.psum_scatter(
            gate_w_grad[None].astype(jnp.bfloat16), "ctx", scatter_dimension=1, tiled=True
        ).astype(jnp.float32),
        lax.psum_scatter(
            up_w_grad[None].astype(jnp.bfloat16), "ctx", scatter_dimension=1, tiled=True
        ).astype(jnp.float32),
        lax.psum_scatter(
            down_grad[None].astype(jnp.bfloat16), "ctx", scatter_dimension=1, tiled=True
        ).astype(jnp.float32),
    )
    unused_mid, second_pull = jax.vjp(norm_rows, middle, dense[6].astype(jnp.float32))
    middle_norm_grad, gain_mlp_grad = second_pull(normed_mlp_grad)
    middle_grad = upstream + middle_norm_grad
    branch_grad = middle_grad.astype(jnp.bfloat16)
    out_w_grad = contract_rows(attn_low, branch_grad)
    attended_grad = contract_last(branch_grad, dense[3]).astype(jnp.bfloat16)
    attended_grad_heads = heads_of(attended_grad)
    delta = jnp.einsum("thd,thd->ht", attended_grad_heads.astype(jnp.float32), attention_output)
    query_acc = jnp.zeros((rows_dev, HEADS, HEAD_DIM), jnp.float32)
    bias_bucket = jnp.zeros((HEADS, BUCKETS), jnp.float32)
    partial_blocks = []
    for stride in range(len(blocks)):
        key_heads = heads_of(blocks[stride][0])
        value_heads = heads_of(blocks[stride][1])
        scores = scores_of(biases[stride], key_heads)
        probs = jnp.exp(scores - logsum[..., None])
        prob_low = probs.astype(jnp.bfloat16)
        prob_grad = jnp.einsum(
            "thd,shd->hts", attended_grad_heads, value_heads, preferred_element_type=jnp.float32
        )
        score_grad = (probs * (prob_grad - delta[..., None])).astype(jnp.bfloat16)
        query_acc = query_acc + jnp.einsum(
            "hts,shd->thd", score_grad, key_heads, preferred_element_type=jnp.float32
        )
        key_part = (
            jnp.einsum("hts,thd->shd", score_grad, query_heads, preferred_element_type=jnp.float32)
            * scale
        )
        value_part = jnp.einsum(
            "hts,thd->shd", prob_low, attended_grad_heads, preferred_element_type=jnp.float32
        )
        bias_bucket = bias_bucket + jnp.einsum(
            "hts,tsb->hb", score_grad, maps[stride][1], preferred_element_type=jnp.float32
        )
        partial_blocks.append(
            jnp.stack([key_part.reshape(rows_dev, width), value_part.reshape(rows_dev, width)])
        )
    returning = None
    for stride in range(reach, 0, -1):
        if returning is None:
            returning = partial_blocks[stride]
        else:
            returning = returning + partial_blocks[stride]
        returning = from_behind(returning.astype(jnp.bfloat16), "ctx", -1).astype(returning.dtype)
    kv_total = partial_blocks[0] + returning
    key_grad = kv_total[0].astype(jnp.bfloat16)
    value_grad = kv_total[1].astype(jnp.bfloat16)
    query_grad = (query_acc * scale).reshape(rows_dev, width).astype(jnp.bfloat16)
    query_w_grad = contract_rows(normalized_input, query_grad)
    key_w_grad = contract_rows(normalized_input, key_grad)
    value_w_grad = contract_rows(normalized_input, value_grad)
    normed_grad = (
        contract_last(query_grad, dense[0])
        + contract_last(key_grad, dense[1])
        + contract_last(value_grad, dense[2])
    )
    unused_first, first_pull = jax.vjp(norm_rows, inputs, dense[5].astype(jnp.float32))
    input_norm_grad, gain_attn_grad = first_pull(normed_grad)
    input_grad = middle_grad + input_norm_grad
    bias_grad = bias_bucket.reshape(-1)
    dense_grads = (
        lax.psum_scatter(query_w_grad, ("ctx", "exp"), scatter_dimension=0, tiled=True),
        lax.psum_scatter(key_w_grad, ("ctx", "exp"), scatter_dimension=0, tiled=True),
        lax.psum_scatter(value_w_grad, ("ctx", "exp"), scatter_dimension=0, tiled=True),
        lax.psum_scatter(out_w_grad, ("ctx", "exp"), scatter_dimension=0, tiled=True),
        lax.psum_scatter(router_grad, ("ctx", "exp"), scatter_dimension=0, tiled=True),
        lax.psum_scatter(gain_attn_grad, ("ctx", "exp"), scatter_dimension=0, tiled=True),
        lax.psum_scatter(gain_mlp_grad, ("ctx", "exp"), scatter_dimension=0, tiled=True),
        lax.psum_scatter(bias_grad, ("ctx", "exp"), scatter_dimension=0, tiled=True),
    )
    return (
        output,
        input_grad[None],
        dense_grads[0],
        dense_grads[1],
        dense_grads[2],
        dense_grads[3],
        dense_grads[4],
        dense_grads[5],
        dense_grads[6],
        dense_grads[7],
        expert_grads[0],
        expert_grads[1],
        expert_grads[2],
    )


def solution(mesh):
    placed = (
        P("exp", "ctx", None),
        P(("ctx", "exp"), None),
        P(("ctx", "exp"), None),
        P(("ctx", "exp"), None),
        P(("ctx", "exp"), None),
        P(("ctx", "exp"), None),
        P(("ctx", "exp")),
        P(("ctx", "exp")),
        P(("ctx", "exp")),
        P("exp", "ctx", None),
        P("exp", "ctx", None),
        P("exp", "ctx", None),
        P("exp", None),
        P(),
        P("exp", "ctx", None),
        P("exp", "ctx", None),
    )
    return jax.shard_map(
        body,
        mesh=mesh,
        in_specs=placed,
        out_specs=(
            P("exp", "ctx", None),
            P("exp", "ctx", None),
            P(("ctx", "exp"), None),
            P(("ctx", "exp"), None),
            P(("ctx", "exp"), None),
            P(("ctx", "exp"), None),
            P(("ctx", "exp"), None),
            P(("ctx", "exp")),
            P(("ctx", "exp")),
            P(("ctx", "exp")),
            P("exp", "ctx", None),
            P("exp", "ctx", None),
            P("exp", "ctx", None),
        ),
        check_vma=False,
    )
```

profile of v0, /device:TPU:0, one launch (start us, length us, event | category | flops | bytes accessed | tf_op | source)
XLA Modules:
  0.0 5831.2 jit_solution(8483254262866995736)
XLA Ops:
  21.0 1041.2 %gather_fusion.2 = s32[262144]{0:T(1024)S(1)} fusion(s32[1024]{0:T(1024)S(1)} %copy-done, s32[262144]{0:T(1024)S(1)} %broadcast_clamp_fusion.2), kind=kCustom, calls=%fused_computation.clone | custom fusion | bytes 3145728 | tf_op jit(solution)/shard_map/jit(_take)/gather | solution.py:107
  1063.8 1041.2 %gather_fusion.3 = s32[262144]{0:T(1024)S(1)} fusion(s32[1024]{0:T(1024)S(1)} %copy-done, s32[262144]{0:T(1024)S(1)} %broadcast_clamp_fusion.1), kind=kCustom, calls=%fused_computation.1.clone | custom fusion | bytes 3145728 | tf_op jit(solution)/shard_map/jit(_take)/gather | solution.py:107
  2106.6 2125.1 %gather_fusion.4 = s32[262144]{0:T(1024)} fusion(s32[1024]{0:T(1024)S(1)} %copy-done, s32[262144]{0:T(1024)S(1)} %broadcast_clamp_fusion), kind=kCustom, calls=%fused_computation.2.clone | custom fusion | bytes 3145728 | tf_op jit(solution)/shard_map/jit(_take)/gather | solution.py:107
  4240.4 42.3 all-reduce.7
  4359.2 21.2 fusion.187
  4387.7 21.4 fusion.188
  4413.7 21.6 fusion.186
  4435.3 18.0 fusion.28
  4501.5 61.5 %all-gather = bf16[32,32,8]{1,2,0:T(8,128)(2,1)S(1)} all-gather(bf16[1,32,8]{1,2,0:T(8,128)(2,1)S(1)} %bitcast.305), channel_id=1, replica_groups=mesh['ctx'=4,'exp'=8] {'ctx','exp'}, dimensions={0}, use_global_device_ids=true | all-gather | bytes 16896 | tf_op jit(solution)/shard_map/all_gather | solution.py:68
  4587.2 14.0 fusion.67
  4601.2 18.1 all-to-all-done.2
  4619.4 13.9 fusion.61
  4633.2 27.1 fusion.39
  4670.7 34.7 all_to_all.20
  4705.3 15.3 gather_fusion
  4802.0 36.2 all_to_all.21
  4841.1 20.5 gather_fusion.1
  4972.4 81.5 %collective-permute-done.2 = bf16[2,512,1024]{1,2,0:T(8,128)(2,1)} collective-permute-done((bf16[2,512,1024]{1,2,0:T(8,128)(2,1)}, bf16[2,512,1024]{1,2,0:T(8,128)(2,1)}, u32[]{:S(2)}, u32[]{:S(2)}) %collective-permute-start.2) | collective-permute-done | bytes 2097184 | tf_op jit(solution)/shard_map/ppermute | solution.py:20
  5071.2 81.7 %collective-permute-done.3 = bf16[2,512,1024]{1,2,0:T(8,128)(2,1)} collective-permute-done((bf16[2,512,1024]{1,2,0:T(8,128)(2,1)}, bf16[2,512,1024]{1,2,0:T(8,128)(2,1)}, u32[]{:S(2)}, u32[]{:S(2)}) %collective-permute-start.3) | collective-permute-done | bytes 2097184 | tf_op jit(solution)/shard_map/ppermute | solution.py:20
  5210.8 44.5 all-reduce.6
  5270.1 134.8 %reduce-scatter.17.cloned.1.call-done = f32[32,1024]{1,0:T(8,128)} async-done(((f32[1024,1024]{1,0:T(8,128)}), f32[32,1024]{1,0:T(8,128)}) %reduce-scatter.17.cloned.1.call-update) | async-done | bytes 131088 | tf_op jit(solution)/shard_map/reduce_scatter | solution.py:317
  5404.9 139.8 %reduce-scatter.11.cloned.1.call-done = f32[32,1024]{1,0:T(8,128)} async-done(((f32[1024,1024]{1,0:T(8,128)}), f32[32,1024]{1,0:T(8,128)}) %reduce-scatter.11.cloned.1.call-update) | async-done | bytes 131088 | tf_op jit(solution)/shard_map/reduce_scatter | solution.py:314
  5544.7 139.8 %reduce-scatter.13.cloned.1.call-done = f32[32,1024]{1,0:T(8,128)} async-done(((f32[1024,1024]{1,0:T(8,128)}), f32[32,1024]{1,0:T(8,128)}) %reduce-scatter.13.cloned.1.call-update) | async-done | bytes 131088 | tf_op jit(solution)/shard_map/reduce_scatter | solution.py:315
  5684.5 139.8 %reduce-scatter.15.cloned.1.call-done = f32[32,1024]{1,0:T(8,128)} async-done(((f32[1024,1024]{1,0:T(8,128)}), f32[32,1024]{1,0:T(8,128)}) %reduce-scatter.15.cloned.1.call-update) | async-done | bytes 131088 | tf_op jit(solution)/shard_map/reduce_scatter | solution.py:316
  (441 shorter events, 480.3 us)
Async XLA Ops:
  7.2 4290.0 %all-gather.13.cloned.1.call-start = ((), (), s32[]{:S(2)}) async-start(), calls=%async_computation.14 | async-start | bytes 2162688 | tf_op jit(solution)/shard_map/all_gather | solution.py:65
  8.0 4292.2 %all-gather.9.cloned.1.call-start = ((), (), s32[]{:S(2)}) async-start(), calls=%async_computation.12 | async-start | bytes 2162688 | tf_op jit(solution)/shard_map/all_gather | solution.py:66
  8.7 4337.3 %all-gather.11.cloned.1.call-start = ((), (), s32[]{:S(2)}) async-start(), calls=%async_computation.13 | async-start | bytes 2162688 | tf_op jit(solution)/shard_map/all_gather | solution.py:64
  9.4 4471.4 %all-gather.15.cloned.1.call-start = ((), (), s32[]{:S(2)}) async-start(), calls=%async_computation.15 | async-start | bytes 2162688 | tf_op jit(solution)/shard_map/all_gather | solution.py:67
  10.0 4577.2 %all-gather.19.cloned.1.call-start = ((), (), s32[]{:S(2)}) async-start(), calls=%async_computation.17 | async-start | bytes 7208960 | tf_op jit(solution)/shard_map/all_gather | solution.py:77
  10.6 4590.6 %all-gather.21.cloned.1.call-start = ((), (), s32[]{:S(2)}) async-start(), calls=%async_computation.18 | async-start | bytes 7208960 | tf_op jit(solution)/shard_map/all_gather | solution.py:78
  11.2 4622.1 %all-gather.17.cloned.1.call-start = ((), (), s32[]{:S(2)}) async-start(), calls=%async_computation.16 | async-start | bytes 7208960 | tf_op jit(solution)/shard_map/all_gather | solution.py:76
  2106.5 2127.5 %copy-start.50 = (s32[512,512]{1,0:T(8,128)S(1)}, s32[512,512]{1,0:T(8,128)}, u32[]{:S(2)}) copy-start(s32[512,512]{1,0:T(8,128)} %reshape.824) | copy-start | bytes 3145732
  2106.5 2127.5 %copy-start.51 = (s32[512,512]{1,0:T(8,128)S(1)}, s32[512,512]{1,0:T(8,128)}, u32[]{:S(2)}) copy-start(s32[512,512]{1,0:T(8,128)} %reshape.828) | copy-start | bytes 3145732
  2106.5 2127.5 %copy-start.72 = (s32[512]{0:T(512)S(1)}, s32[512]{0:T(512)}, u32[]{:S(2)}) copy-start(s32[512]{0:T(512)} %copy-done.71) | copy-start | bytes 6148
  4305.1 47.9 collective-permute-start
  4353.0 56.1 collective-permute-start.1
  4497.0 86.5 %all-to-all-start = ((bf16[8,160,1024]{2,1,0:T(8,128)(2,1)}), bf16[8,160,1024]{2,1,0:T(8,128)(2,1)}, u32[]{:S(2)}, u32[]{:S(2)}) async-start(bf16[8,160,1024]{2,1,0:T(8,128)(2,1)} %bitcast.274), calls=%async_computation | async-start | bytes 5242880 | tf_op jit(solution)/shard_map/all_to_all | solution.py:182
  4583.5 35.8 all-to-all-start.2
  4587.2 615.7 %reduce-scatter.25.cloned.1.call-start = ((), (), s32[]{:S(2)}) async-start(), calls=%async_computation.26 | async-start | bytes 540672
  4739.9 520.6 %reduce-scatter.23.cloned.1.call-start = ((), (), s32[]{:S(2)}) async-start(), calls=%async_computation.25 | async-start | bytes 7208960 | tf_op jit(solution)/shard_map/reduce_scatter | solution.py:249
  4752.3 511.5 %reduce-scatter.21.cloned.1.call-start = ((), (), s32[]{:S(2)}) async-start(), calls=%async_computation.24 | async-start | bytes 7208960 | tf_op jit(solution)/shard_map/reduce_scatter | solution.py:246
  4765.6 501.4 %reduce-scatter.19.cloned.1.call-start = ((), (), s32[]{:S(2)}) async-start(), calls=%async_computation.23 | async-start | bytes 7208960 | tf_op jit(solution)/shard_map/reduce_scatter | solution.py:243
  4778.7 626.3 %reduce-scatter.17.cloned.1.call-start = ((), (), s32[]{:S(2)}) async-start(), calls=%async_computation.22 | async-start | bytes 4325376 | tf_op jit(solution)/shard_map/reduce_scatter | solution.py:317
  4886.0 658.8 %reduce-scatter.11.cloned.1.call-start = ((), (), s32[]{:S(2)}) async-start(), calls=%async_computation.19 | async-start | bytes 4325376 | tf_op jit(solution)/shard_map/reduce_scatter | solution.py:314
  4942.2 742.3 %reduce-scatter.13.cloned.1.call-start = ((), (), s32[]{:S(2)}) async-start(), calls=%async_computation.20 | async-start | bytes 4325376 | tf_op jit(solution)/shard_map/reduce_scatter | solution.py:315
  4959.7 94.2 %collective-permute-start.2 = (bf16[2,512,1024]{1,2,0:T(8,128)(2,1)}, bf16[2,512,1024]{1,2,0:T(8,128)(2,1)}, u32[]{:S(2)}, u32[]{:S(2)}) collective-permute-start(bf16[2,512,1024]{1,2,0:T(8,128)(2,1)} %pad_maximum_fusion.1), channel_id=1, source_target_pairs={{8,0},{16,8},{24,16},{9,1},{17,9},{25,17},{10,2},{18,10},{26,18},{... | collective-permute-start | bytes 6291464 | tf_op jit(solution)/shard_map/ppermute | solution.py:20
  5057.7 95.2 %collective-permute-start.3 = (bf16[2,512,1024]{1,2,0:T(8,128)(2,1)}, bf16[2,512,1024]{1,2,0:T(8,128)(2,1)}, u32[]{:S(2)}, u32[]{:S(2)}) collective-permute-start(bf16[2,512,1024]{1,2,0:T(8,128)(2,1)} %fusion.75), channel_id=1, source_target_pairs={{8,0},{16,8},{24,16},{9,1},{17,9},{25,17},{10,2},{18,10},{26,18},{... | collective-permute-start | bytes 6291464 | tf_op jit(solution)/shard_map/ppermute | solution.py:20
  5160.1 664.1 %reduce-scatter.15.cloned.1.call-start = ((), (), s32[]{:S(2)}) async-start(), calls=%async_computation.21 | async-start | bytes 4325376 | tf_op jit(solution)/shard_map/reduce_scatter | solution.py:316
  (115 other events, 9030.0 us)
Sparse Core Ops, SparseCore 0:
  10.9 59.0 all-gather.12
  72.9 55.2 all-gather.8
  131.0 55.2 all-gather.10
  189.0 55.2 all-gather.14
  245.7 105.5 all-gather.18
  352.7 105.0 all-gather.20
  459.4 104.9 all-gather.16
  4740.0 131.0 reduce-scatter.24
  4873.6 105.1 reduce-scatter.22
  4981.0 170.8 reduce-scatter.20
  5154.3 106.3 reduce-scatter.18
  5263.5 141.3 reduce-scatter.16
  5407.9 136.8 reduce-scatter.10
  5547.5 136.9 reduce-scatter.12
  5687.3 136.9 reduce-scatter.14
where the time goes:
time: 5840 us; the launch traced here: 5830 us
  local copies, waits for them, and re-layouts  4340 us (74%)
  waiting for transfers between devices  741 us (13%)
  matrix products  407 us (7%)
  blocking collectives  219 us (4%)
  other arithmetic  90 us (2%)
    gather x6, local copies, waits for them, and re-layouts, bucket_map(): picked_bucket = jnp.take(bucket_of, jnp.clip(distance, 0, WINDOW - 1))  4210 us
    ppermute x4, waiting for transfers between devices, from_behind(): return lax.ppermute(block, axis, route)  165 us
    reduce_scatter x1, waiting for transfers between devices, body(): lax.psum_scatter(query_w_grad, ('ctx', 'exp'), scatter_dimension=0, tiled...  140 us
    reduce_scatter x1, waiting for transfers between devices, body(): lax.psum_scatter(key_w_grad, ('ctx', 'exp'), scatter_dimension=0, tiled=T...  140 us
    reduce_scatter x1, waiting for transfers between devices, body(): lax.psum_scatter(value_w_grad, ('ctx', 'exp'), scatter_dimension=0, tiled...  140 us
    reduce_scatter x1, waiting for transfers between devices, body(): lax.psum_scatter(out_w_grad, ('ctx', 'exp'), scatter_dimension=0, tiled=T...  135 us
  transfers between devices with their start and end apart: 21, of which 8 were waited for; matrix products, arithmetic and copies ran while one was open for 81% of the time, Pallas kernels for 0%

commit v1 on v0

v1 whole, which is shorter than its diff:
```python
import functools

import jax
import jax.numpy as jnp
from jax import lax
from jax.experimental import pallas as pl
from jax.experimental.pallas import tpu as pltpu
from jax.sharding import PartitionSpec as P

HEADS = 16
HEAD_DIM = 64
BUCKETS = 32
TOP = 2
WINDOW = 1024

EPSILON = 1e-06
NEGATIVE = -1e30
LANES = 128
CHUNK = 256
FF_TILE = 256
VMEM_LIMIT = 58 * 2**20
BF16 = jnp.bfloat16
F32 = jnp.float32


def shift_ctx(block, distance):
    devices = range(lax.axis_size("ctx"))
    route = [(i - distance, i) for i in devices if i - distance in devices]
    return lax.ppermute(block, "ctx", route)


def norm_rows(values, gain):
    return values * lax.rsqrt(jnp.mean(values * values, axis=-1, keepdims=True) + EPSILON) * gain


def dot(left, right):
    return jnp.dot(left, right, preferred_element_type=F32)


def dot_rows(left, right):
    return lax.dot_general(left, right, (((0,), (0,)), ((), ())), preferred_element_type=F32)


def dot_last(left, right):
    return lax.dot_general(left, right, (((1,), (1,)), ((), ())), preferred_element_type=F32)


def params(**more):
    return pltpu.CompilerParams(vmem_limit_bytes=VMEM_LIMIT, **more)


def band_kernel(bias_ref, band_ref):
    blocks = WINDOW // LANES
    for a in range(blocks + 1):
        upper = bias_ref[0, :, (blocks + 1 - a) * LANES : (blocks + 2 - a) * LANES]
        lower = bias_ref[0, :, (blocks - a) * LANES : (blocks + 1 - a) * LANES]
        row = jnp.concatenate([upper, lower], axis=1)
        wide = jnp.broadcast_to(row, (LANES, 2 * LANES))
        rolled = pltpu.roll(wide, 0, 1, stride=1, stride_axis=0)
        band_ref[0, a * LANES : (a + 1) * LANES, :] = rolled[:, :LANES]


def make_band(bias_dist):
    edge = jnp.full((HEADS, LANES), NEGATIVE, F32)
    padded = jnp.concatenate([edge, bias_dist, edge], axis=1)[:, None, :]
    return pl.pallas_call(
        band_kernel,
        grid=(HEADS,),
        in_specs=[pl.BlockSpec((1, 1, WINDOW + 2 * LANES), lambda h: (h, 0, 0))],
        out_specs=pl.BlockSpec((1, WINDOW + LANES, LANES), lambda h: (h, 0, 0)),
        out_shape=jax.ShapeDtypeStruct((HEADS, WINDOW + LANES, LANES), F32),
        compiler_params=params(),
        name="bias_band",
    )(padded)


def unband_kernel(band_ref, dist_ref):
    blocks = WINDOW // LANES
    row = lax.broadcasted_iota(jnp.int32, (LANES, LANES), 0)
    column = lax.broadcasted_iota(jnp.int32, (LANES, LANES), 1)
    flip = (row + column == LANES - 1).astype(F32)
    sums = [None] * (blocks + 2)
    for a in range(blocks + 1):
        block = band_ref[0, a * LANES : (a + 1) * LANES, :]
        block = jnp.dot(flip, block, precision=lax.Precision.HIGHEST, preferred_element_type=F32)
        wide = jnp.concatenate([block, jnp.zeros((LANES, LANES), F32)], axis=1)
        rolled = pltpu.roll(wide, LANES + 1, 1, stride=1, stride_axis=0)
        total = jnp.sum(rolled, axis=0, keepdims=True)
        for place, part in ((blocks + 1 - a, total[:, :LANES]), (blocks - a, total[:, LANES:])):
            sums[place] = part if sums[place] is None else sums[place] + part
    dist_ref[0, :, :] = jnp.concatenate(sums[1 : blocks + 1], axis=1)


def sum_band(band_grad):
    return pl.pallas_call(
        unband_kernel,
        grid=(HEADS,),
        in_specs=[pl.BlockSpec((1, WINDOW + LANES, LANES), lambda h: (h, 0, 0))],
        out_specs=pl.BlockSpec((1, 1, WINDOW), lambda h: (h, 0, 0)),
        out_shape=jax.ShapeDtypeStruct((HEADS, 1, WINDOW), F32),
        compiler_params=params(),
        name="bias_band_sums",
    )(band_grad)[:, 0, :]


def head_lanes(head):
    lane = lax.broadcasted_iota(jnp.int32, (1, 2 * HEAD_DIM), 1)
    return (lane >= head * HEAD_DIM) & (lane < (head + 1) * HEAD_DIM)


def masked_scores(head, start, q_ref, k_ref, qdoc_ref, kdoc_ref):
    span = WINDOW + CHUNK
    mine = head_lanes(head)
    q_rows, k_rows = pl.ds(start, CHUNK), pl.ds(start, span)
    q_part = jnp.where(mine, q_ref[q_rows, :], qdoc_ref[q_rows, :])
    k_part = jnp.where(mine, k_ref[k_rows, :], kdoc_ref[k_rows, :])
    return dot_last(k_part, q_part)


def sub_blocks():
    return [(s * LANES, WINDOW + LANES) for s in range(CHUNK // LANES)]


def spread(parts):
    span = WINDOW + CHUNK
    columns = []
    for (first, rows), part in zip(sub_blocks(), parts):
        pieces = []
        if first:
            pieces.append(jnp.zeros((first, LANES), part.dtype))
        pieces.append(part)
        if span - first - rows:
            pieces.append(jnp.zeros((span - first - rows, LANES), part.dtype))
        columns.append(jnp.concatenate(pieces, axis=0) if len(pieces) > 1 else part)
    return jnp.concatenate(columns, axis=1)


def attend_kernel(q_ref, k_ref, v_ref, qdoc_ref, kdoc_ref, band_ref, o_ref, lse_ref):
    span = WINDOW + CHUNK
    for start in range(0, q_ref.shape[0], CHUNK):
        v_turned = v_ref[pl.ds(start, span), :].T
        outs = []
        for head in range(2):
            scores = masked_scores(head, start, q_ref, k_ref, qdoc_ref, kdoc_ref)
            band = band_ref[head]
            low, scale, logs = [], [], []
            for s, (first, rows) in enumerate(sub_blocks()):
                part = scores[first : first + rows, s * LANES : (s + 1) * LANES] + band
                top = jnp.max(part, axis=0, keepdims=True)
                expo = jnp.exp(part - top)
                total = jnp.sum(expo, axis=0, keepdims=True)
                low.append(expo.astype(BF16))
                scale.append(1.0 / total)
                logs.append(top + jnp.log(total))
            out = dot(v_turned[head * HEAD_DIM : (head + 1) * HEAD_DIM], spread(low))
            outs.append(out * jnp.concatenate(scale, axis=1))
            lse_ref[0, head : head + 1, pl.ds(start, CHUNK)] = jnp.concatenate(logs, axis=1)
        o_ref[pl.ds(start, CHUNK), :] = jnp.concatenate(outs, axis=0).T.astype(BF16)


def attend(queries, keys, values, query_doc, key_doc, band):
    rows, width = queries.shape
    keys_rows = keys.shape[0]
    pairs = HEADS // 2
    wide = 2 * HEAD_DIM
    cost = pl.CostEstimate(
        flops=4 * rows * WINDOW * width * 4,
        bytes_accessed=2 * (2 * keys_rows + 2 * rows) * width + 4 * HEADS * WINDOW * LANES,
        transcendentals=HEADS * rows * WINDOW,
    )
    return pl.pallas_call(
        attend_kernel,
        grid=(pairs,),
        in_specs=[
            pl.BlockSpec((rows, wide), lambda p: (0, p)),
            pl.BlockSpec((keys_rows, wide), lambda p: (0, p)),
            pl.BlockSpec((keys_rows, wide), lambda p: (0, p)),
            pl.BlockSpec((rows, wide), lambda p: (0, 0)),
            pl.BlockSpec((keys_rows, wide), lambda p: (0, 0)),
            pl.BlockSpec((2, WINDOW + LANES, LANES), lambda p: (p, 0, 0)),
        ],
        out_specs=[
            pl.BlockSpec((rows, wide), lambda p: (0, p)),
            pl.BlockSpec((1, 2, rows), lambda p: (p, 0, 0)),
        ],
        out_shape=[
            jax.ShapeDtypeStruct((rows, width), BF16),
            jax.ShapeDtypeStruct((pairs, 2, rows), F32),
        ],
        compiler_params=params(),
        cost_estimate=cost,
        name="attend",
    )(queries, keys, values, query_doc, key_doc, band)


def attend_back_kernel(
    q_ref, k_ref, v_ref, g_ref, o_ref, lse_ref, qdoc_ref, kdoc_ref, band_ref,
    dq_ref, dk_ref, dv_ref, dband_ref, dk_sum, dv_sum,
):
    span = WINDOW + CHUNK
    dk_sum[...] = jnp.zeros_like(dk_sum)
    dv_sum[...] = jnp.zeros_like(dv_sum)
    for start in range(0, q_ref.shape[0], CHUNK):
        q_rows, k_rows = pl.ds(start, CHUNK), pl.ds(start, span)
        k_turned = k_ref[k_rows, :].T
        product = (g_ref[q_rows, :].astype(F32) * o_ref[q_rows, :].astype(F32)).T
        dq_parts = []
        for head in range(2):
            mine = head_lanes(head)
            zero = jnp.zeros((), BF16)
            scores = masked_scores(head, start, q_ref, k_ref, qdoc_ref, kdoc_ref)
            g_part = jnp.where(mine, g_ref[q_rows, :], zero)
            q_part = jnp.where(mine, q_ref[q_rows, :], zero)
            prob_grad = dot_last(v_ref[k_rows, :], g_part)
            delta = jnp.sum(product[head * HEAD_DIM : (head + 1) * HEAD_DIM], axis=0, keepdims=True)
            lse = lse_ref[0, head : head + 1, q_rows]
            band = band_ref[head]
            prob_low, grad_low, grad_sum = [], [], None
            for s, (first, rows) in enumerate(sub_blocks()):
                lanes = slice(s * LANES, (s + 1) * LANES)
                probs = jnp.exp(scores[first : first + rows, lanes] + band - lse[:, lanes])
                grad = probs * (prob_grad[first : first + rows, lanes] - delta[:, lanes])
                prob_low.append(probs.astype(BF16))
                grad_low.append(grad.astype(BF16))
                grad_sum = grad if grad_sum is None else grad_sum + grad
            if start == 0:
                dband_ref[head] = grad_sum
            else:
                dband_ref[head] = dband_ref[head] + grad_sum
            grads = spread(grad_low)
            dk_sum[k_rows, :] += dot(grads, q_part)
            dv_sum[k_rows, :] += dot(spread(prob_low), g_part)
            dq_parts.append(dot(k_turned[head * HEAD_DIM : (head + 1) * HEAD_DIM], grads))
        turned = jnp.concatenate(dq_parts, axis=0).T
        dq_ref[q_rows, :] = (turned * HEAD_DIM ** (-0.5)).astype(BF16)
    dk_ref[...] = dk_sum[...].astype(BF16)
    dv_ref[...] = dv_sum[...].astype(BF16)


def attend_back(queries, keys, values, grad, out, lse, query_doc, key_doc, band):
    rows, width = queries.shape
    keys_rows = keys.shape[0]
    pairs = HEADS // 2
    wide = 2 * HEAD_DIM
    cost = pl.CostEstimate(
        flops=10 * rows * WINDOW * width * 4,
        bytes_accessed=2 * (4 * keys_rows + 4 * rows) * width + 8 * HEADS * WINDOW * LANES,
        transcendentals=HEADS * rows * WINDOW,
    )
    q_spec = pl.BlockSpec((rows, wide), lambda p: (0, p))
    k_spec = pl.BlockSpec((keys_rows, wide), lambda p: (0, p))
    band_spec = pl.BlockSpec((2, WINDOW + LANES, LANES), lambda p: (p, 0, 0))
    return pl.pallas_call(
        attend_back_kernel,
        grid=(pairs,),
        in_specs=[
            q_spec,
            k_spec,
            k_spec,
            q_spec,
            q_spec,
            pl.BlockSpec((1, 2, rows), lambda p: (p, 0, 0)),
            pl.BlockSpec((rows, wide), lambda p: (0, 0)),
            pl.BlockSpec((keys_rows, wide), lambda p: (0, 0)),
            band_spec,
        ],
        out_specs=[q_spec, k_spec, k_spec, band_spec],
        out_shape=[
            jax.ShapeDtypeStruct((rows, width), BF16),
            jax.ShapeDtypeStruct((keys_rows, width), BF16),
            jax.ShapeDtypeStruct((keys_rows, width), BF16),
            jax.ShapeDtypeStruct((HEADS, WINDOW + LANES, LANES), F32),
        ],
        scratch_shapes=[pltpu.VMEM((keys_rows, wide), F32), pltpu.VMEM((keys_rows, wide), F32)],
        compiler_params=params(),
        cost_estimate=cost,
        name="attend_back",
    )(queries, keys, values, grad, out, lse, query_doc, key_doc, band)


def expert_kernel(
    x_ref, c_ref, names_ref, router_ref, gate_ref, up_ref, down_ref,
    made_ref, back_ref, drouter_ref, dgate_ref, dup_ref, ddown_ref,
    x_turned, grad_low, gate_col, hidden_s, dgate_s, dup_s, made_sum, back_sum,
):
    step = pl.program_id(0)
    last = pl.num_programs(0) - 1
    rows, width = x_ref.shape
    tile = 256
    lane = lax.broadcasted_iota(jnp.int32, (1, LANES), 1)
    own = lane == lax.axis_index("exp")

    def each_tile(body):
        def loop(i, carry):
            body(pl.ds(pl.multiple_of(i * tile, tile), tile))
            return carry

        lax.fori_loop(0, rows // tile, loop, 0)

    @pl.when(step == 0)
    def _():
        def start(at):
            x = x_ref[at, :]
            names = names_ref[at, :].astype(F32)
            logits = dot_last(x, router_ref[...]) * names
            mine = jnp.sum(jnp.where(own, logits, 0.0), axis=1, keepdims=True)
            theirs = jnp.sum(jnp.where(own, 0.0, logits), axis=1, keepdims=True)
            gate = jax.nn.sigmoid(mine - theirs)
            gate_col[at, :] = jnp.broadcast_to(gate, (tile, LANES))
            grad_low[at, :] = (gate * c_ref[at, :].astype(F32)).astype(BF16)
            x_turned[:, at] = x.T
            made_sum[at, :] = jnp.zeros((tile, width), F32)
            back_sum[at, :] = jnp.zeros((tile, width), F32)

        each_tile(start)

    def middle(at):
        x = x_ref[at, :]
        grad = grad_low[at, :]
        gate_pre = dot(x, gate_ref[...])
        up_pre = dot(x, up_ref[...])
        hidden_grad = dot_last(grad, down_ref[...])
        root = 0.7978845608028654
        square = gate_pre * gate_pre
        bent = jnp.tanh(gate_pre * (root + root * 0.044715 * square))
        half = 0.5 * (1.0 + bent)
        act = gate_pre * half
        slope = half + 0.5 * gate_pre * (1.0 - bent * bent) * (root + 3.0 * root * 0.044715 * square)
        hidden = (act * up_pre).astype(BF16)
        dgate = (hidden_grad * up_pre * slope).astype(BF16)
        dup = (hidden_grad * act).astype(BF16)
        hidden_s[at, :] = hidden
        dgate_s[at, :] = dgate
        dup_s[at, :] = dup
        made_sum[at, :] += dot(hidden, down_ref[...])
        back_sum[at, :] += dot_last(dgate, gate_ref[...]) + dot_last(dup, up_ref[...])

    each_tile(middle)

    def weights(i, carry):
        at = pl.ds(pl.multiple_of(i * tile, tile), tile)
        turned = x_turned[at, :]
        dgate_ref[at, :] = dot(turned, dgate_s[...]).astype(BF16)
        dup_ref[at, :] = dot(turned, dup_s[...]).astype(BF16)
        return carry

    lax.fori_loop(0, width // tile, weights, 0)
    ddown_ref[...] = dot(hidden_s[...].T, grad_low[...]).astype(BF16)

    @pl.when(step == last)
    def _():
        drouter_ref[...] = jnp.zeros_like(drouter_ref)

        def finish(at):
            made = made_sum[at, :].astype(BF16).astype(F32)
            gate = gate_col[at, :][:, :1]
            names = names_ref[at, :].astype(F32)
            push = jnp.sum(c_ref[at, :].astype(F32) * made, axis=1, keepdims=True)
            push = push * gate * (1.0 - gate)
            logits_grad = push * jnp.where(own, names, -names)
            high = logits_grad.astype(BF16)
            low = (logits_grad - high.astype(F32)).astype(BF16)
            back_ref[at, :] = (back_sum[at, :] + dot(high, router_ref[...]) + dot(low, router_ref[...])).astype(BF16)
            drouter_ref[...] += dot(x_turned[:, at], high) + dot(x_turned[:, at], low)
            made_ref[at, :] = (gate * made).astype(BF16)

        each_tile(finish)


def run_expert(rows_in, cot_in, names_in, router_turned, gate_w, up_w, down_w):
    rows, width = rows_in.shape
    units = gate_w.shape[1]
    whole = lambda f: (0, 0)
    cost = pl.CostEstimate(
        flops=18 * rows * width * units,
        bytes_accessed=12 * units * width + 10 * rows * width,
        transcendentals=rows * units,
    )
    return pl.pallas_call(
        expert_kernel,
        grid=(units // FF_TILE,),
        in_specs=[
            pl.BlockSpec((rows, width), whole),
            pl.BlockSpec((rows, width), whole),
            pl.BlockSpec((rows, LANES), whole),
            pl.BlockSpec((LANES, width), whole),
            pl.BlockSpec((width, FF_TILE), lambda f: (0, f)),
            pl.BlockSpec((width, FF_TILE), lambda f: (0, f)),
            pl.BlockSpec((FF_TILE, width), lambda f: (f, 0)),
        ],
        out_specs=[
            pl.BlockSpec((rows, width), whole),
            pl.BlockSpec((rows, width), whole),
            pl.BlockSpec((width, LANES), whole),
            pl.BlockSpec((width, FF_TILE), lambda f: (0, f)),
            pl.BlockSpec((width, FF_TILE), lambda f: (0, f)),
            pl.BlockSpec((FF_TILE, width), lambda f: (f, 0)),
        ],
        out_shape=[
            jax.ShapeDtypeStruct((rows, width), BF16),
            jax.ShapeDtypeStruct((rows, width), BF16),
            jax.ShapeDtypeStruct((width, LANES), F32),
            jax.ShapeDtypeStruct((width, units), BF16),
            jax.ShapeDtypeStruct((width, units), BF16),
            jax.ShapeDtypeStruct((units, width), BF16),
        ],
        scratch_shapes=[
            pltpu.VMEM((width, rows), BF16),
            pltpu.VMEM((rows, width), BF16),
            pltpu.VMEM((rows, LANES), F32),
            pltpu.VMEM((rows, FF_TILE), BF16),
            pltpu.VMEM((rows, FF_TILE), BF16),
            pltpu.VMEM((rows, FF_TILE), BF16),
            pltpu.VMEM((rows, width), F32),
            pltpu.VMEM((rows, width), F32),
        ],
        compiler_params=params(),
        cost_estimate=cost,
        name="expert",
    )(rows_in, cot_in, names_in, router_turned, gate_w, up_w, down_w)


def exchange(blocks):
    return lax.all_to_all(blocks, "exp", split_axis=0, concat_axis=0, tiled=True)


def body(
    tokens,
    w_query,
    w_key,
    w_value,
    w_out,
    w_router,
    gain_attn,
    gain_mlp,
    pos_bias,
    exp_gate,
    exp_up,
    exp_down,
    doc_lengths,
    bucket_of,
    expert_ids,
    cotangent,
):
    both = ("ctx", "exp")
    own_tokens = tokens[0]
    rows, width = own_tokens.shape
    experts = w_router.shape[1]
    capacity = (5 * TOP * rows + 4 * experts - 1) // (4 * experts)
    reach = (WINDOW + rows - 2) // rows
    scale = HEAD_DIM ** (-0.5)
    ctx_index = lax.axis_index("ctx")
    exp_index = lax.axis_index("exp")
    part = w_query.shape[0]
    bias_part = pos_bias.shape[0]
    devices = width // part

    small = jnp.concatenate([w_router.reshape(-1), gain_attn, gain_mlp, pos_bias])
    small = jnp.pad(small, (0, width - small.shape[0]))[None]
    packed = jnp.concatenate([small, w_query, w_key, w_value, w_out], axis=0)
    gathered = lax.all_gather(packed, both, axis=0)
    full_query, full_key, full_value, full_out = (
        gathered[:, 1 + i * part : 1 + (i + 1) * part].reshape(width, width) for i in range(4)
    )
    small = gathered[:, 0]
    at = part * experts
    full_router = small[:, :at].reshape(width, experts)
    full_gain_attn = small[:, at : at + part].reshape(width).astype(F32)
    full_gain_mlp = small[:, at + part : at + 2 * part].reshape(width).astype(F32)
    table = small[:, at + 2 * part : at + 2 * part + bias_part].reshape(HEADS, BUCKETS)
    gate_w = lax.all_gather(exp_gate[0], "ctx", axis=0, tiled=True)
    up_w = lax.all_gather(exp_up[0], "ctx", axis=0, tiled=True)
    down_w = lax.all_gather(exp_down[0], "ctx", axis=0, tiled=True)

    halo = [own_tokens]
    for _ in range(reach):
        halo.insert(0, shift_ctx(halo[0], 1))
    inputs_all = jnp.concatenate(halo, axis=0).astype(F32)
    inputs = own_tokens.astype(F32)

    expert_range = jnp.arange(experts, dtype=jnp.int32)
    named = jnp.any(expert_ids[0][:, :, None] == expert_range, axis=1)
    named_low = named.astype(BF16)
    step = jnp.arange(rows, dtype=jnp.int32)
    earlier = (step[:, None] > step[None, :]).astype(BF16)
    slots = dot(earlier, named_low).astype(jnp.int32)
    slots = jnp.where(named, slots, -1).T
    routes = (slots[:, None, :] == jnp.arange(capacity, dtype=jnp.int32)[None, :, None]).astype(BF16)
    routes = routes.reshape(experts * capacity, rows)

    names = jnp.pad(named_low, ((0, 0), (0, LANES - experts)))
    early = dot(routes, jnp.concatenate([cotangent[0], names], axis=1)).astype(BF16)
    early = exchange(early.reshape(experts, capacity, width + LANES)).reshape(-1, width + LANES)
    cot_in, names_in = early[:, :width], early[:, width:]

    onehot_bucket = (bucket_of[None, :] == jnp.arange(BUCKETS, dtype=jnp.int32)[:, None]).astype(BF16)
    band = make_band(dot(table, onehot_bucket))
    ends = jnp.cumsum(doc_lengths[0])

    def documents(positions):
        return jnp.sum((positions[:, None] >= ends[None, :]).astype(jnp.int32), axis=1)[:, None]

    feature = (jnp.arange(2 * HEAD_DIM, dtype=jnp.int32) % HEAD_DIM)[None, :]
    docs = doc_lengths.shape[1] + 1
    query_pos = ctx_index * rows + step
    key_pos = (ctx_index - reach) * rows + jnp.arange((reach + 1) * rows, dtype=jnp.int32)
    query_doc = (feature == documents(query_pos)).astype(BF16)
    same = (feature == documents(key_pos)) & (key_pos[:, None] >= 0)
    key_doc = jnp.where(same | (feature >= docs), 0.0, NEGATIVE).astype(BF16)

    normed_all = norm_rows(inputs_all, full_gain_attn).astype(BF16)
    normed = normed_all[reach * rows :]
    queries = (dot(normed, full_query).astype(BF16)) * jnp.asarray(scale, BF16)
    keys = dot(normed_all, full_key).astype(BF16)
    values = dot(normed_all, full_value).astype(BF16)
    attended, lse = attend(queries, keys, values, query_doc, key_doc, band)
    middle = inputs + dot(attended, full_out)
    normed_mlp = norm_rows(middle, full_gain_mlp).astype(BF16)

    sent = dot(routes, normed_mlp).astype(BF16)
    arrived = exchange(sent.reshape(experts, capacity, width)).reshape(-1, width)
    router_turned = jnp.pad(full_router.T, ((0, LANES - experts), (0, 0)))
    made, back, router_grad, gate_grad, up_grad, down_grad = run_expert(
        arrived, cot_in, names_in, router_turned, gate_w, up_w, down_w
    )
    back = exchange(back.reshape(experts, capacity, width)).reshape(-1, width)
    made = exchange(made.reshape(experts, capacity, width)).reshape(-1, width)
    output = (middle + dot_rows(routes, made)).astype(BF16)
    expert_grads = [
        lax.psum_scatter(grad, "ctx", scatter_dimension=0, tiled=True).astype(F32)[None]
        for grad in (gate_grad, up_grad, down_grad)
    ]

    upstream = cotangent[0].astype(F32)
    normed_mlp_grad = dot_rows(routes, back)
    _, second_pull = jax.vjp(norm_rows, middle, full_gain_mlp)
    middle_norm_grad, gain_mlp_grad = second_pull(normed_mlp_grad)
    middle_grad = upstream + middle_norm_grad
    branch_grad = middle_grad.astype(BF16)
    out_grad = dot_rows(attended, branch_grad)
    attended_grad = dot_last(branch_grad, full_out).astype(BF16)
    query_grad, key_grad, value_grad, band_grad = attend_back(
        queries, keys, values, attended_grad, attended, lse, query_doc, key_doc, band
    )
    bias_grad = jnp.dot(
        sum_band(band_grad), onehot_bucket.T.astype(F32), precision=lax.Precision.HIGHEST
    )

    normed_grad_all = dot_last(key_grad, full_key) + dot_last(value_grad, full_value)
    own_grad = normed_grad_all[reach * rows :] + dot_last(query_grad, full_query)
    halo_grad = normed_grad_all[: reach * rows]
    returning = None
    for stride in range(reach, 0, -1):
        piece = halo_grad[(reach - stride) * rows : (reach - stride + 1) * rows]
        piece = piece if returning is None else piece + returning.astype(F32)
        returning = shift_ctx(piece.astype(BF16), -1)
    _, first_pull = jax.vjp(norm_rows, inputs_all, full_gain_attn)
    gain_attn_grad = first_pull(jnp.concatenate([halo_grad, own_grad], axis=0))[1]
    _, own_pull = jax.vjp(norm_rows, inputs, full_gain_attn)
    input_grad = middle_grad + own_pull(own_grad + returning.astype(F32))[0]

    bias_column = jnp.pad(bias_grad.reshape(devices, bias_part), ((0, 0), (0, part - bias_part)))
    tail = jnp.concatenate(
        [
            router_grad[:, :experts],
            gain_attn_grad[:, None],
            gain_mlp_grad[:, None],
            bias_column.reshape(width, 1),
        ],
        axis=1,
    )
    tail = jnp.pad(tail, ((0, 0), (0, LANES - tail.shape[1])))
    grads = jnp.concatenate(
        [
            dot_rows(normed, query_grad),
            dot_rows(normed_all, key_grad),
            dot_rows(normed_all, value_grad),
            tail,
        ],
        axis=1,
    )
    out_sum = lax.psum_scatter(out_grad, both, scatter_dimension=0, tiled=True)
    sums = lax.psum_scatter(grads, both, scatter_dimension=0, tiled=True)
    tail = sums[:, 3 * width :]
    return (
        output[None],
        input_grad[None],
        sums[:, :width],
        sums[:, width : 2 * width],
        sums[:, 2 * width : 3 * width],
        out_sum,
        tail[:, :experts],
        tail[:, experts],
        tail[:, experts + 1],
        tail[:bias_part, experts + 2],
        expert_grads[0],
        expert_grads[1],
        expert_grads[2],
    )


def solution(mesh):
    rows3 = P("exp", "ctx", None)
    dense2 = P(("ctx", "exp"), None)
    dense1 = P(("ctx", "exp"))
    return jax.shard_map(
        body,
        mesh=mesh,
        in_specs=(
            rows3,
            dense2,
            dense2,
            dense2,
            dense2,
            dense2,
            dense1,
            dense1,
            dense1,
            rows3,
            rows3,
            rows3,
            P("exp", None),
            P(),
            rows3,
            rows3,
        ),
        out_specs=(
            rows3,
            rows3,
            dense2,
            dense2,
            dense2,
            dense2,
            dense2,
            dense1,
            dense1,
            dense1,
            rows3,
            rows3,
            rows3,
        ),
        check_vma=False,
    )
```

time: 5840 us -> 1210 us (0.21)
  local copies, waits for them, and re-layouts: 4340 us -> 51 us
  matrix products: 407 us -> 62.3 us
  Pallas kernels: 0 us -> 198 us
  blocking collectives: 219 us -> 37.3 us
    gather x8 -> x0, local copies, waits for them, and re-layouts: 4250 us -> none  [the longest x6 4210 us: bucket_map(): picked_bucket = jnp.take(bucket_of, jnp.clip(distance, 0, WINDOW - 1))]
    reduce_scatter x7 -> x4, waiting for transfers between devices: 554 us -> 157 us  [the longest x1 134 us: body(): out_sum = lax.psum_scatter(out_grad, both, scatter_dimension=0, tiled=True)]
    dot_general x47 -> x19, matrix products: 405 us -> 62.3 us  [the longest x6 23.4 us: dot_rows(): lax.dot_general(left, right, (((0,), (0,)), ((), ())), preferred_element_...]
    all_gather x7 -> x4, waiting for transfers between devices: 0.05 us -> 254 us  [the longest x1 107 us: body(): up_w = lax.all_gather(exp_up[0], 'ctx', axis=0, tiled=True)]
    pallas_call x0 -> x5, Pallas kernels: none -> 198 us  [the longest x1 110 us: run_expert(): pl.pallas_call(expert_kernel, grid=(units // FF_TILE,), in_specs=[pl.Bloc...]
    unnamed x16 -> x10, waiting for transfers between devices: 4.46 us -> 161 us
    unnamed x2 -> x0, blocking collectives: 86.8 us -> none
    all_gather x1 -> x0, blocking collectives: 61.5 us -> none  [fetch_dense(): lax.all_gather(w_router, ('ctx', 'exp'), axis=0, tiled=True)]
  transfers between devices with their start and end apart: 21 -> 16, of which waited for: 8 -> 12; matrix products, arithmetic and copies ran while one was open for 81% -> 12% of each run, Pallas kernels for 0% -> 7%
where the time goes in v1:
time: 1210 us; the launch traced here: 1200 us
  waiting for transfers between devices  776 us (64%)
  Pallas kernels  198 us (16%)
  matrix products  62.3 us (5%)
  local copies, waits for them, and re-layouts  51 us (4%)
  other arithmetic  39.1 us (3%)
  blocking collectives  37.3 us (3%)
  starting transfers between devices  26.4 us (2%)
  between operations  14.7 us (1%)
    ppermute x4, waiting for transfers between devices, shift_ctx(): return lax.ppermute(block, 'ctx', route)  174 us
    unnamed x10, waiting for transfers between devices  161 us
    reduce_scatter x1, waiting for transfers between devices, body(): out_sum = lax.psum_scatter(out_grad, both, scatter_dimension=0, tiled=True)  134 us
    pallas_call x1, Pallas kernels, run_expert(): pl.pallas_call(expert_kernel, grid=(units // FF_TILE,), in_specs=[pl.Bloc...  110 us
    all_gather x1, waiting for transfers between devices, body(): up_w = lax.all_gather(exp_up[0], 'ctx', axis=0, tiled=True)  107 us
    all_gather x1, waiting for transfers between devices, body(): down_w = lax.all_gather(exp_down[0], 'ctx', axis=0, tiled=True)  106 us
    all_to_all x1, blocking collectives, exchange(): lax.all_to_all(blocks, 'exp', split_axis=0, concat_axis=0, tiled=True)  37.3 us
    pallas_call x1, Pallas kernels, attend_back(): pl.pallas_call(attend_back_kernel, grid=(pairs,), in_specs=[q_spec, k_spe...  31.4 us
  transfers between devices with their start and end apart: 16, of which 12 were waited for; matrix products, arithmetic and copies ran while one was open for 12% of the time, Pallas kernels for 7%

profile of v1, /device:TPU:0, one launch (start us, length us, event | category | flops | bytes accessed | tf_op | source)
XLA Modules:
  0.0 1204.8 jit_solution(6197489567452338860)
XLA Ops:
  9.0 6.7 concatenate.26
  32.1 22.5 %collective-permute-done = bf16[512,1024]{1,0:T(8,128)(2,1)S(1)} collective-permute-done((bf16[512,1024]{1,0:T(8,128)(2,1)S(1)}, bf16[512,1024]{1,0:T(8,128)(2,1)S(1)}, u32[]{:S(2)}, u32[]{:S(2)}) %collective-permute-start) | collective-permute-done | bytes 1048608 | tf_op jit(solution)/shard_map/ppermute | solution.py:29
  62.5 30.8 %collective-permute-done.1 = bf16[512,1024]{1,0:T(8,128)(2,1)S(1)} collective-permute-done((bf16[512,1024]{1,0:T(8,128)(2,1)S(1)}, bf16[512,1024]{1,0:T(8,128)(2,1)S(1)}, u32[]{:S(2)}, u32[]{:S(2)}) %collective-permute-start.1) | collective-permute-done | bytes 1048608 | tf_op jit(solution)/shard_map/ppermute | solution.py:29
  94.1 16.7 %all-gather.16.cloned.1.call-done = bf16[32,129,1024]{2,1,0:T(8,128)(2,1)} async-done(((bf16[1,129,1024]{2,1,0:T(8,128)(2,1)}), bf16[32,129,1024]{2,1,0:T(8,128)(2,1)}) %all-gather.16.cloned.1.call-update) | async-done | bytes 8454160 | tf_op jit(solution)/shard_map/all_gather | solution.py:461
  112.4 9.2 fusion.48
  135.7 11.5 bias_band.1.band_ref
  147.2 6.3 convolution_convert_fusion.3.k_ref
  153.5 29.0 %attend.1 = (bf16[512,1024]{1,0:T(8,128)(2,1)}, f32[8,2,512]{2,1,0:T(2,128)}) custom-call(bf16[512,1024]{1,0:T(8,128)(2,1)} %fusion.15.q_ref, bf16[1536,1024]{1,0:T(8,128)(2,1)} %convolution_convert_fusion.3.k_ref, bf16[1536,1024]{1,0:T(8,128)(2,1)} %convolution_convert_fusion.2.v_ref, bf16[512,128]{1,0:T(8,128)(2,1)} %compare_convert_fusion.qdoc_ref, ...), custom_call_target="tpu_custom_call" | custom-call | flops 8589934592 | bytes 16777216 | tf_op jit(solution)/shard_map/attend/pallas_call | solution.py:171
  199.2 24.4 %all-gather.10.cloned.1.call-done = bf16[1,1024,2816]{2,1,0:T(8,128)(2,1)} async-done(((bf16[1,256,2816]{2,1,0:T(8,128)(2,1)}), bf16[1,1024,2816]{2,1,0:T(8,128)(2,1)}) %all-gather.10.cloned.1.call-update) | async-done | bytes 5767184 | tf_op jit(solution)/shard_map/all_gather | solution.py:471
  223.6 106.6 %all-gather.12.cloned.1.call-done = bf16[1,1024,2816]{2,1,0:T(8,128)(2,1)} async-done(((bf16[1,256,2816]{2,1,0:T(8,128)(2,1)}), bf16[1,1024,2816]{2,1,0:T(8,128)(2,1)}) %all-gather.12.cloned.1.call-update) | async-done | bytes 5767184 | tf_op jit(solution)/shard_map/all_gather | solution.py:472
  330.2 106.5 %all-gather.14.cloned.1.call-done = bf16[1,2816,1024]{2,1,0:T(8,128)(2,1)} async-done(((bf16[1,704,1024]{2,1,0:T(8,128)(2,1)}), bf16[1,2816,1024]{2,1,0:T(8,128)(2,1)}) %all-gather.14.cloned.1.call-update) | async-done | bytes 5767184 | tf_op jit(solution)/shard_map/all_gather | solution.py:473
  436.7 110.0 %expert.1 = (bf16[1280,1024]{1,0:T(8,128)(2,1)}, bf16[1280,1024]{1,0:T(8,128)(2,1)}, f32[1024,128]{1,0:T(8,128)}, bf16[1024,2816]{1,0:T(8,128)(2,1)}, bf16[1024,...) custom-call(bf16[1280,1024]{1,0:T(8,128)(2,1)} %bitcast.13.x_ref, bf16[1280,1024]{1,0:T(8,128)(2,1)} %slice.113.c_ref, ...), custom_call_target="tpu_custom_call" | custom-call | flops 66437775360 | bytes 47710208 | tf_op jit(solution)/shard_map/expert/pallas_call | solution.py:379
  553.7 30.3 %all-to-all-done.3 = bf16[8,160,1024]{2,1,0:T(8,128)(2,1)} async-done(((bf16[8,160,1024]{2,1,0:T(8,128)(2,1)}), bf16[8,160,1024]{2,1,0:T(8,128)(2,1)}, u32[]{:S(2)}, u32[]{:S(2)}) %all-to-all-start.3) | async-done | bytes 2621472 | tf_op jit(solution)/shard_map/all_to_all | solution.py:424
  592.4 31.4 %attend_back.1 = (bf16[512,1024]{1,0:T(8,128)(2,1)}, bf16[1536,1024]{1,0:T(8,128)(2,1)}, bf16[1536,1024]{1,0:T(8,128)(2,1)}, f32[16,1152,128]{2,1,0:T(8,128)}) custom-call(bf16[512,1024]{1,0:T(8,128)(2,1)} %fusion.15.q_ref, bf16[1536,1024]{1,0:T(8,128)(2,1)} %convolution_convert_fusion.3.k_ref, bf16[1536,1024]{1,0:T(8,128)(2,1)} %convolution_convert_fusion.2.v_ref, ...), custom_call_target="tpu_custom_call" | custom-call | flops 21474836480 | bytes 33554432 | tf_op jit(solution)/shard_map/attend_back/pallas_call | solution.py:253
  635.8 16.2 %bias_band_sums.1 = f32[16,1,1024]{2,1,0:T(1,128)} custom-call(f32[16,1152,128]{2,1,0:T(8,128)} %get-tuple-element.33.band_ref), custom_call_target="tpu_custom_call" | custom-call | tf_op jit(solution)/shard_map/bias_band_sums/pallas_call | solution.py:95
  654.7 7.7 fusion.52
  662.4 57.9 %collective-permute-done.2 = bf16[512,1024]{1,0:T(8,128)(2,1)} collective-permute-done((bf16[512,1024]{1,0:T(8,128)(2,1)}, bf16[512,1024]{1,0:T(8,128)(2,1)}, u32[]{:S(2)}, u32[]{:S(2)}) %collective-permute-start.2) | collective-permute-done | bytes 1048608 | tf_op jit(solution)/shard_map/ppermute | solution.py:29
  728.8 62.5 %collective-permute-done.3 = bf16[512,1024]{1,0:T(8,128)(2,1)S(1)} collective-permute-done((bf16[512,1024]{1,0:T(8,128)(2,1)S(1)}, bf16[512,1024]{1,0:T(8,128)(2,1)S(1)}, u32[]{:S(2)}, u32[]{:S(2)}) %collective-permute-start.3) | collective-permute-done | bytes 1048608 | tf_op jit(solution)/shard_map/ppermute | solution.py:29
  794.8 7.1 fusion.3
  807.3 13.7 %copy.78 = f32[1024,3200]{1,0:T(8,128)} copy(f32[1024,3200]{0,1:T(8,128)} %pad_maximum_fusion) | data formatting | bytes 26214400
  825.6 37.3 %all_to_all.20 = bf16[8,160,1024]{2,1,0:T(8,128)(2,1)S(1)} all-to-all(bf16[8,160,1024]{2,1,0:T(8,128)(2,1)} %bitcast.101), channel_id=1, replica_groups=mesh['ctx'=4,'exp'=8] {'exp'}, dimensions={0} | all-to-all | bytes 5242880 | tf_op jit(solution)/shard_map/all_to_all | solution.py:424
  873.9 23.4 %reduce-scatter.10.cloned.1.call-done = bf16[256,2816]{1,0:T(8,128)(2,1)} async-done(((bf16[1024,2816]{1,0:T(8,128)(2,1)}), bf16[256,2816]{1,0:T(8,128)(2,1)}) %reduce-scatter.10.cloned.1.call-update) | async-done | bytes 1441808 | tf_op jit(solution)/shard_map/reduce_scatter | solution.py:530
  900.5 157.4 %reduce-scatter.16.cloned.1.call-done = f32[32,3200]{1,0:T(8,128)} async-done(((f32[1024,3200]{1,0:T(8,128)}), f32[32,3200]{1,0:T(8,128)}) %reduce-scatter.16.cloned.1.call-update) | async-done | bytes 409616
  1064.5 133.6 %reduce-scatter.8.cloned.1.call-done = f32[32,1024]{1,0:T(8,128)} async-done(((f32[1024,1024]{1,0:T(8,128)}), f32[32,1024]{1,0:T(8,128)}) %reduce-scatter.8.cloned.1.call-update) | async-done | bytes 131088 | tf_op jit(solution)/shard_map/reduce_scatter | solution.py:582
  (187 shorter events, 131.2 us)
Async XLA Ops:
  7.2 103.6 %all-gather.16.cloned.1.call-start = ((), (), s32[]{:S(2)}) async-start(), calls=%async_computation.16 | async-start | bytes 9191424 | tf_op jit(solution)/shard_map/all_gather | solution.py:461
  15.8 207.8 %all-gather.10.cloned.1.call-start = ((), (), s32[]{:S(2)}) async-start(), calls=%async_computation.13 | async-start | bytes 7208960 | tf_op jit(solution)/shard_map/all_gather | solution.py:471
  16.5 313.7 %all-gather.12.cloned.1.call-start = ((), (), s32[]{:S(2)}) async-start(), calls=%async_computation.14 | async-start | bytes 7208960 | tf_op jit(solution)/shard_map/all_gather | solution.py:472
  17.3 37.3 %collective-permute-start = (bf16[512,1024]{1,0:T(8,128)(2,1)S(1)}, bf16[512,1024]{1,0:T(8,128)(2,1)S(1)}, u32[]{:S(2)}, u32[]{:S(2)}) collective-permute-start(bf16[512,1024]{1,0:T(8,128)(2,1)S(1)} %bitcast.96), channel_id=1, source_target_pairs={{0,8},{8,16},{16,24},{1,9},{9,17},{17,25},{2,10},{10,18},{18,26},{... | collective-permute-start | bytes 3145736 | tf_op jit(solution)/shard_map/ppermute | solution.py:29
  26.9 161.5 %all-to-all-start.1 = ((bf16[8,160,1152]{2,1,0:T(8,128)(2,1)}), bf16[8,160,1152]{2,1,0:T(8,128)(2,1)}, u32[]{:S(2)}, u32[]{:S(2)}) async-start(bf16[8,160,1152]{2,1,0:T(8,128)(2,1)} %bitcast.100), calls=%async_computation.1 | async-start | bytes 5898240 | tf_op jit(solution)/shard_map/all_to_all | solution.py:424
  31.4 80.8 %copy-start.32 = (s32[1024]{0:T(1024)S(1)}, s32[1024]{0:T(1024)}, u32[]{:S(2)}) copy-start(s32[1024]{0:T(1024)} %param.29) | copy-start | bytes 12292
  31.4 405.3 %all-gather.14.cloned.1.call-start = ((), (), s32[]{:S(2)}) async-start(), calls=%async_computation.15 | async-start | bytes 7208960 | tf_op jit(solution)/shard_map/all_gather | solution.py:473
  54.6 67.0 %copy-start.3 = (bf16[512,1024]{1,0:T(8,128)(2,1)}, bf16[512,1024]{1,0:T(8,128)(2,1)S(1)}, u32[]{:S(2)}) copy-start(bf16[512,1024]{1,0:T(8,128)(2,1)S(1)} %collective-permute-done) | copy-start | bytes 3145732
  54.6 38.7 %collective-permute-start.1 = (bf16[512,1024]{1,0:T(8,128)(2,1)S(1)}, bf16[512,1024]{1,0:T(8,128)(2,1)S(1)}, u32[]{:S(2)}, u32[]{:S(2)}) collective-permute-start(bf16[512,1024]{1,0:T(8,128)(2,1)S(1)} %collective-permute-done), channel_id=1, source_target_pairs={{0,8},{8,16},{16,24},{1,9},{9,17},{17,25},{2,10},{10,18},{18,26},{... | collective-permute-start | bytes 3145736 | tf_op jit(solution)/shard_map/ppermute | solution.py:29
  185.2 398.8 %copy-start.12 = (f32[512,1024]{1,0:T(8,128)}, f32[512,1024]{1,0:T(8,128)S(1)}, u32[]{:S(2)}) copy-start(f32[512,1024]{1,0:T(8,128)S(1)} %get-tuple-element.120) | copy-start | bytes 6291460
  188.4 248.3 %all-to-all-start = ((bf16[8,160,1024]{2,1,0:T(8,128)(2,1)}), bf16[8,160,1024]{2,1,0:T(8,128)(2,1)}, u32[]{:S(2)}, u32[]{:S(2)}) async-start(bf16[8,160,1024]{2,1,0:T(8,128)(2,1)} %bitcast.103), calls=%async_computation | async-start | bytes 5242880 | tf_op jit(solution)/shard_map/all_to_all | solution.py:424
  192.8 674.7 %reduce-scatter.14.cloned.1.call-start = ((), (), s32[]{:S(2)}) async-start(), calls=%async_computation.12 | async-start | bytes 7208960 | tf_op jit(solution)/shard_map/reduce_scatter | solution.py:530
  546.7 324.1 %reduce-scatter.12.cloned.1.call-start = ((), (), s32[]{:S(2)}) async-start(), calls=%async_computation.11 | async-start | bytes 7208960 | tf_op jit(solution)/shard_map/reduce_scatter | solution.py:530
  547.3 36.7 %all-to-all-start.3 = ((bf16[8,160,1024]{2,1,0:T(8,128)(2,1)}), bf16[8,160,1024]{2,1,0:T(8,128)(2,1)}, u32[]{:S(2)}, u32[]{:S(2)}) async-start(bf16[8,160,1024]{2,1,0:T(8,128)(2,1)} %bitcast.102), calls=%async_computation.3 | async-start | bytes 5242880 | tf_op jit(solution)/shard_map/all_to_all | solution.py:424
  551.7 345.6 %reduce-scatter.10.cloned.1.call-start = ((), (), s32[]{:S(2)}) async-start(), calls=%async_computation.10 | async-start | bytes 7208960 | tf_op jit(solution)/shard_map/reduce_scatter | solution.py:530
  552.5 505.4 %reduce-scatter.16.cloned.1.call-start = ((), (), s32[]{:S(2)}) async-start(), calls=%async_computation.17 | async-start | bytes 13516800
  652.0 68.3 %collective-permute-start.2 = (bf16[512,1024]{1,0:T(8,128)(2,1)}, bf16[512,1024]{1,0:T(8,128)(2,1)}, u32[]{:S(2)}, u32[]{:S(2)}) collective-permute-start(bf16[512,1024]{1,0:T(8,128)(2,1)} %slice.138), channel_id=1, source_target_pairs={{8,0},{16,8},{24,16},{9,1},{17,9},{25,17},{10,2},{18,10},{26,18},{... | collective-permute-start | bytes 3145736 | tf_op jit(solution)/shard_map/ppermute | solution.py:29
  721.9 69.4 %collective-permute-start.3 = (bf16[512,1024]{1,0:T(8,128)(2,1)S(1)}, bf16[512,1024]{1,0:T(8,128)(2,1)S(1)}, u32[]{:S(2)}, u32[]{:S(2)}) collective-permute-start(bf16[512,1024]{1,0:T(8,128)(2,1)S(1)} %fusion.12), channel_id=1, source_target_pairs={{8,0},{16,8},{24,16},{9,1},{17,9},{25,17},{10,2},{18,10},{26,18},{... | collective-permute-start | bytes 3145736 | tf_op jit(solution)/shard_map/ppermute | solution.py:29
  725.2 66.2 %copy-start.15 = (bf16[32,32,1024]{2,1,0:T(8,128)(2,1)S(1)}, bf16[32,32,1024]{2,1,0:T(8,128)(2,1)}, u32[]{:S(2)}) copy-start(bf16[32,32,1024]{2,1,0:T(8,128)(2,1)} %copy-done.14) | copy-start | bytes 6291460
  725.2 66.2 %copy-start.31 = (f32[1024]{0:T(1024)S(1)}, f32[1024]{0:T(1024)}, u32[]{:S(2)}) copy-start(f32[1024]{0:T(1024)} %copy-done.30) | copy-start | bytes 12292
  728.8 66.0 %slice-start = ((f32[1536,1024]{1,0:T(8,128)}), f32[1024,1024]{1,0:T(8,128)S(1)}, s32[]{:S(2)}) async-start(f32[1536,1024]{1,0:T(8,128)} %copy-done.1), calls=%async_computation.18 | async-start | bytes 8388608 | tf_op jit(solution)/shard_map/slice | solution.py:551
  728.8 66.0 %copy-start.4 = (bf16[512,1024]{1,0:T(8,128)(2,1)S(1)}, bf16[512,1024]{1,0:T(8,128)(2,1)}, u32[]{:S(2)}) copy-start(bf16[512,1024]{1,0:T(8,128)(2,1)} %copy-done.3) | copy-start | bytes 3145732
  728.8 66.0 %copy-start.6 = (bf16[512,1024]{1,0:T(8,128)(2,1)S(1)}, bf16[512,1024]{1,0:T(8,128)(2,1)}, u32[]{:S(2)}) copy-start(bf16[512,1024]{1,0:T(8,128)(2,1)} %copy-done.5) | copy-start | bytes 3145732
  821.1 377.0 %reduce-scatter.8.cloned.1.call-start = ((), (), s32[]{:S(2)}) async-start(), calls=%async_computation.9 | async-start | bytes 4325376 | tf_op jit(solution)/shard_map/reduce_scatter | solution.py:582
  (31 other events, 580.7 us)
Sparse Core Ops, SparseCore 0:
  15.9 94.8 all-gather.15
  112.4 111.1 all-gather.9
  225.2 104.9 all-gather.11
  331.7 104.9 all-gather.13
  546.9 100.5 reduce-scatter.13
  649.6 142.0 reduce-scatter.11
  794.0 103.3 reduce-scatter.9
  899.7 158.1 reduce-scatter.15
  1060.8 137.1 reduce-scatter.7

commit v2 on v1

v2 whole, which is shorter than its diff:
```python
import functools

import jax
import jax.numpy as jnp
from jax import lax
from jax.experimental import pallas as pl
from jax.experimental.pallas import tpu as pltpu
from jax.sharding import PartitionSpec as P

HEADS = 16
HEAD_DIM = 64
BUCKETS = 32
TOP = 2
WINDOW = 1024

EPSILON = 1e-06
NEGATIVE = -1e30
LANES = 128
CHUNK = 256
FF_TILE = 256
ROW_TILE = 256
VMEM_LIMIT = 58 * 2**20
BF16 = jnp.bfloat16
F32 = jnp.float32


def shift_ctx(block, distance):
    devices = range(lax.axis_size("ctx"))
    route = [(i - distance, i) for i in devices if i - distance in devices]
    return lax.ppermute(block, "ctx", route)


def norm_rows(values, gain):
    return values * lax.rsqrt(jnp.mean(values * values, axis=-1, keepdims=True) + EPSILON) * gain


def dot(left, right):
    return jnp.dot(left, right, preferred_element_type=F32)


def dot_rows(left, right):
    return lax.dot_general(left, right, (((0,), (0,)), ((), ())), preferred_element_type=F32)


def dot_last(left, right):
    return lax.dot_general(left, right, (((1,), (1,)), ((), ())), preferred_element_type=F32)


def params(**more):
    return pltpu.CompilerParams(vmem_limit_bytes=VMEM_LIMIT, **more)


def brief():
    return pl.CostEstimate(flops=2**20, bytes_accessed=2**20, transcendentals=0)


def band_kernel(bias_ref, band_ref):
    blocks = WINDOW // LANES
    size = (blocks + 2) * LANES
    for head in range(bias_ref.shape[0]):
        row = jnp.broadcast_to(bias_ref[head : head + 1, :], (8, size))
        eight = pltpu.roll(row, 0, 1, stride=1, stride_axis=0)
        for group in range(LANES // 8):
            wide = pltpu.roll(eight, 8 * group, 1) if group else eight
            for a in range(blocks + 1):
                first = a * LANES + group * 8
                at = (blocks + 1 - a) * LANES
                band_ref[head, first : first + 8, :] = wide[:, at : at + LANES]


def make_band(bias_dist):
    group = 8
    edge = jnp.full((HEADS, LANES), NEGATIVE, F32)
    padded = jnp.concatenate([edge, bias_dist, edge], axis=1)
    return pl.pallas_call(
        band_kernel,
        grid=(HEADS // group,),
        in_specs=[pl.BlockSpec((group, WINDOW + 2 * LANES), lambda h: (h, 0))],
        out_specs=pl.BlockSpec((group, WINDOW + LANES, LANES), lambda h: (h, 0, 0)),
        out_shape=jax.ShapeDtypeStruct((HEADS, WINDOW + LANES, LANES), F32),
        compiler_params=params(),
        cost_estimate=brief(),
        name="bias_band",
    )(padded)


def unband_kernel(band_ref, dist_ref):
    blocks = WINDOW // LANES
    size = (blocks + 2) * LANES
    row = lax.broadcasted_iota(jnp.int32, (8, 1), 0)
    edge = jnp.zeros((8, LANES), F32)
    for head in range(band_ref.shape[0]):
        total = None
        for group in range(LANES // 8):
            pieces = [edge]
            for a in range(blocks, -1, -1):
                first = a * LANES + group * 8
                pieces.append(band_ref[head, first : first + 8, :])
            wide = jnp.concatenate(pieces, axis=1)
            if group:
                wide = pltpu.roll(wide, size - 8 * group, 1)
            total = wide if total is None else total + wide
        dist = jnp.zeros_like(total)
        for r in range(8):
            turned = pltpu.roll(total, size - r, 1) if r else total
            dist = dist + jnp.where(row == r, turned, 0.0)
        dist_ref[head : head + 1, :] = jnp.sum(dist, axis=0, keepdims=True)[:, LANES : LANES + WINDOW]


def sum_band(band_grad):
    group = 8
    return pl.pallas_call(
        unband_kernel,
        grid=(HEADS // group,),
        in_specs=[pl.BlockSpec((group, WINDOW + LANES, LANES), lambda h: (h, 0, 0))],
        out_specs=pl.BlockSpec((group, WINDOW), lambda h: (h, 0)),
        out_shape=jax.ShapeDtypeStruct((HEADS, WINDOW), F32),
        compiler_params=params(),
        cost_estimate=brief(),
        name="bias_band_sums",
    )(band_grad)


def head_lanes(head):
    lane = lax.broadcasted_iota(jnp.int32, (1, 2 * HEAD_DIM), 1)
    return (lane >= head * HEAD_DIM) & (lane < (head + 1) * HEAD_DIM)


def masked_scores(head, start, q_ref, k_ref, qdoc_ref, kdoc_ref):
    span = WINDOW + CHUNK
    mine = head_lanes(head)
    q_rows, k_rows = pl.ds(start, CHUNK), pl.ds(start, span)
    q_part = jnp.where(mine, q_ref[q_rows, :], qdoc_ref[q_rows, :])
    k_part = jnp.where(mine, k_ref[k_rows, :], kdoc_ref[k_rows, :])
    return dot_last(k_part, q_part)


def sub_blocks():
    return [(s * LANES, WINDOW + LANES) for s in range(CHUNK // LANES)]


def spread(parts):
    span = WINDOW + CHUNK
    columns = []
    for (first, rows), part in zip(sub_blocks(), parts):
        pieces = []
        if first:
            pieces.append(jnp.zeros((first, LANES), part.dtype))
        pieces.append(part)
        if span - first - rows:
            pieces.append(jnp.zeros((span - first - rows, LANES), part.dtype))
        columns.append(jnp.concatenate(pieces, axis=0) if len(pieces) > 1 else part)
    return jnp.concatenate(columns, axis=1)


def attend_kernel(q_ref, k_ref, v_ref, qdoc_ref, kdoc_ref, band_ref, o_ref, lse_ref):
    span = WINDOW + CHUNK
    for start in range(0, q_ref.shape[0], CHUNK):
        v_turned = v_ref[pl.ds(start, span), :].T
        outs = []
        for head in range(2):
            scores = masked_scores(head, start, q_ref, k_ref, qdoc_ref, kdoc_ref)
            band = band_ref[head]
            low, scale, logs = [], [], []
            for s, (first, rows) in enumerate(sub_blocks()):
                part = scores[first : first + rows, s * LANES : (s + 1) * LANES] + band
                top = jnp.max(part, axis=0, keepdims=True)
                expo = jnp.exp(part - top)
                total = jnp.sum(expo, axis=0, keepdims=True)
                low.append(expo.astype(BF16))
                scale.append(1.0 / total)
                logs.append(top + jnp.log(total))
            out = dot(v_turned[head * HEAD_DIM : (head + 1) * HEAD_DIM], spread(low))
            outs.append(out * jnp.concatenate(scale, axis=1))
            lse_ref[0, head : head + 1, pl.ds(start, CHUNK)] = jnp.concatenate(logs, axis=1)
        o_ref[pl.ds(start, CHUNK), :] = jnp.concatenate(outs, axis=0).T.astype(BF16)


def attend(queries, keys, values, query_doc, key_doc, band):
    rows, width = queries.shape
    keys_rows = keys.shape[0]
    pairs = HEADS // 2
    wide = 2 * HEAD_DIM
    return pl.pallas_call(
        attend_kernel,
        grid=(pairs,),
        in_specs=[
            pl.BlockSpec((rows, wide), lambda p: (0, p)),
            pl.BlockSpec((keys_rows, wide), lambda p: (0, p)),
            pl.BlockSpec((keys_rows, wide), lambda p: (0, p)),
            pl.BlockSpec((rows, wide), lambda p: (0, 0)),
            pl.BlockSpec((keys_rows, wide), lambda p: (0, 0)),
            pl.BlockSpec((2, WINDOW + LANES, LANES), lambda p: (p, 0, 0)),
        ],
        out_specs=[
            pl.BlockSpec((rows, wide), lambda p: (0, p)),
            pl.BlockSpec((1, 2, rows), lambda p: (p, 0, 0)),
        ],
        out_shape=[
            jax.ShapeDtypeStruct((rows, width), BF16),
            jax.ShapeDtypeStruct((pairs, 2, rows), F32),
        ],
        compiler_params=params(),
        cost_estimate=brief(),
        name="attend",
    )(queries, keys, values, query_doc, key_doc, band)


def attend_back_kernel(
    q_ref, k_ref, v_ref, g_ref, o_ref, lse_ref, qdoc_ref, kdoc_ref, band_ref,
    dq_ref, dk_ref, dv_ref, dband_ref, dk_sum, dv_sum,
):
    span = WINDOW + CHUNK
    dk_sum[...] = jnp.zeros_like(dk_sum)
    dv_sum[...] = jnp.zeros_like(dv_sum)
    for start in range(0, q_ref.shape[0], CHUNK):
        q_rows, k_rows = pl.ds(start, CHUNK), pl.ds(start, span)
        k_turned = k_ref[k_rows, :].T
        product = (g_ref[q_rows, :].astype(F32) * o_ref[q_rows, :].astype(F32)).T
        dq_parts = []
        for head in range(2):
            mine = head_lanes(head)
            zero = jnp.zeros((), BF16)
            scores = masked_scores(head, start, q_ref, k_ref, qdoc_ref, kdoc_ref)
            g_part = jnp.where(mine, g_ref[q_rows, :], zero)
            q_part = jnp.where(mine, q_ref[q_rows, :], zero)
            prob_grad = dot_last(v_ref[k_rows, :], g_part)
            delta = jnp.sum(product[head * HEAD_DIM : (head + 1) * HEAD_DIM], axis=0, keepdims=True)
            lse = lse_ref[0, head : head + 1, q_rows]
            band = band_ref[head]
            prob_low, grad_low, grad_sum = [], [], None
            for s, (first, rows) in enumerate(sub_blocks()):
                lanes = slice(s * LANES, (s + 1) * LANES)
                probs = jnp.exp(scores[first : first + rows, lanes] + band - lse[:, lanes])
                grad = probs * (prob_grad[first : first + rows, lanes] - delta[:, lanes])
                prob_low.append(probs.astype(BF16))
                grad_low.append(grad.astype(BF16))
                grad_sum = grad if grad_sum is None else grad_sum + grad
            if start == 0:
                dband_ref[head] = grad_sum
            else:
                dband_ref[head] = dband_ref[head] + grad_sum
            grads = spread(grad_low)
            dk_sum[k_rows, :] += dot(grads, q_part)
            dv_sum[k_rows, :] += dot(spread(prob_low), g_part)
            dq_parts.append(dot(k_turned[head * HEAD_DIM : (head + 1) * HEAD_DIM], grads))
        turned = jnp.concatenate(dq_parts, axis=0).T
        dq_ref[q_rows, :] = (turned * HEAD_DIM ** (-0.5)).astype(BF16)
    dk_ref[...] = dk_sum[...].astype(BF16)
    dv_ref[...] = dv_sum[...].astype(BF16)


def attend_back(queries, keys, values, grad, out, lse, query_doc, key_doc, band):
    rows, width = queries.shape
    keys_rows = keys.shape[0]
    pairs = HEADS // 2
    wide = 2 * HEAD_DIM
    q_spec = pl.BlockSpec((rows, wide), lambda p: (0, p))
    k_spec = pl.BlockSpec((keys_rows, wide), lambda p: (0, p))
    band_spec = pl.BlockSpec((2, WINDOW + LANES, LANES), lambda p: (p, 0, 0))
    return pl.pallas_call(
        attend_back_kernel,
        grid=(pairs,),
        in_specs=[
            q_spec,
            k_spec,
            k_spec,
            q_spec,
            q_spec,
            pl.BlockSpec((1, 2, rows), lambda p: (p, 0, 0)),
            pl.BlockSpec((rows, wide), lambda p: (0, 0)),
            pl.BlockSpec((keys_rows, wide), lambda p: (0, 0)),
            band_spec,
        ],
        out_specs=[q_spec, k_spec, k_spec, band_spec],
        out_shape=[
            jax.ShapeDtypeStruct((rows, width), BF16),
            jax.ShapeDtypeStruct((keys_rows, width), BF16),
            jax.ShapeDtypeStruct((keys_rows, width), BF16),
            jax.ShapeDtypeStruct((HEADS, WINDOW + LANES, LANES), F32),
        ],
        scratch_shapes=[pltpu.VMEM((keys_rows, wide), F32), pltpu.VMEM((keys_rows, wide), F32)],
        compiler_params=params(),
        cost_estimate=brief(),
        name="attend_back",
    )(queries, keys, values, grad, out, lse, query_doc, key_doc, band)


def down_blocks(units, width, count):
    held, share = width // count, units // count
    spare = held - share
    if not spare:
        return [((0, 0), (0, 0), (units, width))]
    wide = width * share // held
    blocks = []
    for z in range(count):
        blocks.append(((z * held, 0), (z * share, 0), (share, wide)))
        for m in range(share // spare):
            thin = width - wide
            blocks.append(((z * held + share, m * thin), (z * share + m * spare, wide), (spare, thin)))
    return blocks


def expert_kernel(first, last, units, count, *refs):
    refs = list(refs)
    take = lambda: refs.pop(0)
    x_ref, chunk_ref = take(), take()
    if first or last:
        c_ref, names_ref, router_ref = take(), take(), take()
    if not first:
        low_ref, made_in, back_in = take(), take(), take()
    if last and not first:
        gate_in = take()
    hidden_ref, dboth_ref = take(), take()
    if first:
        low_out = take()
    if first and not last:
        gate_out = take()
    made_ref, back_ref = take(), take()
    if last:
        drouter_ref = take()
    down_s = take()
    rows, width = x_ref.shape
    x = x_ref[...]
    own = lax.broadcasted_iota(jnp.int32, (1, LANES), 1) == lax.axis_index("exp")
    if first:
        names = names_ref[...].astype(F32)
        logits = dot_last(x, router_ref[...]) * names
        mine = jnp.sum(jnp.where(own, logits, 0.0), axis=1, keepdims=True)
        theirs = jnp.sum(jnp.where(own, 0.0, logits), axis=1, keepdims=True)
        gate = jax.nn.sigmoid(mine - theirs)
        low_out[...] = (gate * c_ref[...].astype(F32)).astype(BF16)
        if not last:
            gate_out[...] = jnp.broadcast_to(gate, (rows, LANES))
        low_ref = low_out
    elif last:
        gate = gate_in[...][:, :1]
    @pl.when(pl.program_id(0) == 0)
    def _():
        for (row, column), (to_row, to_column), (high, wide) in down_blocks(units, width, count):
            from_columns = slice(2 * units + column, 2 * units + column + wide)
            down_s[to_row : to_row + high, to_column : to_column + wide] = chunk_ref[row : row + high, from_columns]

    for t in range(units // FF_TILE):
        at = slice(t * FF_TILE, (t + 1) * FF_TILE)
        up_at = slice(units + t * FF_TILE, units + (t + 1) * FF_TILE)
        gate_pre = dot(x, chunk_ref[:, at])
        up_pre = dot(x, chunk_ref[:, up_at])
        hidden_grad = dot_last(low_ref[...], down_s[at, :])
        root = 0.7978845608028654
        square = gate_pre * gate_pre
        bent = jnp.tanh(gate_pre * (root + root * 0.044715 * square))
        half = 0.5 * (1.0 + bent)
        act = gate_pre * half
        slope = half + 0.5 * gate_pre * (1.0 - bent * bent) * (root + 3.0 * root * 0.044715 * square)
        hidden_ref[:, at] = (act * up_pre).astype(BF16)
        dboth_ref[:, at] = (hidden_grad * up_pre * slope).astype(BF16)
        dboth_ref[:, up_at] = (hidden_grad * act).astype(BF16)
    made = dot(hidden_ref[...], down_s[...])
    back = dot_last(dboth_ref[...], chunk_ref[:, : 2 * units])
    if not first:
        made = made + made_in[...]
        back = back + back_in[...]
    if last:
        made = made.astype(BF16).astype(F32)
        names = names_ref[...].astype(F32)
        push = jnp.sum(c_ref[...].astype(F32) * made, axis=1, keepdims=True)
        push = push * gate * (1.0 - gate)
        logits_grad = push * jnp.where(own, names, -names)
        high = logits_grad.astype(BF16)
        low = (logits_grad - high.astype(F32)).astype(BF16)
        made = gate * made
        back = back + dot(high, router_ref[...]) + dot(low, router_ref[...])
        turned = x.T
        update = dot(turned, high) + dot(turned, low)

        @pl.when(pl.program_id(0) == 0)
        def _():
            drouter_ref[...] = update

        @pl.when(pl.program_id(0) > 0)
        def _():
            drouter_ref[...] += update

    made_ref[...] = made.astype(made_ref.dtype)
    back_ref[...] = back.astype(back_ref.dtype)


def run_expert(first, last, units, count, x, chunk, extras, carried):
    rows, width = x.shape
    whole = lambda i: (0, 0)
    step = lambda i: (i, 0)
    wide = pl.BlockSpec((ROW_TILE, width), step)
    thin = pl.BlockSpec((ROW_TILE, LANES), step)
    struct = jax.ShapeDtypeStruct
    cot_in, names_in, router = extras
    operands = [x, chunk]
    in_specs = [wide, pl.BlockSpec(chunk.shape, whole, pipeline_mode=pl.Buffered(1))]
    if first or last:
        operands += [cot_in, names_in, router]
        in_specs += [wide, thin, pl.BlockSpec((LANES, width), whole)]
    if not first:
        low, made, back, gate = carried
        operands += [low, made, back]
        in_specs += [wide, wide, wide]
        if last:
            operands.append(gate)
            in_specs.append(thin)
    out_shape = [struct((rows, units), BF16), struct((rows, 2 * units), BF16)]
    out_specs = [pl.BlockSpec((ROW_TILE, units), step), pl.BlockSpec((ROW_TILE, 2 * units), step)]
    if first:
        out_shape.append(struct((rows, width), BF16))
        out_specs.append(wide)
        if not last:
            out_shape.append(struct((rows, LANES), F32))
            out_specs.append(thin)
    kept = BF16 if last else F32
    out_shape += [struct((rows, width), kept), struct((rows, width), kept)]
    out_specs += [wide, wide]
    if last:
        out_shape.append(struct((width, LANES), F32))
        out_specs.append(pl.BlockSpec((width, LANES), whole))
    outs = list(
        pl.pallas_call(
            functools.partial(expert_kernel, first, last, units, count),
            grid=(rows // ROW_TILE,),
            in_specs=in_specs,
            out_specs=out_specs,
            out_shape=out_shape,
            scratch_shapes=[pltpu.VMEM((units, width), BF16)],
            compiler_params=params(),
            cost_estimate=brief(),
            name="expert",
        )(*operands)
    )
    hidden, dboth = outs[:2]
    if first:
        low = outs[2]
        gate = None if last else outs[3]
    if last:
        made, back, drouter = outs[-3:]
        return hidden, dboth, (low, made, back, gate), drouter
    made, back = outs[-2:]
    return hidden, dboth, (low, made, back, gate), None


def expert_weights_kernel(units, count, x_ref, low_ref, dboth_ref, hidden_ref, grad_ref, x_turned, hidden_turned, rest):
    step = pl.program_id(0)
    tile = low_ref.shape[1]
    width = x_ref.shape[1]
    both_steps = 2 * units // tile

    @pl.when(step == 0)
    def _():
        x_turned[...] = x_ref[...].T

    @pl.when(step < both_steps)
    def _():
        grad_ref[...] = dot(x_turned[...], dboth_ref[...]).astype(BF16)

    @pl.when(step == both_steps)
    def _():
        hidden_turned[...] = hidden_ref[...].T

    blocks = down_blocks(units, width, count)
    if len(blocks) == 1:

        @pl.when(step >= both_steps)
        def _():
            grad_ref[...] = dot(hidden_turned[...], low_ref[...]).astype(BF16)

    else:
        @pl.when(step == both_steps)
        def _():
            rest[...] = dot(hidden_turned[...], low_ref[...]).astype(BF16)

        for place in range(width // tile - 1):

            @pl.when(step == both_steps + 1 + place)
            def _(place=place):
                total = dot(hidden_turned[...], low_ref[...]).astype(BF16)
                for (row, column), (from_row, from_column), (high, wide) in blocks:
                    if from_column == 0:
                        grad_ref[row : row + high, :] = total[from_row : from_row + high]
                    elif column == place * tile:
                        grad_ref[row : row + high, :] = rest[from_row : from_row + high, :]


def expert_weights(units, count, x, low, dboth, hidden):
    rows, width = x.shape
    tile = 256
    both_steps, down_steps = 2 * units // tile, width // tile
    uneven = units < width
    if uneven:
        assert width - width * units // width == tile
    columns = 2 * units + width - (tile if uneven else 0)
    whole = lambda i: (0, 0)

    def low_at(i):
        place = jnp.maximum(i - both_steps, 0)
        return (0, lax.rem(place + down_steps - 1, down_steps) if uneven else place)

    def grad_at(i):
        return (0, jnp.where(i < both_steps, i, jnp.maximum(i - 1, both_steps)) if uneven else i)

    return pl.pallas_call(
        functools.partial(expert_weights_kernel, units, count),
        grid=(both_steps + down_steps,),
        in_specs=[
            pl.BlockSpec((rows, width), whole),
            pl.BlockSpec((rows, tile), low_at),
            pl.BlockSpec((rows, tile), lambda i: (0, jnp.minimum(i, both_steps - 1))),
            pl.BlockSpec((rows, units), whole),
        ],
        out_specs=pl.BlockSpec((width, tile), grad_at),
        out_shape=jax.ShapeDtypeStruct((width, columns), BF16),
        scratch_shapes=[
            pltpu.VMEM((width, rows), BF16),
            pltpu.VMEM((units, rows), BF16),
            pltpu.VMEM((units, tile), BF16),
        ],
        compiler_params=params(),
        cost_estimate=brief(),
        name="expert_weights",
    )(x, low, dboth, hidden)


def ctx_moves(distance):
    devices = range(lax.axis_size("ctx"))
    return [(i - distance, i) for i in devices if i - distance in devices]


def after(value, *others):
    return lax.optimization_barrier((value,) + others)[0]


def gather_ctx(piece, marks=()):
    count, index, size = lax.axis_size("ctx"), lax.axis_index("ctx"), piece.shape[0]
    full = jnp.zeros((count * size,) + piece.shape[1:], piece.dtype)
    place = lambda buffer, part, at: lax.dynamic_update_slice_in_dim(buffer, part, at * size, 0)
    full = place(full, piece, index)
    up = down = piece
    for hop in range(1, count):
        up, down = shift_ctx(up, 1), shift_ctx(down, -1)
        if hop <= len(marks):
            up, down, _ = lax.optimization_barrier((up, down, marks[hop - 1]))
        for part, at, held in ((up, index - hop, index >= hop), (down, index + hop, index + hop < count)):
            at = jnp.clip(at, 0, count - 1)
            old = lax.dynamic_slice_in_dim(full, at * size, size, 0)
            full = place(full, jnp.where(held, part, old), at)
    return full


def swap_exp(block, bit):
    return lax.ppermute(block, "exp", [(i, i ^ bit) for i in range(lax.axis_size("exp"))])


def bit_set(bit):
    return (lax.axis_index("exp") // bit) % 2 == 1


def exp_bits():
    size, bits = lax.axis_size("exp"), []
    while 1 << len(bits) < size:
        bits.append(1 << len(bits))
    return bits


def gather_both(piece, marks):
    count = lax.axis_size("ctx")
    bits = exp_bits()
    start = column = gather_ctx(piece[None])
    if marks:
        column = after(column, marks[0])
    halves = []
    for half, order in ((column[: count // 2], bits[1:]), (column[count // 2 :], bits[:0:-1])):
        half = half[None]
        for bit in order:
            other = swap_exp(half, bit)
            half = jnp.where(bit_set(bit), jnp.concatenate([other, half]), jnp.concatenate([half, other]))
        halves.append((half, order))
    done = []
    for half, order in halves:
        half = after(half, marks[-1])
        other = swap_exp(half, 1)
        mine_first = bit_set(1)
        pair = jnp.stack([jnp.where(mine_first, other, half), jnp.where(mine_first, half, other)])
        shape = (2,) + (2,) * len(order) + half.shape[1:]
        pair = pair.reshape(shape)
        axes = [1 + order[::-1].index(bit) for bit in bits[:0:-1]] + [0]
        axes = [len(axes)] + axes + list(range(len(axes) + 1, pair.ndim))
        pair = pair.transpose(axes)
        done.append(pair.reshape((count // 2, 1 << len(bits)) + piece.shape))
    return done, start


def join_weights(done, first, rows):
    width = done[0].shape[-1]
    return jnp.concatenate([half[:, :, first : first + rows].reshape(-1, width) for half in done])


def scatter_ctx(parts, marks=(), seen=None):
    count, index = lax.axis_size("ctx"), lax.axis_index("ctx")

    def part(at):
        return lax.dynamic_index_in_dim(parts, jnp.clip(at, 0, count - 1), 0, keepdims=False).astype(F32)

    up = down = None
    for hop in range(1, count):
        distance = count - hop
        mine_up, mine_down = part(index + distance), part(index - distance)
        up = mine_up if up is None else mine_up + up.astype(F32)
        down = mine_down if down is None else mine_down + down.astype(F32)
        route = [(i, i + 1) for i in range(hop)]
        up = lax.ppermute(up.astype(BF16), "ctx", route)
        down = lax.ppermute(down.astype(BF16), "ctx", [(count - 1 - i, count - 1 - j) for i, j in route])
        if hop <= len(marks) and marks[hop - 1] is not None:
            up, down, _ = lax.optimization_barrier((up, down, marks[hop - 1]))
        if seen is not None:
            seen.append((up, down))
    if seen is not None:
        return part(index)
    return part(index) + up.astype(F32) + down.astype(F32)


def scatter_both(keep, send):
    count, bits = lax.axis_size("ctx"), exp_bits()
    whole = keep.astype(F32) + swap_exp(send, 1).astype(F32)
    chip = whole.reshape((count, -1) + whole.shape[1:])
    sums = []
    for half, order in ((chip[: count // 2], bits[1:]), (chip[count // 2 :], bits[:0:-1])):
        half = half.reshape((count // 2,) + (2,) * (len(bits) - 1) + half.shape[2:])
        left = bits[:0:-1]
        for bit in order:
            axis = 1 + left.index(bit)
            low = lax.index_in_dim(half, 0, axis, keepdims=False)
            high = lax.index_in_dim(half, 1, axis, keepdims=False)
            keep = jnp.where(bit_set(bit), high, low)
            send = jnp.where(bit_set(bit), low, high).astype(BF16)
            half = keep + swap_exp(send, bit).astype(F32)
            left = [b for b in left if b != bit]
        sums.append(half)
    return scatter_ctx(jnp.concatenate(sums)), whole


def slab_kernel(part, x_ref, q_ref, k_ref, v_ref, o_ref, g_ref, tail_ref, keep_ref, send_ref, x_turned, o_turned, total):
    core = lax.rem(lax.axis_index("exp"), 2)
    own = q_ref.shape[0]

    @pl.when(pl.program_id(0) == 0)
    def _():
        x_turned[...] = x_ref[...].T
        o_turned[...] = o_ref[...].T

    for place, (left, right) in enumerate(
        (
            (x_turned[:, x_turned.shape[1] - own :], q_ref[...]),
            (x_turned[...], k_ref[...]),
            (x_turned[...], v_ref[...]),
            (o_turned[...], g_ref[...]),
        )
    ):
        total[...] = dot(left, right)
        rows = slice(place * part, (place + 1) * part)
        for slab in range(keep_ref.shape[0]):
            first = 2 * slab * part
            keep_ref[slab, rows, :] = total[pl.ds(first + core * part, part), :].astype(BF16)
            send_ref[slab, rows, :] = total[pl.ds(first + (1 - core) * part, part), :].astype(BF16)
    for slab in range(keep_ref.shape[0]):
        keep_ref[slab, 4 * part :, :] = tail_ref[2 * slab + core]
        send_ref[slab, 4 * part :, :] = tail_ref[2 * slab + 1 - core]


def make_slabs(normed_all, query_grad, key_grad, value_grad, attended, branch_grad, tail):
    devices, extra, width = tail.shape
    all_rows, own = normed_all.shape[0], query_grad.shape[0]
    part, tile = width // devices, 256
    slab_rows = 4 * part + extra
    whole = lambda i: (0, 0)
    column = lambda i: (0, i)
    out = pl.BlockSpec((devices // 2, slab_rows, tile), lambda i: (0, 0, i))
    shape = jax.ShapeDtypeStruct((devices // 2, slab_rows, width), BF16)
    return pl.pallas_call(
        functools.partial(slab_kernel, part),
        grid=(width // tile,),
        in_specs=[
            pl.BlockSpec((all_rows, width), whole),
            pl.BlockSpec((own, tile), column),
            pl.BlockSpec((all_rows, tile), column),
            pl.BlockSpec((all_rows, tile), column),
            pl.BlockSpec((own, width), whole),
            pl.BlockSpec((own, tile), column),
            pl.BlockSpec((devices, extra, tile), lambda i: (0, 0, i)),
        ],
        out_specs=[out, out],
        out_shape=[shape, shape],
        scratch_shapes=[
            pltpu.VMEM((width, all_rows), BF16),
            pltpu.VMEM((width, own), BF16),
            pltpu.VMEM((width, tile), F32),
        ],
        compiler_params=params(),
        cost_estimate=brief(),
        name="slabs",
    )(normed_all, query_grad, key_grad, value_grad, attended, branch_grad, tail)


def exchange(blocks):
    return lax.all_to_all(blocks, "exp", split_axis=0, concat_axis=0, tiled=True)


def body(
    tokens,
    w_query,
    w_key,
    w_value,
    w_out,
    w_router,
    gain_attn,
    gain_mlp,
    pos_bias,
    exp_gate,
    exp_up,
    exp_down,
    doc_lengths,
    bucket_of,
    expert_ids,
    cotangent,
):
    both = ("ctx", "exp")
    own_tokens = tokens[0]
    rows, width = own_tokens.shape
    experts = w_router.shape[1]
    capacity = (5 * TOP * rows + 4 * experts - 1) // (4 * experts)
    reach = (WINDOW + rows - 2) // rows
    scale = HEAD_DIM ** (-0.5)
    ctx_index, ctx_count = lax.axis_index("ctx"), lax.axis_size("ctx")
    exp_index = lax.axis_index("exp")
    part = w_query.shape[0]
    bias_part = pos_bias.shape[0]
    devices = width // part

    small = jnp.concatenate([w_router.reshape(-1), gain_attn, gain_mlp, pos_bias])
    small = jnp.pad(small, (0, width - small.shape[0]))[None]
    small = jnp.pad(small, ((0, 15), (0, 0)))
    halo = [own_tokens]
    for _ in range(reach):
        halo.insert(0, shift_ctx(halo[0], 1))
    dense, column = gather_both(
        jnp.concatenate([w_query, w_key, w_value, w_out, small], axis=0), halo[-2::-1]
    )
    full_query, full_key, full_value, full_out = (join_weights(dense, i * part, part) for i in range(4))
    small = join_weights(dense, 4 * part, 1)
    at = part * experts
    full_router = small[:, :at].reshape(width, experts)
    full_gain_attn = small[:, at : at + part].reshape(width).astype(F32)
    full_gain_mlp = small[:, at + part : at + 2 * part].reshape(width).astype(F32)
    table = small[:, at + 2 * part : at + 2 * part + bias_part].reshape(HEADS, BUCKETS)

    inputs_all = jnp.concatenate(halo, axis=0).astype(F32)
    inputs = own_tokens.astype(F32)

    held, share = exp_gate.shape[1], exp_down.shape[1]
    chunks, first = [], 0
    while first < share:
        size = min(held, share - first)
        units = size * ctx_count
        columns = [slice(z * share + first, z * share + first + size) for z in range(ctx_count)]
        parts = [weight[0][:, at] for weight in (exp_gate, exp_up) for at in columns]
        down = exp_down[0][first : first + size]
        if size < held:
            wide, spare = width * size // held, held - size
            below = [down[m * spare : (m + 1) * spare, wide:] for m in range(size // spare)]
            down = jnp.concatenate([down[:, :wide], jnp.concatenate(below, axis=1)], axis=0)
        packed = after(jnp.concatenate(parts + [down], axis=1), column, halo[0])
        chunks.append((units, size, lax.all_gather(packed, "ctx", axis=0, tiled=True)))
        first += size

    expert_range = jnp.arange(experts, dtype=jnp.int32)
    named = jnp.any(expert_ids[0][:, :, None] == expert_range, axis=1)
    named_low = named.astype(BF16)
    step = jnp.arange(rows, dtype=jnp.int32)
    earlier = (step[:, None] > step[None, :]).astype(BF16)
    slots = dot(earlier, named_low).astype(jnp.int32)
    slots = jnp.where(named, slots, -1).T
    routes = (slots[:, None, :] == jnp.arange(capacity, dtype=jnp.int32)[None, :, None]).astype(BF16)
    routes = routes.reshape(experts * capacity, rows)

    names = jnp.pad(named_low, ((0, 0), (0, LANES - experts)))
    early = dot(routes, jnp.concatenate([cotangent[0], names], axis=1)).astype(BF16)
    early = after(early, full_router)
    early = exchange(early.reshape(experts, capacity, width + LANES)).reshape(-1, width + LANES)
    cot_in, names_in = early[:, :width], early[:, width:]

    onehot_bucket = (bucket_of[None, :] == jnp.arange(BUCKETS, dtype=jnp.int32)[:, None]).astype(BF16)
    band = make_band(dot(table, onehot_bucket))
    ends = jnp.cumsum(doc_lengths[0])

    def documents(positions):
        return jnp.sum((positions[:, None] >= ends[None, :]).astype(jnp.int32), axis=1)[:, None]

    feature = (jnp.arange(2 * HEAD_DIM, dtype=jnp.int32) % HEAD_DIM)[None, :]
    docs = doc_lengths.shape[1] + 1
    query_pos = ctx_index * rows + step
    key_pos = (ctx_index - reach) * rows + jnp.arange((reach + 1) * rows, dtype=jnp.int32)
    query_doc = (feature == documents(query_pos)).astype(BF16)
    same = (feature == documents(key_pos)) & (key_pos[:, None] >= 0)
    key_doc = jnp.where(same | (feature >= docs), 0.0, NEGATIVE).astype(BF16)

    normed_all = norm_rows(inputs_all, full_gain_attn).astype(BF16)
    normed = normed_all[reach * rows :]
    queries = (dot(normed, full_query).astype(BF16)) * jnp.asarray(scale, BF16)
    keys = dot(normed_all, full_key).astype(BF16)
    values = dot(normed_all, full_value).astype(BF16)
    attended, lse = attend(queries, keys, values, query_doc, key_doc, band)
    middle = inputs + dot(attended, full_out)
    normed_mlp = norm_rows(middle, full_gain_mlp).astype(BF16)

    sent = dot(routes, normed_mlp).astype(BF16)
    arrived = exchange(sent.reshape(experts, capacity, width)).reshape(-1, width)
    router_turned = jnp.pad(full_router.T, ((0, LANES - experts), (0, 0)))
    extras = (cot_in, names_in, router_turned)
    carried, grads, rows_in, seen = None, [], arrived, []
    first_sum = None
    for place, (units, _, chunk) in enumerate(chunks):
        last = place == len(chunks) - 1
        hidden, dboth, carried, router_grad = run_expert(
            place == 0, last, units, ctx_count, rows_in, chunk, extras, carried
        )
        grads.append(expert_weights(units, ctx_count, arrived, carried[0], dboth, hidden))
        if place == 0:
            first_sum = scatter_ctx(grads[0].reshape(ctx_count, held, -1), (), seen)
        rows_in = after(arrived, grads[-1], *seen[min(place, len(seen) - 1)])
    _, made, back, _ = carried
    back = exchange(back.reshape(experts, capacity, width)).reshape(-1, width)
    made = exchange(made.reshape(experts, capacity, width)).reshape(-1, width)
    back = after(back, grads[-1])
    output = (middle + dot_rows(routes, made)).astype(BF16)

    upstream = cotangent[0].astype(F32)
    normed_mlp_grad = dot_rows(routes, back)
    _, second_pull = jax.vjp(norm_rows, middle, full_gain_mlp)
    middle_norm_grad, gain_mlp_grad = second_pull(normed_mlp_grad)
    middle_grad = upstream + middle_norm_grad
    branch_grad = middle_grad.astype(BF16)
    attended_grad = dot_last(branch_grad, full_out).astype(BF16)
    query_grad, key_grad, value_grad, band_grad = attend_back(
        queries, keys, values, attended_grad, attended, lse, query_doc, key_doc, band
    )
    bias_grad = jnp.dot(
        sum_band(band_grad), onehot_bucket.T.astype(F32), precision=lax.Precision.HIGHEST
    )

    normed_grad_all = dot_last(key_grad, full_key) + dot_last(value_grad, full_value)
    own_grad = normed_grad_all[reach * rows :] + dot_last(query_grad, full_query)
    halo_grad = normed_grad_all[: reach * rows]
    _, first_pull = jax.vjp(norm_rows, inputs_all, full_gain_attn)
    gain_attn_grad = first_pull(jnp.concatenate([halo_grad, own_grad], axis=0))[1]
    tail = jnp.concatenate(
        [
            router_grad[:, :experts].reshape(devices, -1),
            gain_attn_grad.reshape(devices, part),
            gain_mlp_grad.reshape(devices, part),
            bias_grad.reshape(devices, bias_part),
        ],
        axis=1,
    ).astype(BF16)
    tail = jnp.pad(tail[:, None, :], ((0, 0), (0, 15), (0, width - tail.shape[1])))
    keep, send = make_slabs(normed_all, query_grad, key_grad, value_grad, attended, branch_grad, tail)
    sums, chip = scatter_both(keep, send)

    first_up, first_down = seen[-1]
    first_sum = first_sum + after(first_up, sums).astype(F32) + after(first_down, sums).astype(F32)
    expert_sums = [first_sum] + [lax.psum_scatter(grad, "ctx", scatter_dimension=0, tiled=True).astype(F32) for grad in grads[1:]]
    gate_parts, up_parts, down_parts = [], [], []
    for (units, size, _), total in zip(chunks, expert_sums):
        gate_parts.append(total[:, :units])
        up_parts.append(total[:, units : 2 * units])
        down = total[:, 2 * units :]
        if size < held:
            wide, spare = width * size // held, held - size
            thin = width - wide
            below = [down[size:, m * thin : (m + 1) * thin] for m in range(size // spare)]
            down = jnp.concatenate([down[:size], jnp.concatenate(below, axis=0)], axis=1)
        down_parts.append(down)
    def in_order(parts):
        shares = [part[:, z * (part.shape[1] // ctx_count) : (z + 1) * (part.shape[1] // ctx_count)]
                  for z in range(ctx_count) for part in parts]
        return jnp.concatenate(shares, axis=1)[None]

    expert_grads = (
        in_order(gate_parts),
        in_order(up_parts),
        jnp.concatenate(down_parts, axis=0)[None],
    )
    returning = None
    for stride, mark in zip(range(reach, 0, -1), [keep] * (reach - 1) + [chip]):
        piece = halo_grad[(reach - stride) * rows : (reach - stride + 1) * rows]
        piece = piece if returning is None else piece + returning.astype(F32)
        returning = after(shift_ctx(piece.astype(BF16), -1), mark)
    _, own_pull = jax.vjp(norm_rows, inputs, full_gain_attn)
    input_grad = middle_grad + own_pull(own_grad + returning.astype(F32))[0]
    tail = sums[4 * part]
    at = part * experts
    return (
        output[None],
        input_grad[None],
        sums[:part],
        sums[part : 2 * part],
        sums[2 * part : 3 * part],
        sums[3 * part : 4 * part],
        tail[:at].reshape(part, experts),
        tail[at : at + part],
        tail[at + part : at + 2 * part],
        tail[at + 2 * part : at + 2 * part + bias_part],
        expert_grads[0],
        expert_grads[1],
        expert_grads[2],
    )


def solution(mesh):
    rows3 = P("exp", "ctx", None)
    dense2 = P(("ctx", "exp"), None)
    dense1 = P(("ctx", "exp"))
    return jax.shard_map(
        body,
        mesh=mesh,
        in_specs=(
            rows3,
            dense2,
            dense2,
            dense2,
            dense2,
            dense2,
            dense1,
            dense1,
            dense1,
            rows3,
            rows3,
            rows3,
            P("exp", None),
            P(),
            rows3,
            rows3,
        ),
        out_specs=(
            rows3,
            rows3,
            dense2,
            dense2,
            dense2,
            dense2,
            dense2,
            dense1,
            dense1,
            dense1,
            rows3,
            rows3,
            rows3,
        ),
        check_vma=False,
    )
```

time: 1210 us -> 885 us (0.73)
  waiting for transfers between devices: 776 us -> 336 us
  starting transfers between devices: 26.4 us -> 95.6 us
  other arithmetic: 39.1 us -> 80.5 us
  blocking collectives: 37.3 us -> 0 us
  local copies, waits for them, and re-layouts: 51 us -> 86 us
  Pallas kernels: 198 us -> 218 us
  matrix products: 62.3 us -> 47.5 us
    all_gather x4 -> x3, waiting for transfers between devices: 254 us -> 0.03 us  [body(): lax.all_gather(packed, 'ctx', axis=0, tiled=True)]
    unnamed x10 -> x5, waiting for transfers between devices: 161 us -> 0.76 us
    reduce_scatter x1 -> x0, waiting for transfers between devices: 134 us -> none  [body(): out_sum = lax.psum_scatter(out_grad, both, scatter_dimension=0, tiled=True)]
    ppermute x0 -> x23, waiting for transfers between devices: none -> 129 us  [the longest x6 72.6 us: scatter_ctx(): up = lax.ppermute(up.astype(BF16), 'ctx', route)]
    ppermute x0 -> x23, starting transfers between devices: none -> 49.1 us  [the longest x6 32.2 us: scatter_ctx(): up = lax.ppermute(up.astype(BF16), 'ctx', route)]
    all_to_all x1 -> x0, blocking collectives: 37.3 us -> none  [exchange(): lax.all_to_all(blocks, 'exp', split_axis=0, concat_axis=0, tiled=True)]
    reduce_scatter x3 -> x2, waiting for transfers between devices: 23.4 us -> 0.01 us  [body(): lax.psum_scatter(grad, 'ctx', scatter_dimension=0, tiled=True).astype(F32)]
    pallas_call x3 -> x9, Pallas kernels: 138 us -> 158 us  [the longest x3 73.8 us: run_expert(): pl.pallas_call(functools.partial(expert_kernel, first, last, units, count...]
  transfers between devices with their start and end apart: 16 -> 42, of which waited for: 12 -> 15; matrix products, arithmetic and copies ran while one was open for 12% -> 21% of each run, Pallas kernels for 7% -> 22%
where the time goes in v2:
time: 885 us; the launch traced here: 879 us
  waiting for transfers between devices  336 us (38%)
  Pallas kernels  218 us (25%)
  starting transfers between devices  95.6 us (11%)
  local copies, waits for them, and re-layouts  86 us (10%)
  other arithmetic  80.5 us (9%)
  matrix products  47.5 us (5%)
  between operations  15.3 us (2%)
    ppermute x10, waiting for transfers between devices, shift_ctx(): return lax.ppermute(block, 'ctx', route)  164 us
    pallas_call x3, Pallas kernels, run_expert(): pl.pallas_call(functools.partial(expert_kernel, first, last, units, count...  73.8 us
    ppermute x6, waiting for transfers between devices, scatter_ctx(): up = lax.ppermute(up.astype(BF16), 'ctx', route)  72.6 us
    ppermute x11, waiting for transfers between devices, swap_exp(): lax.ppermute(block, 'exp', [(i, i ^ bit) for i in range(lax.axis_size('ex...  56.7 us
    pallas_call x3, Pallas kernels, expert_weights(): pl.pallas_call(functools.partial(expert_weights_kernel, units, count), gr...  50.2 us
    all_to_all x4, waiting for transfers between devices, exchange(): lax.all_to_all(blocks, 'exp', split_axis=0, concat_axis=0, tiled=True)  42.1 us
    ppermute x6, starting transfers between devices, scatter_ctx(): up = lax.ppermute(up.astype(BF16), 'ctx', route)  32.2 us
    pallas_call x1, Pallas kernels, attend_back(): pl.pallas_call(attend_back_kernel, grid=(pairs,), in_specs=[q_spec, k_spe...  30.9 us
  transfers between devices with their start and end apart: 42, of which 15 were waited for; matrix products, arithmetic and copies ran while one was open for 21% of the time, Pallas kernels for 22%

profile of v2, /device:TPU:0, one launch (start us, length us, event | category | flops | bytes accessed | tf_op | source)
XLA Modules:
  0.0 879.4 jit_solution(16520762265905877592)
XLA Ops:
  60.0 21.2 %collective-permute-done.6 = bf16[1,144,1024]{2,1,0:T(8,128)(2,1)S(1)} collective-permute-done((bf16[1,144,1024]{2,1,0:T(8,128)(2,1)S(1)}, bf16[1,144,1024]{2,1,0:T(8,128)(2,1)S(1)}, u32[]{:S(2)}, u32[]{:S(2)}) %collective-permute-start.6) | collective-permute-done | bytes 294944 | tf_op jit(solution)/shard_map/ppermute | solution.py:30
  85.4 12.5 %collective-permute-done.11 = bf16[1,2,144,1024]{3,2,1,0:T(8,128)(2,1)} collective-permute-done((bf16[1,2,144,1024]{3,2,1,0:T(8,128)(2,1)}, bf16[1,2,144,1024]{3,2,1,0:T(8,128)(2,1)}, u32[]{:S(2)}, u32[]{:S(2)}) %collective-permute-start.11) | collective-permute-done | bytes 589856 | tf_op jit(solution)/shard_map/ppermute | solution.py:555
  103.9 34.1 %collective-permute-done.8 = bf16[1,2,144,1024]{3,2,1,0:T(8,128)(2,1)} collective-permute-done((bf16[1,2,144,1024]{3,2,1,0:T(8,128)(2,1)}, bf16[1,2,144,1024]{3,2,1,0:T(8,128)(2,1)}, u32[]{:S(2)}, u32[]{:S(2)}) %collective-permute-start.8) | collective-permute-done | bytes 589856 | tf_op jit(solution)/shard_map/ppermute | solution.py:555
  156.2 9.4 %collective-permute-done.9 = bf16[2,2,144,1024]{3,2,1,0:T(8,128)(2,1)} collective-permute-done((bf16[2,2,144,1024]{3,2,1,0:T(8,128)(2,1)}, bf16[2,2,144,1024]{3,2,1,0:T(8,128)(2,1)}, u32[]{:S(2)}, u32[]{:S(2)}) %collective-permute-start.9) | collective-permute-done | bytes 1179680 | tf_op jit(solution)/shard_map/ppermute | solution.py:555
  206.0 7.0 bias_band.1.band_ref
  213.0 7.0 convolution_convert_fusion.3.k_ref
  224.9 29.0 %attend.1 = (bf16[512,1024]{1,0:T(8,128)(2,1)}, f32[8,2,512]{2,1,0:T(2,128)}) custom-call(bf16[512,1024]{1,0:T(8,128)(2,1)} %fusion.23.q_ref, bf16[1536,1024]{1,0:T(8,128)(2,1)} %convolution_convert_fusion.3.k_ref, bf16[1536,1024]{1,0:T(8,128)(2,1)} %convolution_convert_fusion.2.v_ref, bf16[512,128]{1,0:T(8,128)(2,1)} %compare_convert_fusion.qdoc_ref, ...), custom_call_target="tpu_custom_call" | custom-call | flops 1048576 | bytes 1048576 | tf_op jit(solution)/shard_map/attend/pallas_call | solution.py:184
  271.6 26.2 %all-to-all-done = bf16[8,160,1024]{2,1,0:T(8,128)(2,1)S(1)} async-done(((bf16[8,160,1024]{2,1,0:T(8,128)(2,1)}), bf16[8,160,1024]{2,1,0:T(8,128)(2,1)S(1)}, u32[]{:S(2)}, u32[]{:S(2)}) %all-to-all-start) | async-done | bytes 2621472 | tf_op jit(solution)/shard_map/all_to_all | solution.py:709
  299.3 24.9 %expert.3 = (bf16[1280,1024]{1,0:T(8,128)(2,1)}, bf16[1280,2048]{1,0:T(8,128)(2,1)}, bf16[1280,1024]{1,0:T(8,128)(2,1)}, f32[1280,128]{1,0:T(8,128)}, f32[1280,1024]{1,0:T(8,128)}, /*index=5*/f32[1280,1024]{1,0:T(8,128)}) custom-call(bf16[1280,1024]{1,0:T(8,128)(2,1)} %bitcast.169, bf16[1024,3072]{1,0:T(8,128)(2,1)} %all-gather.4.cloned.1.call-done.refs_1_, ...), custom_call_target="tpu_custom_call" | custom-call | flops 1048576 | bytes 1048576 | tf_op jit(solution)/shard_map/expert/pallas_call | solution.py:424
  324.1 17.8 %expert_weights.3 = bf16[1024,3072]{1,0:T(8,128)(2,1)} custom-call(bf16[1280,1024]{1,0:T(8,128)(2,1)} %bitcast.170, bf16[1280,1024]{1,0:T(8,128)(2,1)} %get-tuple-element.56.low_ref.refs_2_.refs_5_, bf16[1280,2048]{1,0:T(8,128)(2,1)} %get-tuple-element.57.dboth_ref, bf16[1280,1024]{1,0:T(8,128)(2,1)} %get-tuple-element.58.hidden_ref), custom_call_target="tpu_custom_call" | custom-call | flops 1048576 | bytes 1048576 | tf_op jit(solution)/shard_map/expert_weights/pallas_call | solution.py:506
  349.3 66.4 %collective-permute-done.14 = bf16[256,3072]{1,0:T(8,128)(2,1)S(1)} collective-permute-done((bf16[256,3072]{1,0:T(8,128)(2,1)S(1)}, bf16[256,3072]{1,0:T(8,128)(2,1)S(1)}, u32[]{:S(2)}, u32[]{:S(2)}) %collective-permute-start.14) | collective-permute-done | bytes 1572896 | tf_op jit(solution)/shard_map/ppermute | solution.py:615
  423.9 24.0 %expert.4 = (bf16[1280,1024]{1,0:T(8,128)(2,1)}, bf16[1280,2048]{1,0:T(8,128)(2,1)}, f32[1280,1024]{1,0:T(8,128)}, f32[1280,1024]{1,0:T(8,128)}) custom-call(bf16[1280,1024]{1,0:T(8,128)(2,1)} %bitcast.171, bf16[1024,3072]{1,0:T(8,128)(2,1)} %all-gather.6.cloned.1.call-done.refs_1_, bf16[1280,1024]{1,0:T(8,128)(2,1)} %get-tuple-element.56.low_ref.refs_2_.refs_5_, ...), custom_call_target="tpu_custom_call" | custom-call | flops 1048576 | bytes 1048576 | tf_op jit(solution)/shard_map/expert/pallas_call | solution.py:424
  447.8 17.7 %expert_weights.4 = bf16[1024,3072]{1,0:T(8,128)(2,1)} custom-call(bf16[1280,1024]{1,0:T(8,128)(2,1)} %bitcast.172, bf16[1280,1024]{1,0:T(8,128)(2,1)} %get-tuple-element.56.low_ref.refs_2_.refs_5_, bf16[1280,2048]{1,0:T(8,128)(2,1)} %get-tuple-element.63.dboth_ref, bf16[1280,1024]{1,0:T(8,128)(2,1)} %get-tuple-element.64.hidden_ref), custom_call_target="tpu_custom_call" | custom-call | flops 1048576 | bytes 1048576 | tf_op jit(solution)/shard_map/expert_weights/pallas_call | solution.py:506
  466.6 25.0 %expert.5 = (bf16[1280,768]{1,0:T(8,128)(2,1)}, bf16[1280,1536]{1,0:T(8,128)(2,1)}, bf16[1280,1024]{1,0:T(8,128)(2,1)}, bf16[1280,1024]{1,0:T(8,128)(2,1)}, f32[1024,128]{1,0:T(8,128)}) custom-call(bf16[1280,1024]{1,0:T(8,128)(2,1)} %bitcast.173, bf16[1024,2304]{1,0:T(8,128)(2,1)} %all-gather.8.cloned.1.call-done.refs_1_, ...), custom_call_target="tpu_custom_call" | custom-call | flops 1048576 | bytes 1048576 | tf_op jit(solution)/shard_map/expert/pallas_call | solution.py:424
  496.1 14.7 %expert_weights.5 = bf16[1024,2304]{1,0:T(8,128)(2,1)} custom-call(bf16[1280,1024]{1,0:T(8,128)(2,1)} %bitcast.174, bf16[1280,1024]{1,0:T(8,128)(2,1)} %get-tuple-element.56.low_ref.refs_2_.refs_5_, bf16[1280,1536]{1,0:T(8,128)(2,1)} %get-tuple-element.72.dboth_ref, bf16[1280,768]{1,0:T(8,128)(2,1)} %get-tuple-element.73.hidden_ref), custom_call_target="tpu_custom_call" | custom-call | flops 1048576 | bytes 1048576 | tf_op jit(solution)/shard_map/expert_weights/pallas_call | solution.py:506
  512.4 15.9 %all-to-all-done.3 = bf16[8,160,1024]{2,1,0:T(8,128)(2,1)} async-done(((bf16[8,160,1024]{2,1,0:T(8,128)(2,1)}), bf16[8,160,1024]{2,1,0:T(8,128)(2,1)}, u32[]{:S(2)}, u32[]{:S(2)}) %all-to-all-start.3) | async-done | bytes 2621472 | tf_op jit(solution)/shard_map/all_to_all | solution.py:709
  536.6 30.9 %attend_back.1 = (bf16[512,1024]{1,0:T(8,128)(2,1)}, bf16[1536,1024]{1,0:T(8,128)(2,1)}, bf16[1536,1024]{1,0:T(8,128)(2,1)}, f32[16,1152,128]{2,1,0:T(8,128)}) custom-call(bf16[512,1024]{1,0:T(8,128)(2,1)} %fusion.23.q_ref, bf16[1536,1024]{1,0:T(8,128)(2,1)} %convolution_convert_fusion.3.k_ref, bf16[1536,1024]{1,0:T(8,128)(2,1)} %convolution_convert_fusion.2.v_ref, ...), custom_call_target="tpu_custom_call" | custom-call | flops 1048576 | bytes 1048576 | tf_op jit(solution)/shard_map/attend_back/pallas_call | solution.py:261
  567.5 8.0 bias_band_sums.1
  593.1 7.2 fusion.3
  601.6 19.2 %slabs.1 = (bf16[16,144,1024]{2,1,0:T(8,128)(2,1)}, bf16[16,144,1024]{2,1,0:T(8,128)(2,1)}) custom-call(bf16[1536,1024]{1,0:T(8,128)(2,1)} %copy-done.11, bf16[512,1024]{1,0:T(8,128)(2,1)} %get-tuple-element.78.q_ref, bf16[1536,1024]{1,0:T(8,128)(2,1)} %get-tuple-element.76.k_ref, bf16[1536,1024]{1,0:T(8,128)(2,1)} %get-tuple-element.77.v_ref, ...), custom_call_target="tpu_custom_call" | custom-call | flops 1048576 | bytes 1048576 | tf_op jit(solution)/shard_map/slabs/pallas_call | solution.py:683
  650.8 7.8 collective-permute-start.31
  658.6 36.2 %collective-permute-done.18 = bf16[512,1024]{1,0:T(8,128)(2,1)} collective-permute-done((bf16[512,1024]{1,0:T(8,128)(2,1)S(1)}, bf16[512,1024]{1,0:T(8,128)(2,1)}, u32[]{:S(2)}, u32[]{:S(2)}) %collective-permute-start.18) | collective-permute-done | bytes 1048608 | tf_op jit(solution)/shard_map/ppermute | solution.py:30
  711.1 99.7 %collective-permute-done.19 = bf16[512,1024]{1,0:T(8,128)(2,1)} collective-permute-done((bf16[512,1024]{1,0:T(8,128)(2,1)}, bf16[512,1024]{1,0:T(8,128)(2,1)}, u32[]{:S(2)}, u32[]{:S(2)}) %collective-permute-start.19) | collective-permute-done | bytes 1048608 | tf_op jit(solution)/shard_map/ppermute | solution.py:30
  835.8 7.7 collective-permute-start.27
  (390 shorter events, 294.7 us)
Async XLA Ops:
  7.2 290.6 %all-gather.4.cloned.1.call-start = ((), (), s32[]{:S(2)}) async-start(), calls=%async_computation.6 | async-start | bytes 7864320 | tf_op jit(solution)/shard_map/all_gather | solution.py:776
  47.8 33.6 %collective-permute-start.1 = (bf16[512,1024]{1,0:T(8,128)(2,1)S(1)}, bf16[512,1024]{1,0:T(8,128)(2,1)S(1)}, u32[]{:S(2)}, u32[]{:S(2)}) collective-permute-start(bf16[512,1024]{1,0:T(8,128)(2,1)S(1)} %collective-permute-done), channel_id=1, source_target_pairs={{0,8},{8,16},{16,24},{1,9},{9,17},{17,25},{2,10},{10,18},{18,26},{... | collective-permute-start | bytes 3145736 | tf_op jit(solution)/shard_map/ppermute | solution.py:30
  81.4 342.4 %all-gather.6.cloned.1.call-start = ((), (), s32[]{:S(2)}) async-start(), calls=%async_computation.7 | async-start | bytes 7864320 | tf_op jit(solution)/shard_map/all_gather | solution.py:776
  82.2 384.4 %all-gather.8.cloned.1.call-start = ((), (), s32[]{:S(2)}) async-start(), calls=%async_computation.8 | async-start | bytes 5898240 | tf_op jit(solution)/shard_map/all_gather | solution.py:776
  99.7 42.9 %collective-permute-start.12 = (bf16[2,2,144,1024]{3,2,1,0:T(8,128)(2,1)S(1)}, bf16[2,2,144,1024]{3,2,1,0:T(8,128)(2,1)}, u32[]{:S(2)}, u32[]{:S(2)}) collective-permute-start(bf16[2,2,144,1024]{3,2,1,0:T(8,128)(2,1)S(1)} %maximum_select_fusion.3), channel_id=1, source_target_pairs={{0,2},{1,3},{2,0},{3,1},{4,6},{5,7},{6,4},{7,5},{8,10},{9,11},{10,... | collective-permute-start | bytes 3538952 | tf_op jit(solution)/shard_map/ppermute | solution.py:555
  101.5 36.5 %collective-permute-start.8 = (bf16[1,2,144,1024]{3,2,1,0:T(8,128)(2,1)}, bf16[1,2,144,1024]{3,2,1,0:T(8,128)(2,1)}, u32[]{:S(2)}, u32[]{:S(2)}) collective-permute-start(bf16[1,2,144,1024]{3,2,1,0:T(8,128)(2,1)} %get-tuple-element.213), channel_id=1, source_target_pairs={{0,2},{1,3},{2,0},{3,1},{4,6},{5,7},{6,4},{7,5},{8,10},{9,11},{10,... | collective-permute-start | bytes 1769480 | tf_op jit(solution)/shard_map/ppermute | solution.py:555
  192.1 69.3 %all-to-all-start.1 = ((bf16[8,160,1152]{2,1,0:T(8,128)(2,1)}), bf16[8,160,1152]{2,1,0:T(8,128)(2,1)}, u32[]{:S(2)}, u32[]{:S(2)}) async-start(bf16[8,160,1152]{2,1,0:T(8,128)(2,1)} %bitcast.196), calls=%async_computation.1 | async-start | bytes 5898240 | tf_op jit(solution)/shard_map/all_to_all | solution.py:709
  261.4 36.4 %all-to-all-start = ((bf16[8,160,1024]{2,1,0:T(8,128)(2,1)}), bf16[8,160,1024]{2,1,0:T(8,128)(2,1)S(1)}, u32[]{:S(2)}, u32[]{:S(2)}) async-start(bf16[8,160,1024]{2,1,0:T(8,128)(2,1)} %bitcast.201), calls=%async_computation | async-start | bytes 5242880 | tf_op jit(solution)/shard_map/all_to_all | solution.py:709
  344.2 71.6 %collective-permute-start.14 = (bf16[256,3072]{1,0:T(8,128)(2,1)S(1)}, bf16[256,3072]{1,0:T(8,128)(2,1)S(1)}, u32[]{:S(2)}, u32[]{:S(2)}) collective-permute-start(bf16[256,3072]{1,0:T(8,128)(2,1)S(1)} %get-tuple-element.137), channel_id=1, source_target_pairs={{0,8},{1,9},{2,10},{3,11},{4,12},{5,13},{6,14},{7,15}} | collective-permute-start | bytes 4718600 | tf_op jit(solution)/shard_map/ppermute | solution.py:615
  348.5 67.2 %collective-permute-start.15 = (bf16[256,3072]{1,0:T(8,128)(2,1)S(1)}, bf16[256,3072]{1,0:T(8,128)(2,1)S(1)}, u32[]{:S(2)}, u32[]{:S(2)}) collective-permute-start(bf16[256,3072]{1,0:T(8,128)(2,1)S(1)} %get-tuple-element.136), channel_id=1, source_target_pairs={{24,16},{25,17},{26,18},{27,19},{28,20},{29,21},{30,22},{31,23}} | collective-permute-start | bytes 4718600 | tf_op jit(solution)/shard_map/ppermute | solution.py:616
  418.6 48.0 %collective-permute-start.16 = (bf16[256,3072]{1,0:T(8,128)(2,1)}, bf16[256,3072]{1,0:T(8,128)(2,1)S(1)}, u32[]{:S(2)}, u32[]{:S(2)}) collective-permute-start(bf16[256,3072]{1,0:T(8,128)(2,1)} %get-tuple-element.135), channel_id=1, source_target_pairs={{0,8},{8,16},{1,9},{9,17},{2,10},{10,18},{3,11},{11,19},{4,12},{12... | collective-permute-start | bytes 4718600 | tf_op jit(solution)/shard_map/ppermute | solution.py:615
  423.1 43.5 %collective-permute-start.17 = (bf16[256,3072]{1,0:T(8,128)(2,1)}, bf16[256,3072]{1,0:T(8,128)(2,1)S(1)}, u32[]{:S(2)}, u32[]{:S(2)}) collective-permute-start(bf16[256,3072]{1,0:T(8,128)(2,1)} %get-tuple-element.134), channel_id=1, source_target_pairs={{24,16},{16,8},{25,17},{17,9},{26,18},{18,10},{27,19},{19,11},{28,... | collective-permute-start | bytes 4718600 | tf_op jit(solution)/shard_map/ppermute | solution.py:616
  491.7 36.7 %all-to-all-start.3 = ((bf16[8,160,1024]{2,1,0:T(8,128)(2,1)}), bf16[8,160,1024]{2,1,0:T(8,128)(2,1)}, u32[]{:S(2)}, u32[]{:S(2)}) async-start(bf16[8,160,1024]{2,1,0:T(8,128)(2,1)} %bitcast.200), calls=%async_computation.3 | async-start | bytes 5242880 | tf_op jit(solution)/shard_map/all_to_all | solution.py:709
  496.1 347.4 %reduce-scatter.5.cloned.1.call-start = ((), (), s32[]{:S(2)}) async-start(), calls=%async_computation.10 | async-start | bytes 5898240 | tf_op jit(solution)/shard_map/reduce_scatter | solution.py:874
  510.9 348.1 %reduce-scatter.3.cloned.1.call-start = ((), (), s32[]{:S(2)}) async-start(), calls=%async_computation.9 | async-start | bytes 7864320 | tf_op jit(solution)/shard_map/reduce_scatter | solution.py:874
  620.8 85.9 %all-to-all-start.2 = ((bf16[8,160,1024]{2,1,0:T(8,128)(2,1)}), bf16[8,160,1024]{2,1,0:T(8,128)(2,1)}, u32[]{:S(2)}, u32[]{:S(2)}) async-start(bf16[8,160,1024]{2,1,0:T(8,128)(2,1)} %bitcast.199), calls=%async_computation.2 | async-start | bytes 5242880 | tf_op jit(solution)/shard_map/all_to_all | solution.py:709
  627.0 67.9 %collective-permute-start.18 = (bf16[512,1024]{1,0:T(8,128)(2,1)S(1)}, bf16[512,1024]{1,0:T(8,128)(2,1)}, u32[]{:S(2)}, u32[]{:S(2)}) collective-permute-start(bf16[512,1024]{1,0:T(8,128)(2,1)S(1)} %slice.626), channel_id=1, source_target_pairs={{8,0},{16,8},{24,16},{9,1},{17,9},{25,17},{10,2},{18,10},{26,18},{... | collective-permute-start | bytes 3145736 | tf_op jit(solution)/shard_map/ppermute | solution.py:30
  642.5 57.0 %collective-permute-start.21 = (bf16[2,2,144,1024]{3,2,0,1:T(8,128)(2,1)S(1)}, bf16[2,2,144,1024]{3,2,0,1:T(8,128)(2,1)S(1)}, u32[]{:S(2)}, u32[]{:S(2)}) collective-permute-start(bf16[2,2,144,1024]{3,2,0,1:T(8,128)(2,1)S(1)} %fusion.27), channel_id=1, source_target_pairs={{0,2},{1,3},{2,0},{3,1},{4,6},{5,7},{6,4},{7,5},{8,10},{9,11},{10,... | collective-permute-start | bytes 3538952 | tf_op jit(solution)/shard_map/ppermute | solution.py:555
  644.7 58.2 %collective-permute-start.23 = (bf16[2,2,144,1024]{3,2,0,1:T(8,128)(2,1)S(1)}, bf16[2,2,144,1024]{3,2,0,1:T(8,128)(2,1)S(1)}, u32[]{:S(2)}, u32[]{:S(2)}) collective-permute-start(bf16[2,2,144,1024]{3,2,0,1:T(8,128)(2,1)S(1)} %fusion.28), channel_id=1, source_target_pairs={{0,4},{1,5},{2,6},{3,7},{4,0},{5,1},{6,2},{7,3},{8,12},{9,13},{10,... | collective-permute-start | bytes 3538952 | tf_op jit(solution)/shard_map/ppermute | solution.py:555
  649.6 201.6 %collective-permute-start.32 = (bf16[256,3072]{1,0:T(8,128)(2,1)}, bf16[256,3072]{1,0:T(8,128)(2,1)}, u32[]{:S(2)}, u32[]{:S(2)}) collective-permute-start(bf16[256,3072]{1,0:T(8,128)(2,1)} %get-tuple-element.133), channel_id=1, source_target_pairs={{24,16},{16,8},{8,0},{25,17},{17,9},{9,1},{26,18},{18,10},{10,2},{... | collective-permute-start | bytes 4718600 | tf_op jit(solution)/shard_map/ppermute | solution.py:616
  650.8 200.3 %collective-permute-start.31 = (bf16[256,3072]{1,0:T(8,128)(2,1)}, bf16[256,3072]{1,0:T(8,128)(2,1)}, u32[]{:S(2)}, u32[]{:S(2)}) collective-permute-start(bf16[256,3072]{1,0:T(8,128)(2,1)} %get-tuple-element.132), channel_id=1, source_target_pairs={{0,8},{8,16},{16,24},{1,9},{9,17},{17,25},{2,10},{10,18},{18,26},{... | collective-permute-start | bytes 4718600 | tf_op jit(solution)/shard_map/ppermute | solution.py:615
  698.0 112.8 %collective-permute-start.19 = (bf16[512,1024]{1,0:T(8,128)(2,1)}, bf16[512,1024]{1,0:T(8,128)(2,1)}, u32[]{:S(2)}, u32[]{:S(2)}) collective-permute-start(bf16[512,1024]{1,0:T(8,128)(2,1)} %fusion.21), channel_id=1, source_target_pairs={{8,0},{16,8},{24,16},{9,1},{17,9},{25,17},{10,2},{18,10},{26,18},{... | collective-permute-start | bytes 3145736 | tf_op jit(solution)/shard_map/ppermute | solution.py:30
  701.3 109.5 %collective-permute-start.22 = (bf16[2,144,1024]{2,1,0:T(8,128)(2,1)}, bf16[2,144,1024]{2,1,0:T(8,128)(2,1)}, u32[]{:S(2)}, u32[]{:S(2)}) collective-permute-start(bf16[2,144,1024]{2,1,0:T(8,128)(2,1)} %fusion.43), channel_id=1, source_target_pairs={{0,4},{1,5},{2,6},{3,7},{4,0},{5,1},{6,2},{7,3},{8,12},{9,13},{10,... | collective-permute-start | bytes 1769480 | tf_op jit(solution)/shard_map/ppermute | solution.py:555
  705.2 107.0 %collective-permute-start.24 = (bf16[2,144,1024]{2,1,0:T(8,128)(2,1)}, bf16[2,144,1024]{2,1,0:T(8,128)(2,1)}, u32[]{:S(2)}, u32[]{:S(2)}) collective-permute-start(bf16[2,144,1024]{2,1,0:T(8,128)(2,1)} %fusion.44), channel_id=1, source_target_pairs={{0,2},{1,3},{2,0},{3,1},{4,6},{5,7},{6,4},{7,5},{8,10},{9,11},{10,... | collective-permute-start | bytes 1769480 | tf_op jit(solution)/shard_map/ppermute | solution.py:555
  (101 other events, 1665.9 us)
Sparse Core Ops, SparseCore 0:
  81.5 117.4 all-gather.3
  200.7 113.5 all-gather.5
  315.8 128.4 all-gather.7
  511.0 89.1 reduce-scatter.4
  620.9 189.3 reduce-scatter.2

commit v3 on v2

--- a/solution.py
+++ b/solution.py
@@ -281,30 +281,42 @@
         ],
         scratch_shapes=[pltpu.VMEM((keys_rows, wide), F32), pltpu.VMEM((keys_rows, wide), F32)],
         compiler_params=params(),
-        cost_estimate=brief(),
+        cost_estimate=pl.CostEstimate(flops=20 * rows * WINDOW * width * 2, bytes_accessed=2**20, transcendentals=0),
         name="attend_back",
     )(queries, keys, values, grad, out, lse, query_doc, key_doc, band)
 
 
 def down_blocks(units, width, count):
     held, share = width // count, units // count
-    spare = held - share
-    if not spare:
-        return [((0, 0), (0, 0), (units, width))]
-    wide = width * share // held
+    extra = share - held
+    wide = width * extra // held
     blocks = []
     for z in range(count):
-        blocks.append(((z * held, 0), (z * share, 0), (share, wide)))
-        for m in range(share // spare):
-            thin = width - wide
-            blocks.append(((z * held + share, m * thin), (z * share + m * spare, wide), (spare, thin)))
+        blocks.append(((z * held, 0), (z * share, 0), (held, width)))
+        for m in range(held // extra):
+            blocks.append(((z * held + m * extra, width), (z * share + held, m * wide), (extra, wide)))
     return blocks
 
 
-def expert_kernel(first, last, units, count, *refs):
+def pack_down(down, held):
+    extra, width = down.shape[0] - held, down.shape[1]
+    wide = width * extra // held
+    rest = [down[held:, m * wide : (m + 1) * wide] for m in range(held // extra)]
+    return jnp.concatenate([down[:held], jnp.concatenate(rest, axis=0)], axis=1)
+
+
+def unpack_down(packed, size, width):
+    held = packed.shape[0]
+    extra = size - held
+    rest = [packed[m * extra : (m + 1) * extra, width:] for m in range(held // extra)]
+    return jnp.concatenate([packed[:, :width], jnp.concatenate(rest, axis=1)], axis=0)
+
+
+def expert_kernel(first, last, units, count, parts, *refs):
     refs = list(refs)
     take = lambda: refs.pop(0)
-    x_ref, chunk_ref = take(), take()
+    x_ref = take()
+    pieces = [take() for _ in range(parts)]
     if first or last:
         c_ref, names_ref, router_ref = take(), take(), take()
     if not first:
@@ -319,8 +331,31 @@
     made_ref, back_ref = take(), take()
     if last:
         drouter_ref = take()
-    down_s = take()
+    chunk_ref, down_s, sems = take(), take(), take()
     rows, width = x_ref.shape
+    held = width // count
+    index = lax.axis_index("ctx")
+
+    def slot(z):
+        return chunk_ref.at[z * held : (z + 1) * held]
+
+    @pl.when(pl.program_id(0) == 0)
+    def _():
+        if parts == 1:
+            for z in range(count):
+                pltpu.make_async_copy(pieces[0].at[z * held : (z + 1) * held], slot(z), sems.at[z]).start()
+        for z in range(count if parts > 1 else 0):
+            for here in range(count):
+                hop = abs(here - z)
+                source = pieces[0 if hop == 0 else 2 * hop - 1 if z < here else 2 * hop]
+
+                @pl.when(index == here)
+                def _(source=source, z=z):
+                    pltpu.make_async_copy(source, slot(z), sems.at[z]).start()
+
+        for z in range(count):
+            pltpu.make_async_copy(pieces[0].at[:held], slot(z), sems.at[z]).wait()
+
     x = x_ref[...]
     own = lax.broadcasted_iota(jnp.int32, (1, LANES), 1) == lax.axis_index("exp")
     if first:
@@ -386,19 +421,20 @@
     back_ref[...] = back.astype(back_ref.dtype)
 
 
-def run_expert(first, last, units, count, x, chunk, extras, carried):
+def run_expert(first, last, units, count, x, pieces, extras, carried):
     rows, width = x.shape
     whole = lambda i: (0, 0)
     step = lambda i: (i, 0)
     wide = pl.BlockSpec((ROW_TILE, width), step)
     thin = pl.BlockSpec((ROW_TILE, LANES), step)
     struct = jax.ShapeDtypeStruct
-    cot_in, names_in, router = extras
-    operands = [x, chunk]
-    in_specs = [wide, pl.BlockSpec(chunk.shape, whole, pipeline_mode=pl.Buffered(1))]
+    early, router = extras
+    operands = [x] + pieces
+    in_specs = [wide] + [pl.BlockSpec(memory_space=pl.ANY)] * len(pieces)
     if first or last:
-        operands += [cot_in, names_in, router]
-        in_specs += [wide, thin, pl.BlockSpec((LANES, width), whole)]
+        operands += [early, early, router]
+        names = pl.BlockSpec((ROW_TILE, LANES), lambda i: (i, width // LANES))
+        in_specs += [wide, names, pl.BlockSpec((LANES, width), whole)]
     if not first:
         low, made, back, gate = carried
         operands += [low, made, back]
@@ -422,12 +458,16 @@
         out_specs.append(pl.BlockSpec((width, LANES), whole))
     outs = list(
         pl.pallas_call(
-            functools.partial(expert_kernel, first, last, units, count),
+            functools.partial(expert_kernel, first, last, units, count, len(pieces)),
             grid=(rows // ROW_TILE,),
             in_specs=in_specs,
             out_specs=out_specs,
             out_shape=out_shape,
-            scratch_shapes=[pltpu.VMEM((units, width), BF16)],
+            scratch_shapes=[
+                pltpu.VMEM((width, pieces[0].shape[1]), BF16),
+                pltpu.VMEM((units, width), BF16),
+                pltpu.SemaphoreType.DMA((count,)),
+            ],
             compiler_params=params(),
             cost_estimate=brief(),
             name="expert",
@@ -444,11 +484,13 @@
     return hidden, dboth, (low, made, back, gate), None
 
 
-def expert_weights_kernel(units, count, x_ref, low_ref, dboth_ref, hidden_ref, grad_ref, x_turned, hidden_turned, rest):
+def expert_weights_kernel(
+    units, count, x_ref, low_ref, dboth_ref, hidden_ref, grad_ref, x_turned, hidden_turned, rest
+):
     step = pl.program_id(0)
     tile = low_ref.shape[1]
     width = x_ref.shape[1]
-    both_steps = 2 * units // tile
+    both_steps, down_steps = 2 * units // tile, width // tile
 
     @pl.when(step == 0)
     def _():
@@ -462,65 +504,50 @@
     def _():
         hidden_turned[...] = hidden_ref[...].T
 
-    blocks = down_blocks(units, width, count)
-    if len(blocks) == 1:
-
-        @pl.when(step >= both_steps)
-        def _():
-            grad_ref[...] = dot(hidden_turned[...], low_ref[...]).astype(BF16)
-
-    else:
-        @pl.when(step == both_steps)
-        def _():
-            rest[...] = dot(hidden_turned[...], low_ref[...]).astype(BF16)
-
-        for place in range(width // tile - 1):
-
-            @pl.when(step == both_steps + 1 + place)
-            def _(place=place):
-                total = dot(hidden_turned[...], low_ref[...]).astype(BF16)
-                for (row, column), (from_row, from_column), (high, wide) in blocks:
-                    if from_column == 0:
-                        grad_ref[row : row + high, :] = total[from_row : from_row + high]
-                    elif column == place * tile:
-                        grad_ref[row : row + high, :] = rest[from_row : from_row + high, :]
-
-
-def expert_weights(units, count, x, low, dboth, hidden):
+    for place in range(down_steps):
+
+        @pl.when(step == both_steps + place)
+        def _(place=place):
+            total = dot(hidden_turned[...], low_ref[...]).astype(BF16)
+            first = place * tile
+            for (row, column), (from_row, from_column), (high, wide) in down_blocks(units, width, count):
+                part = total[from_row : from_row + high]
+                if column == 0:
+                    grad_ref[row : row + high, :] = part
+                elif from_column <= first < from_column + wide:
+                    rest[row : row + high, first - from_column : first - from_column + tile] = part
+
+    for place in range(rest.shape[1] // tile):
+
+        @pl.when(step == both_steps + down_steps + place)
+        def _(place=place):
+            grad_ref[...] = rest[:, place * tile : (place + 1) * tile]
+
+
+def expert_weights(units, count, x, low, dboth, hidden, long=False):
     rows, width = x.shape
     tile = 256
+    extra = units - width
     both_steps, down_steps = 2 * units // tile, width // tile
-    uneven = units < width
-    if uneven:
-        assert width - width * units // width == tile
-    columns = 2 * units + width - (tile if uneven else 0)
     whole = lambda i: (0, 0)
-
-    def low_at(i):
-        place = jnp.maximum(i - both_steps, 0)
-        return (0, lax.rem(place + down_steps - 1, down_steps) if uneven else place)
-
-    def grad_at(i):
-        return (0, jnp.where(i < both_steps, i, jnp.maximum(i - 1, both_steps)) if uneven else i)
-
     return pl.pallas_call(
         functools.partial(expert_weights_kernel, units, count),
-        grid=(both_steps + down_steps,),
+        grid=(both_steps + down_steps + extra // tile,),
         in_specs=[
             pl.BlockSpec((rows, width), whole),
-            pl.BlockSpec((rows, tile), low_at),
+            pl.BlockSpec((rows, tile), lambda i: (0, jnp.clip(i - both_steps, 0, down_steps - 1))),
             pl.BlockSpec((rows, tile), lambda i: (0, jnp.minimum(i, both_steps - 1))),
             pl.BlockSpec((rows, units), whole),
         ],
-        out_specs=pl.BlockSpec((width, tile), grad_at),
-        out_shape=jax.ShapeDtypeStruct((width, columns), BF16),
+        out_specs=pl.BlockSpec((width, tile), lambda i: (0, i)),
+        out_shape=jax.ShapeDtypeStruct((width, 3 * units), BF16),
         scratch_shapes=[
             pltpu.VMEM((width, rows), BF16),
             pltpu.VMEM((units, rows), BF16),
-            pltpu.VMEM((units, tile), BF16),
+            pltpu.VMEM((width, extra), BF16),
         ],
         compiler_params=params(),
-        cost_estimate=brief(),
+        cost_estimate=pl.CostEstimate(flops=(6 * rows * width * units) if long else 2**20, bytes_accessed=2**20, transcendentals=0),
         name="expert_weights",
     )(x, low, dboth, hidden)
 
@@ -530,11 +557,11 @@
     return [(i - distance, i) for i in devices if i - distance in devices]
 
 
-def after(value, *others):
-    return lax.optimization_barrier((value,) + others)[0]
-
-
-def gather_ctx(piece, marks=()):
+def together(*values):
+    return lax.optimization_barrier(values)
+
+
+def gather_ctx(piece):
     count, index, size = lax.axis_size("ctx"), lax.axis_index("ctx"), piece.shape[0]
     full = jnp.zeros((count * size,) + piece.shape[1:], piece.dtype)
     place = lambda buffer, part, at: lax.dynamic_update_slice_in_dim(buffer, part, at * size, 0)
@@ -542,8 +569,6 @@
     up = down = piece
     for hop in range(1, count):
         up, down = shift_ctx(up, 1), shift_ctx(down, -1)
-        if hop <= len(marks):
-            up, down, _ = lax.optimization_barrier((up, down, marks[hop - 1]))
         for part, at, held in ((up, index - hop, index >= hop), (down, index + hop, index + hop < count)):
             at = jnp.clip(at, 0, count - 1)
             old = lax.dynamic_slice_in_dim(full, at * size, size, 0)
@@ -551,6 +576,38 @@
     return full
 
 
+def gather_hop(up, down, hop):
+    count = lax.axis_size("ctx")
+    route = [(i, i + 1) for i in range(hop - 1, count - 1)]
+    back = [(count - 1 - i, count - 1 - j) for i, j in route]
+    return lax.ppermute(up, "ctx", route), lax.ppermute(down, "ctx", back)
+
+
+def scatter_add(parts, hop, up=None, down=None):
+    count, index = lax.axis_size("ctx"), lax.axis_index("ctx")
+
+    def part(at):
+        return lax.dynamic_index_in_dim(parts, jnp.clip(at, 0, count - 1), 0, keepdims=False).astype(F32)
+
+    distance = count - hop
+    mine_up, mine_down = part(index + distance), part(index - distance)
+    if up is not None:
+        mine_up, mine_down = mine_up + up.astype(F32), mine_down + down.astype(F32)
+    return mine_up.astype(BF16), mine_down.astype(BF16)
+
+
+def scatter_hop(up, down, hop):
+    count = lax.axis_size("ctx")
+    route = [(i, i + 1) for i in range(hop)]
+    back = [(count - 1 - i, count - 1 - j) for i, j in route]
+    return lax.ppermute(up, "ctx", route), lax.ppermute(down, "ctx", back)
+
+
+def scatter_end(parts, up, down):
+    own = lax.dynamic_index_in_dim(parts, lax.axis_index("ctx"), 0, keepdims=False).astype(F32)
+    return own + up.astype(F32) + down.astype(F32)
+
+
 def swap_exp(block, bit):
     return lax.ppermute(block, "exp", [(i, i ^ bit) for i in range(lax.axis_size("exp"))])
 
@@ -566,32 +623,36 @@
     return bits
 
 
-def gather_both(piece, marks):
-    count = lax.axis_size("ctx")
+def routes_exp():
     bits = exp_bits()
-    start = column = gather_ctx(piece[None])
-    if marks:
-        column = after(column, marks[0])
+    return bits[1:], bits[:0:-1]
+
+
+def spread_exp(column):
+    count = column.shape[0]
     halves = []
-    for half, order in ((column[: count // 2], bits[1:]), (column[count // 2 :], bits[:0:-1])):
+    for half, order in zip((column[: count // 2], column[count // 2 :]), routes_exp()):
         half = half[None]
         for bit in order:
             other = swap_exp(half, bit)
             half = jnp.where(bit_set(bit), jnp.concatenate([other, half]), jnp.concatenate([half, other]))
-        halves.append((half, order))
+        halves.append(half)
+    return halves
+
+
+def spread_core(halves):
+    bits = exp_bits()
     done = []
-    for half, order in halves:
-        half = after(half, marks[-1])
+    for half, order in zip(halves, routes_exp()):
         other = swap_exp(half, 1)
         mine_first = bit_set(1)
         pair = jnp.stack([jnp.where(mine_first, other, half), jnp.where(mine_first, half, other)])
-        shape = (2,) + (2,) * len(order) + half.shape[1:]
-        pair = pair.reshape(shape)
+        pair = pair.reshape((2,) + (2,) * len(order) + half.shape[1:])
         axes = [1 + order[::-1].index(bit) for bit in bits[:0:-1]] + [0]
         axes = [len(axes)] + axes + list(range(len(axes) + 1, pair.ndim))
         pair = pair.transpose(axes)
-        done.append(pair.reshape((count // 2, 1 << len(bits)) + piece.shape))
-    return done, start
+        done.append(pair.reshape((half.shape[1], 1 << len(bits)) + half.shape[2:]))
+    return done
 
 
 def join_weights(done, first, rows):
@@ -599,36 +660,12 @@
     return jnp.concatenate([half[:, :, first : first + rows].reshape(-1, width) for half in done])
 
 
-def scatter_ctx(parts, marks=(), seen=None):
-    count, index = lax.axis_size("ctx"), lax.axis_index("ctx")
-
-    def part(at):
-        return lax.dynamic_index_in_dim(parts, jnp.clip(at, 0, count - 1), 0, keepdims=False).astype(F32)
-
-    up = down = None
-    for hop in range(1, count):
-        distance = count - hop
-        mine_up, mine_down = part(index + distance), part(index - distance)
-        up = mine_up if up is None else mine_up + up.astype(F32)
-        down = mine_down if down is None else mine_down + down.astype(F32)
-        route = [(i, i + 1) for i in range(hop)]
-        up = lax.ppermute(up.astype(BF16), "ctx", route)
-        down = lax.ppermute(down.astype(BF16), "ctx", [(count - 1 - i, count - 1 - j) for i, j in route])
-        if hop <= len(marks) and marks[hop - 1] is not None:
-            up, down, _ = lax.optimization_barrier((up, down, marks[hop - 1]))
-        if seen is not None:
-            seen.append((up, down))
-    if seen is not None:
-        return part(index)
-    return part(index) + up.astype(F32) + down.astype(F32)
-
-
-def scatter_both(keep, send):
+def scatter_exp(keep, send):
     count, bits = lax.axis_size("ctx"), exp_bits()
-    whole = keep.astype(F32) + swap_exp(send, 1).astype(F32)
-    chip = whole.reshape((count, -1) + whole.shape[1:])
+    chip = (keep.astype(F32) + swap_exp(send, 1).astype(F32)).astype(BF16)
+    chip = chip.reshape((count, -1) + chip.shape[1:])
     sums = []
-    for half, order in ((chip[: count // 2], bits[1:]), (chip[count // 2 :], bits[:0:-1])):
+    for half, order in zip((chip[: count // 2], chip[count // 2 :]), routes_exp()):
         half = half.reshape((count // 2,) + (2,) * (len(bits) - 1) + half.shape[2:])
         left = bits[:0:-1]
         for bit in order:
@@ -636,11 +673,18 @@
             low = lax.index_in_dim(half, 0, axis, keepdims=False)
             high = lax.index_in_dim(half, 1, axis, keepdims=False)
             keep = jnp.where(bit_set(bit), high, low)
-            send = jnp.where(bit_set(bit), low, high).astype(BF16)
-            half = keep + swap_exp(send, bit).astype(F32)
+            send = jnp.where(bit_set(bit), low, high)
+            half = (keep.astype(F32) + swap_exp(send, bit).astype(F32)).astype(BF16)
             left = [b for b in left if b != bit]
         sums.append(half)
-    return scatter_ctx(jnp.concatenate(sums)), whole
+    return jnp.concatenate(sums)
+
+
+def scatter_ctx(parts):
+    sent = (None, None)
+    for hop in range(1, lax.axis_size("ctx")):
+        sent = scatter_hop(*scatter_add(parts, hop, *sent), hop)
+    return scatter_end(parts, *sent)
 
 
 def slab_kernel(part, x_ref, q_ref, k_ref, v_ref, o_ref, g_ref, tail_ref, keep_ref, send_ref, x_turned, o_turned, total):
@@ -740,42 +784,6 @@
     bias_part = pos_bias.shape[0]
     devices = width // part
 
-    small = jnp.concatenate([w_router.reshape(-1), gain_attn, gain_mlp, pos_bias])
-    small = jnp.pad(small, (0, width - small.shape[0]))[None]
-    small = jnp.pad(small, ((0, 15), (0, 0)))
-    halo = [own_tokens]
-    for _ in range(reach):
-        halo.insert(0, shift_ctx(halo[0], 1))
-    dense, column = gather_both(
-        jnp.concatenate([w_query, w_key, w_value, w_out, small], axis=0), halo[-2::-1]
-    )
-    full_query, full_key, full_value, full_out = (join_weights(dense, i * part, part) for i in range(4))
-    small = join_weights(dense, 4 * part, 1)
-    at = part * experts
-    full_router = small[:, :at].reshape(width, experts)
-    full_gain_attn = small[:, at : at + part].reshape(width).astype(F32)
-    full_gain_mlp = small[:, at + part : at + 2 * part].reshape(width).astype(F32)
-    table = small[:, at + 2 * part : at + 2 * part + bias_part].reshape(HEADS, BUCKETS)
-
-    inputs_all = jnp.concatenate(halo, axis=0).astype(F32)
-    inputs = own_tokens.astype(F32)
-
-    held, share = exp_gate.shape[1], exp_down.shape[1]
-    chunks, first = [], 0
-    while first < share:
-        size = min(held, share - first)
-        units = size * ctx_count
-        columns = [slice(z * share + first, z * share + first + size) for z in range(ctx_count)]
-        parts = [weight[0][:, at] for weight in (exp_gate, exp_up) for at in columns]
-        down = exp_down[0][first : first + size]
-        if size < held:
-            wide, spare = width * size // held, held - size
-            below = [down[m * spare : (m + 1) * spare, wide:] for m in range(size // spare)]
-            down = jnp.concatenate([down[:, :wide], jnp.concatenate(below, axis=1)], axis=0)
-        packed = after(jnp.concatenate(parts + [down], axis=1), column, halo[0])
-        chunks.append((units, size, lax.all_gather(packed, "ctx", axis=0, tiled=True)))
-        first += size
-
     expert_range = jnp.arange(experts, dtype=jnp.int32)
     named = jnp.any(expert_ids[0][:, :, None] == expert_range, axis=1)
     named_low = named.astype(BF16)
@@ -788,12 +796,40 @@
 
     names = jnp.pad(named_low, ((0, 0), (0, LANES - experts)))
     early = dot(routes, jnp.concatenate([cotangent[0], names], axis=1)).astype(BF16)
-    early = after(early, full_router)
     early = exchange(early.reshape(experts, capacity, width + LANES)).reshape(-1, width + LANES)
-    cot_in, names_in = early[:, :width], early[:, width:]
-
+
+    held, share = exp_gate.shape[1], exp_down.shape[1]
+    sizes = (share * 5 // 11, share * 6 // 11)
+    packed, first = [], 0
+    for size in sizes:
+        columns = [slice(z * share + first, z * share + first + size) for z in range(ctx_count)]
+        parts = [weight[0][:, at] for weight in (exp_gate, exp_up) for at in columns]
+        packed.append(jnp.concatenate(parts + [pack_down(exp_down[0][first : first + size], held)], axis=1))
+        first += size
+
+    small = jnp.concatenate([w_router.reshape(-1), gain_attn, gain_mlp, pos_bias])
+    small = jnp.pad(small, (0, width - small.shape[0]))[None]
+    small = lax.all_gather(jnp.pad(small, ((0, 15), (0, 0))), both, axis=0)[:, 0]
+    at = part * experts
+    full_router = small[:, :at].reshape(width, experts)
+    full_gain_attn = small[:, at : at + part].reshape(width).astype(F32)
+    full_gain_mlp = small[:, at + part : at + 2 * part].reshape(width).astype(F32)
+    table = small[:, at + 2 * part : at + 2 * part + bias_part].reshape(HEADS, BUCKETS)
+    column = gather_ctx(jnp.concatenate([w_query, w_key, w_value, w_out], axis=0)[None])
+    halo = [shift_ctx(own_tokens, 1), own_tokens]
+    column, halo[0], early, packed[0] = together(column, halo[0], early, packed[0])
+    for _ in range(1, reach):
+        halo.insert(0, shift_ctx(halo[0], 1))
+    packed[0], halo[0] = together(packed[0], halo[0])
+    chunk0 = lax.all_gather(packed[0], "ctx", axis=0, tiled=True)
     onehot_bucket = (bucket_of[None, :] == jnp.arange(BUCKETS, dtype=jnp.int32)[:, None]).astype(BF16)
     band = make_band(dot(table, onehot_bucket))
+    *halves, band = together(*spread_exp(column), band)
+    dense = spread_core(halves)
+    full_query, full_key, full_value, full_out = (join_weights(dense, i * part, part) for i in range(4))
+    inputs_all = jnp.concatenate(halo, axis=0).astype(F32)
+    inputs = own_tokens.astype(F32)
+
     ends = jnp.cumsum(doc_lengths[0])
 
     def documents(positions):
@@ -819,23 +855,33 @@
     sent = dot(routes, normed_mlp).astype(BF16)
     arrived = exchange(sent.reshape(experts, capacity, width)).reshape(-1, width)
     router_turned = jnp.pad(full_router.T, ((0, LANES - experts), (0, 0)))
-    extras = (cot_in, names_in, router_turned)
-    carried, grads, rows_in, seen = None, [], arrived, []
-    first_sum = None
-    for place, (units, _, chunk) in enumerate(chunks):
-        last = place == len(chunks) - 1
-        hidden, dboth, carried, router_grad = run_expert(
-            place == 0, last, units, ctx_count, rows_in, chunk, extras, carried
-        )
-        grads.append(expert_weights(units, ctx_count, arrived, carried[0], dboth, hidden))
-        if place == 0:
-            first_sum = scatter_ctx(grads[0].reshape(ctx_count, held, -1), (), seen)
-        rows_in = after(arrived, grads[-1], *seen[min(place, len(seen) - 1)])
-    _, made, back, _ = carried
+    extras = (early, router_turned)
+    units0, units1 = (size * ctx_count for size in sizes)
+    arrived, packed[1] = together(arrived, packed[1])
+    up = down = packed[1]
+    pieces = [up]
+    hidden, dboth, carried, _ = run_expert(True, False, units0, ctx_count, arrived, [chunk0], extras, None)
+    grad0 = expert_weights(units0, ctx_count, arrived, carried[0], dboth, hidden)
+    sent = (None, None)
+    for hop in range(1, ctx_count):
+        up, down = gather_hop(up, down, hop)
+        if hop == 1:
+            up, down, grad0 = together(up, down, grad0)
+            parts0 = grad0.reshape(ctx_count, held, -1)
+        else:
+            sent = scatter_hop(*scatter_add(parts0, hop - 1, *sent), hop - 1)
+            up, down, *sent = together(up, down, *sent)
+        pieces += [up, down]
+    arrived, *sent = together(arrived, *scatter_add(parts0, ctx_count - 1, *sent))
+    sent = scatter_hop(*sent, ctx_count - 1)
+    hidden, dboth, carried, router_grad = run_expert(
+        False, True, units1, ctx_count, arrived, pieces, extras, carried
+    )
+    low, made, back, _ = carried
+    hidden, dboth, low, made, back, *sent = together(hidden, dboth, low, made, back, *sent)
+    grad1 = expert_weights(units1, ctx_count, arrived, low, dboth, hidden, True)
+    total1 = lax.psum_scatter(grad1, "ctx", scatter_dimension=0, tiled=True)
     back = exchange(back.reshape(experts, capacity, width)).reshape(-1, width)
-    made = exchange(made.reshape(experts, capacity, width)).reshape(-1, width)
-    back = after(back, grads[-1])
-    output = (middle + dot_rows(routes, made)).astype(BF16)
 
     upstream = cotangent[0].astype(F32)
     normed_mlp_grad = dot_rows(routes, back)
@@ -844,6 +890,8 @@
     middle_grad = upstream + middle_norm_grad
     branch_grad = middle_grad.astype(BF16)
     attended_grad = dot_last(branch_grad, full_out).astype(BF16)
+    made, attended_grad = together(made, attended_grad)
+    made = exchange(made.reshape(experts, capacity, width)).reshape(-1, width)
     query_grad, key_grad, value_grad, band_grad = attend_back(
         queries, keys, values, attended_grad, attended, lse, query_doc, key_doc, band
     )
@@ -866,23 +914,29 @@
         axis=1,
     ).astype(BF16)
     tail = jnp.pad(tail[:, None, :], ((0, 0), (0, 15), (0, width - tail.shape[1])))
+    query_grad, made = together(query_grad, made)
+    output = (middle + dot_rows(routes, made)).astype(BF16)
     keep, send = make_slabs(normed_all, query_grad, key_grad, value_grad, attended, branch_grad, tail)
-    sums, chip = scatter_both(keep, send)
-
-    first_up, first_down = seen[-1]
-    first_sum = first_sum + after(first_up, sums).astype(F32) + after(first_down, sums).astype(F32)
-    expert_sums = [first_sum] + [lax.psum_scatter(grad, "ctx", scatter_dimension=0, tiled=True).astype(F32) for grad in grads[1:]]
+    parts = scatter_exp(keep, send)
+
+    returning = None
+    for stride in range(reach, 0, -1):
+        piece = halo_grad[(reach - stride) * rows : (reach - stride + 1) * rows]
+        if returning is not None:
+            parts, returning, *sent = together(parts, returning, *sent)
+            piece = piece + returning.astype(F32)
+        returning = shift_ctx(piece.astype(BF16), -1)
+    sums = scatter_ctx(parts)
+    _, own_pull = jax.vjp(norm_rows, inputs, full_gain_attn)
+    input_grad = middle_grad + own_pull(own_grad + returning.astype(F32))[0]
+    scattered = [scatter_end(parts0, *sent), total1.astype(F32)]
     gate_parts, up_parts, down_parts = [], [], []
-    for (units, size, _), total in zip(chunks, expert_sums):
+    for size, total in zip(sizes, scattered):
+        units = size * ctx_count
         gate_parts.append(total[:, :units])
         up_parts.append(total[:, units : 2 * units])
-        down = total[:, 2 * units :]
-        if size < held:
-            wide, spare = width * size // held, held - size
-            thin = width - wide
-            below = [down[size:, m * thin : (m + 1) * thin] for m in range(size // spare)]
-            down = jnp.concatenate([down[:size], jnp.concatenate(below, axis=0)], axis=1)
-        down_parts.append(down)
+        down_parts.append(unpack_down(total[:, 2 * units :], size, width))
+
     def in_order(parts):
         shares = [part[:, z * (part.shape[1] // ctx_count) : (z + 1) * (part.shape[1] // ctx_count)]
                   for z in range(ctx_count) for part in parts]
@@ -893,13 +947,6 @@
         in_order(up_parts),
         jnp.concatenate(down_parts, axis=0)[None],
     )
-    returning = None
-    for stride, mark in zip(range(reach, 0, -1), [keep] * (reach - 1) + [chip]):
-        piece = halo_grad[(reach - stride) * rows : (reach - stride + 1) * rows]
-        piece = piece if returning is None else piece + returning.astype(F32)
-        returning = after(shift_ctx(piece.astype(BF16), -1), mark)
-    _, own_pull = jax.vjp(norm_rows, inputs, full_gain_attn)
-    input_grad = middle_grad + own_pull(own_grad + returning.astype(F32))[0]
     tail = sums[4 * part]
     at = part * experts
     return (

time: 885 us -> 767 us (0.87)
  waiting for transfers between devices: 336 us -> 248 us
  other arithmetic: 80.5 us -> 55.2 us
  local copies, waits for them, and re-layouts: 86 us -> 64.1 us
  starting transfers between devices: 95.6 us -> 110 us
    ppermute x10, waiting for transfers between devices: 164 us -> 32.2 us  [shift_ctx(): return lax.ppermute(block, 'ctx', route)]
    ppermute x12 -> x18, waiting for transfers between devices: 72.6 us -> 108 us  [the longest x12 99.5 us: scatter_hop(): return (lax.ppermute(up, 'ctx', route), lax.ppermute(down, 'ctx', back))]
    all_gather x3 -> x2, waiting for transfers between devices: 0.03 us -> 26 us  [the longest x1 26 us: body(): chunk0 = lax.all_gather(packed[0], 'ctx', axis=0, tiled=True)]
    ppermute x12 -> x18, starting transfers between devices: 37.7 us -> 52.5 us  [the longest x12 40.9 us: scatter_hop(): return (lax.ppermute(up, 'ctx', route), lax.ppermute(down, 'ctx', back))]
    all_to_all x4, waiting for transfers between devices: 42.1 us -> 27.3 us  [exchange(): lax.all_to_all(blocks, 'exp', split_axis=0, concat_axis=0, tiled=True)]
    add x7 -> x2, other arithmetic: 15 us -> 3.51 us  [scatter_end(): return own + up.astype(F32) + down.astype(F32)]
    slice x13 -> x16, local copies, waits for them, and re-layouts: 19.6 us -> 10.1 us  [the longest x2 2.06 us: body(): exp_down[0][first:first + size]]
    unnamed x179 -> x148, local copies, waits for them, and re-layouts: 29.2 us -> 22.6 us
  transfers between devices with their start and end apart: 42 -> 46, of which waited for: 15 -> 24; matrix products, arithmetic and copies ran while one was open for 21% -> 19% of each run, Pallas kernels for 22% -> 28%
where the time goes in v3:
time: 767 us; the launch traced here: 757 us
  waiting for transfers between devices  248 us (32%)
  Pallas kernels  211 us (28%)
  starting transfers between devices  110 us (14%)
  local copies, waits for them, and re-layouts  64.1 us (8%)
  other arithmetic  55.2 us (7%)
  matrix products  51 us (7%)
  between operations  17.3 us (2%)
    ppermute x12, waiting for transfers between devices, scatter_hop(): return (lax.ppermute(up, 'ctx', route), lax.ppermute(down, 'ctx', back))  99.5 us
    pallas_call x2, Pallas kernels, run_expert(): pl.pallas_call(functools.partial(expert_kernel, first, last, units, count...  73 us
    ppermute x11, waiting for transfers between devices, swap_exp(): lax.ppermute(block, 'exp', [(i, i ^ bit) for i in range(lax.axis_size('ex...  54.2 us
    pallas_call x2, Pallas kernels, expert_weights(): pl.pallas_call(functools.partial(expert_weights_kernel, units, count), gr...  44.1 us
    ppermute x12, starting transfers between devices, scatter_hop(): return (lax.ppermute(up, 'ctx', route), lax.ppermute(down, 'ctx', back))  40.9 us
    ppermute x10, waiting for transfers between devices, shift_ctx(): return lax.ppermute(block, 'ctx', route)  32.2 us
    pallas_call x1, Pallas kernels, attend_back(): pl.pallas_call(attend_back_kernel, grid=(pairs,), in_specs=[q_spec, k_spe...  30.9 us
    ppermute x10, starting transfers between devices, shift_ctx(): return lax.ppermute(block, 'ctx', route)  29.2 us
  transfers between devices with their start and end apart: 46, of which 24 were waited for; matrix products, arithmetic and copies ran while one was open for 19% of the time, Pallas kernels for 28%

profile of v3, /device:TPU:0, one launch (start us, length us, event | category | flops | bytes accessed | tf_op | source)
XLA Modules:
  0.0 756.7 jit_solution(2076404886261954315)
XLA Ops:
  98.2 6.9 bias_band.1.band_ref
  105.2 9.8 %collective-permute-done.9 = bf16[2,2,128,1024]{3,2,1,0:T(8,128)(2,1)} collective-permute-done((bf16[2,2,128,1024]{3,2,1,0:T(8,128)(2,1)}, bf16[2,2,128,1024]{3,2,1,0:T(8,128)(2,1)}, u32[]{:S(2)}, u32[]{:S(2)}) %collective-permute-start.9) | collective-permute-done | bytes 1048608 | tf_op jit(solution)/shard_map/ppermute | solution.py:612
  150.2 29.1 %attend.1 = (bf16[512,1024]{1,0:T(8,128)(2,1)}, f32[8,2,512]{2,1,0:T(2,128)}) custom-call(bf16[512,1024]{1,0:T(8,128)(2,1)} %fusion.25.q_ref, bf16[1536,1024]{1,0:T(8,128)(2,1)} %convolution_convert_fusion.3.k_ref, bf16[1536,1024]{1,0:T(8,128)(2,1)} %convolution_convert_fusion.2.v_ref, bf16[512,128]{1,0:T(8,128)(2,1)} %compare_convert_fusion.qdoc_ref, ...), custom_call_target="tpu_custom_call" | custom-call | flops 1048576 | bytes 1048576 | tf_op jit(solution)/shard_map/attend/pallas_call | solution.py:184
  202.5 18.5 %all-to-all-done.1 = bf16[8,160,1024]{2,1,0:T(8,128)(2,1)S(1)} async-done(((bf16[8,160,1024]{2,1,0:T(8,128)(2,1)}), bf16[8,160,1024]{2,1,0:T(8,128)(2,1)S(1)}, u32[]{:S(2)}, u32[]{:S(2)}) %all-to-all-start.1) | async-done | bytes 2621472 | tf_op jit(solution)/shard_map/all_to_all | solution.py:753
  222.3 5.9 collective-permute-start.14
  229.4 26.0 %all-gather.4.cloned.1.call-done.refs_1_ = bf16[1024,3840]{1,0:T(8,128)(2,1)} async-done(((bf16[256,3840]{1,0:T(8,128)(2,1)}), bf16[1024,3840]{1,0:T(8,128)(2,1)}) %all-gather.4.cloned.1.call-update) | async-done | bytes 7864336 | tf_op jit(solution)/shard_map/all_gather | solution.py:824
  255.4 32.7 %expert.2 = (bf16[1280,1280]{1,0:T(8,128)(2,1)}, bf16[1280,2560]{1,0:T(8,128)(2,1)}, bf16[1280,1024]{1,0:T(8,128)(2,1)}, f32[1280,128]{1,0:T(8,128)}, f32[1280,1024]{1,0:T(8,128)}, /*index=5*/f32[1280,1024]{1,0:T(8,128)}) custom-call(bf16[1280,1024]{1,0:T(8,128)(2,1)} %bitcast.177, bf16[1024,3840]{1,0:T(8,128)(2,1)} %all-gather.4.cloned.1.call-done.refs_1_, ...), custom_call_target="tpu_custom_call" | custom-call | flops 1048576 | bytes 1048576 | tf_op jit(solution)/shard_map/expert/pallas_call | solution.py:460
  288.1 20.3 %expert_weights.2 = bf16[1024,3840]{1,0:T(8,128)(2,1)} custom-call(bf16[1280,1024]{1,0:T(8,128)(2,1)} %bitcast.178, bf16[1280,1024]{1,0:T(8,128)(2,1)} %get-tuple-element.128.low_ref.refs_11_, bf16[1280,2560]{1,0:T(8,128)(2,1)} %get-tuple-element.85.dboth_ref, bf16[1280,1280]{1,0:T(8,128)(2,1)} %get-tuple-element.86.hidden_ref), custom_call_target="tpu_custom_call" | custom-call | flops 1048576 | bytes 1048576 | tf_op jit(solution)/shard_map/expert_weights/pallas_call | solution.py:533
  314.0 14.1 %collective-permute-start.18 = (bf16[256,3840]{1,0:T(8,128)(2,1)S(1)}, bf16[256,3840]{1,0:T(8,128)(2,1)S(1)}, u32[]{:S(2)}, u32[]{:S(2)}) collective-permute-start(bf16[256,3840]{1,0:T(8,128)(2,1)S(1)} %get-tuple-element.179), channel_id=1, source_target_pairs={{0,8},{1,9},{2,10},{3,11},{4,12},{5,13},{6,14},{7,15}} | collective-permute-start | bytes 5898248 | tf_op jit(solution)/shard_map/ppermute | solution.py:603
  328.2 40.9 %collective-permute-done.18 = bf16[256,3840]{1,0:T(8,128)(2,1)S(1)} collective-permute-done((bf16[256,3840]{1,0:T(8,128)(2,1)S(1)}, bf16[256,3840]{1,0:T(8,128)(2,1)S(1)}, u32[]{:S(2)}, u32[]{:S(2)}) %collective-permute-start.18) | collective-permute-done | bytes 1966112 | tf_op jit(solution)/shard_map/ppermute | solution.py:603
  382.4 39.9 %collective-permute-done.22 = bf16[256,3840]{1,0:T(8,128)(2,1)S(1)} collective-permute-done((bf16[256,3840]{1,0:T(8,128)(2,1)S(1)}, bf16[256,3840]{1,0:T(8,128)(2,1)S(1)}, u32[]{:S(2)}, u32[]{:S(2)}) %collective-permute-start.22) | collective-permute-done | bytes 1966112 | tf_op jit(solution)/shard_map/ppermute | solution.py:603
  432.4 40.2 %expert.3 = (bf16[1280,1536]{1,0:T(8,128)(2,1)}, bf16[1280,3072]{1,0:T(8,128)(2,1)}, bf16[1280,1024]{1,0:T(8,128)(2,1)}, bf16[1280,1024]{1,0:T(8,128)(2,1)}, f32[1024,128]{1,0:T(8,128)}) custom-call(bf16[1280,1024]{1,0:T(8,128)(2,1)} %bitcast.179, bf16[256,4608]{1,0:T(8,128)(2,1)} %maximum_dynamic-update-slice_fusion.refs_1_, ...), custom_call_target="tpu_custom_call" | custom-call | flops 1048576 | bytes 1048576 | tf_op jit(solution)/shard_map/expert/pallas_call | solution.py:460
  480.2 23.9 %expert_weights.3 = bf16[1024,4608]{1,0:T(8,128)(2,1)} custom-call(bf16[1280,1024]{1,0:T(8,128)(2,1)} %bitcast.180, bf16[1280,1024]{1,0:T(8,128)(2,1)} %get-tuple-element.128.low_ref.refs_11_, bf16[1280,3072]{1,0:T(8,128)(2,1)} %get-tuple-element.129.dboth_ref, bf16[1280,1536]{1,0:T(8,128)(2,1)} %get-tuple-element.130.hidden_ref), custom_call_target="tpu_custom_call" | custom-call | flops 12079595520 | bytes 1048576 | tf_op jit(solution)/shard_map/expert_weights/pallas_call | solution.py:533
  504.1 7.6 %all-to-all-done.2 = bf16[8,160,1024]{2,1,0:T(8,128)(2,1)} async-done(((bf16[8,160,1024]{2,1,0:T(8,128)(2,1)}), bf16[8,160,1024]{2,1,0:T(8,128)(2,1)}, u32[]{:S(2)}, u32[]{:S(2)}) %all-to-all-start.2) | async-done | bytes 2621472 | tf_op jit(solution)/shard_map/all_to_all | solution.py:753
  524.5 30.9 %attend_back.1 = (bf16[512,1024]{1,0:T(8,128)(2,1)}, bf16[1536,1024]{1,0:T(8,128)(2,1)}, bf16[1536,1024]{1,0:T(8,128)(2,1)}, f32[16,1152,128]{2,1,0:T(8,128)}) custom-call(bf16[512,1024]{1,0:T(8,128)(2,1)} %fusion.25.q_ref, bf16[1536,1024]{1,0:T(8,128)(2,1)} %convolution_convert_fusion.3.k_ref, bf16[1536,1024]{1,0:T(8,128)(2,1)} %convolution_convert_fusion.2.v_ref, ...), custom_call_target="tpu_custom_call" | custom-call | flops 21474836480 | bytes 1048576 | tf_op jit(solution)/shard_map/attend_back/pallas_call | solution.py:261
  555.4 7.9 %bias_band_sums.1 = f32[16,1024]{1,0:T(8,128)} custom-call(f32[16,1152,128]{2,1,0:T(8,128)} %get-tuple-element.119.band_ref), custom_call_target="tpu_custom_call" | custom-call | flops 1048576 | bytes 1048576 | tf_op jit(solution)/shard_map/bias_band_sums/pallas_call | solution.py:112
  563.3 7.1 fusion.27
  570.7 9.0 %convolution_add_fusion = f32[1536,1024]{1,0:T(8,128)S(1)} fusion(f32[1536,1024]{1,0:T(8,128)} %fusion.27, bf16[1536,1024]{1,0:T(8,128)(2,1)} %get-tuple-element.116.v_ref, bf16[512,1024]{1,0:T(8,128)(2,1)S(1)} %bitcast.218, bf16[512,1024]{1,0:T(8,128)(2,1)S(1)} %bitcast.214), kind=kOutput, calls=%fused_computation.9 | convolution fusion | flops 3226992640 | bytes 17825792 | tf_op jit(solution)/shard_map/dot_general | solution.py:46
  588.8 19.1 %slabs.1 = (bf16[16,144,1024]{2,1,0:T(8,128)(2,1)}, bf16[16,144,1024]{2,1,0:T(8,128)(2,1)}) custom-call(bf16[1536,1024]{1,0:T(8,128)(2,1)} %copy-done.7, bf16[512,1024]{1,0:T(8,128)(2,1)} %get-tuple-element.117.q_ref, bf16[1536,1024]{1,0:T(8,128)(2,1)} %get-tuple-element.115.k_ref, bf16[1536,1024]{1,0:T(8,128)(2,1)} %get-tuple-element.116.v_ref, ...), custom_call_target="tpu_custom_call" | custom-call | flops 1048576 | bytes 1048576 | tf_op jit(solution)/shard_map/slabs/pallas_call | solution.py:727
  608.3 7.7 %collective-permute-done.26 = bf16[16,144,1024]{2,1,0:T(8,128)(2,1)S(1)} collective-permute-done((bf16[16,144,1024]{2,1,0:T(8,128)(2,1)}, bf16[16,144,1024]{2,1,0:T(8,128)(2,1)S(1)}, u32[]{:S(2)}, u32[]{:S(2)}) %collective-permute-start.26) | collective-permute-done | bytes 4718624 | tf_op jit(solution)/shard_map/ppermute | solution.py:612
  627.5 22.8 %collective-permute-done.29 = bf16[2,2,144,1024]{3,2,0,1:T(8,128)(2,1)S(1)} collective-permute-done((bf16[2,2,144,1024]{3,2,0,1:T(8,128)(2,1)S(1)}, bf16[2,2,144,1024]{3,2,0,1:T(8,128)(2,1)S(1)}, u32[]{:S(2)}, u32[]{:S(2)}) %collective-permute-start.29) | collective-permute-done | bytes 1179680 | tf_op jit(solution)/shard_map/ppermute | solution.py:612
  659.6 6.7 collective-permute-done.30
  668.7 16.4 %collective-permute-done.31 = bf16[512,1024]{1,0:T(8,128)(2,1)S(1)} collective-permute-done((bf16[512,1024]{1,0:T(8,128)(2,1)S(1)}, bf16[512,1024]{1,0:T(8,128)(2,1)S(1)}, u32[]{:S(2)}, u32[]{:S(2)}) %collective-permute-start.31) | collective-permute-done | bytes 1048608 | tf_op jit(solution)/shard_map/ppermute | solution.py:30
  719.3 11.3 %collective-permute-done.38 = bf16[144,1024]{1,0:T(8,128)(2,1)S(1)} collective-permute-done((bf16[144,1024]{1,0:T(8,128)(2,1)S(1)}, bf16[144,1024]{1,0:T(8,128)(2,1)S(1)}, u32[]{:S(2)}, u32[]{:S(2)}) %collective-permute-start.38) | collective-permute-done | bytes 294944 | tf_op jit(solution)/shard_map/ppermute | solution.py:603
  (364 shorter events, 284.6 us)
Async XLA Ops:
  8.0 88.1 %all-gather.6.cloned.1.call-start = ((), (), s32[]{:S(2)}) async-start(), calls=%async_computation.7 | async-start | bytes 1081344 | tf_op jit(solution)/shard_map/all_gather | solution.py:812
  9.7 37.2 %collective-permute-start = (bf16[1,128,1024]{2,1,0:T(8,128)(2,1)}, bf16[1,128,1024]{2,1,0:T(8,128)(2,1)}, u32[]{:S(2)}, u32[]{:S(2)}) collective-permute-start(bf16[1,128,1024]{2,1,0:T(8,128)(2,1)} %maximum_bitcast_fusion.2), channel_id=1, source_target_pairs={{0,8},{8,16},{16,24},{1,9},{9,17},{17,25},{2,10},{10,18},{18,26},{... | collective-permute-start | bytes 786440 | tf_op jit(solution)/shard_map/ppermute | solution.py:30
  15.3 33.4 %collective-permute-start.1 = (bf16[1,128,1024]{2,1,0:T(8,128)(2,1)}, bf16[1,128,1024]{2,1,0:T(8,128)(2,1)}, u32[]{:S(2)}, u32[]{:S(2)}) collective-permute-start(bf16[1,128,1024]{2,1,0:T(8,128)(2,1)} %maximum_bitcast_fusion.2), channel_id=1, source_target_pairs={{8,0},{16,8},{24,16},{9,1},{17,9},{25,17},{10,2},{18,10},{26,18},{... | collective-permute-start | bytes 786440 | tf_op jit(solution)/shard_map/ppermute | solution.py:30
  18.9 53.3 %collective-permute-start.6 = (bf16[512,1024]{1,0:T(8,128)(2,1)}, bf16[512,1024]{1,0:T(8,128)(2,1)}, u32[]{:S(2)}, u32[]{:S(2)}) collective-permute-start(bf16[512,1024]{1,0:T(8,128)(2,1)} %bitcast.181), channel_id=1, source_target_pairs={{0,8},{8,16},{16,24},{1,9},{9,17},{17,25},{2,10},{10,18},{18,26},{... | collective-permute-start | bytes 3145736 | tf_op jit(solution)/shard_map/ppermute | solution.py:30
  31.1 42.3 %all-to-all-start = ((bf16[8,160,1152]{2,1,0:T(8,128)(2,1)}), bf16[8,160,1152]{2,1,0:T(8,128)(2,1)S(1)}, u32[]{:S(2)}, u32[]{:S(2)}) async-start(bf16[8,160,1152]{2,1,0:T(8,128)(2,1)} %bitcast.196), calls=%async_computation | async-start | bytes 5898240 | tf_op jit(solution)/shard_map/all_to_all | solution.py:753
  34.9 220.5 %all-gather.4.cloned.1.call-start = ((), (), s32[]{:S(2)}) async-start(), calls=%async_computation.5 | async-start | bytes 9830400 | tf_op jit(solution)/shard_map/all_gather | solution.py:824
  78.3 26.9 %collective-permute-start.7 = (bf16[512,1024]{1,0:T(8,128)(2,1)}, bf16[512,1024]{1,0:T(8,128)(2,1)}, u32[]{:S(2)}, u32[]{:S(2)}) collective-permute-start(bf16[512,1024]{1,0:T(8,128)(2,1)} %collective-permute-done.6), channel_id=1, source_target_pairs={{0,8},{8,16},{16,24},{1,9},{9,17},{17,25},{2,10},{10,18},{18,26},{... | collective-permute-start | bytes 3145736 | tf_op jit(solution)/shard_map/ppermute | solution.py:30
  185.1 35.9 %all-to-all-start.1 = ((bf16[8,160,1024]{2,1,0:T(8,128)(2,1)}), bf16[8,160,1024]{2,1,0:T(8,128)(2,1)S(1)}, u32[]{:S(2)}, u32[]{:S(2)}) async-start(bf16[8,160,1024]{2,1,0:T(8,128)(2,1)} %bitcast.200), calls=%async_computation.1 | async-start | bytes 5242880 | tf_op jit(solution)/shard_map/all_to_all | solution.py:753
  221.0 87.4 %collective-permute-start.15 = (bf16[256,4608]{1,0:T(8,128)(2,1)}, bf16[256,4608]{1,0:T(8,128)(2,1)}, u32[]{:S(2)}, u32[]{:S(2)}) collective-permute-start(bf16[256,4608]{1,0:T(8,128)(2,1)} %maximum_dynamic-update-slice_fusion.refs_1_), channel_id=1, source_target_pairs={{24,16},{16,8},{8,0},{25,17},{17,9},{9,1},{26,18},{18,10},{10,2},{... | collective-permute-start | bytes 7077896 | tf_op jit(solution)/shard_map/ppermute | solution.py:583
  222.3 86.1 %collective-permute-start.14 = (bf16[256,4608]{1,0:T(8,128)(2,1)}, bf16[256,4608]{1,0:T(8,128)(2,1)}, u32[]{:S(2)}, u32[]{:S(2)}) collective-permute-start(bf16[256,4608]{1,0:T(8,128)(2,1)} %maximum_dynamic-update-slice_fusion.refs_1_), channel_id=1, source_target_pairs={{0,8},{8,16},{16,24},{1,9},{9,17},{17,25},{2,10},{10,18},{18,26},{... | collective-permute-start | bytes 7077896 | tf_op jit(solution)/shard_map/ppermute | solution.py:583
  308.4 60.6 %collective-permute-start.16 = (bf16[256,4608]{1,0:T(8,128)(2,1)}, bf16[256,4608]{1,0:T(8,128)(2,1)S(1)}, u32[]{:S(2)}, u32[]{:S(2)}) collective-permute-start(bf16[256,4608]{1,0:T(8,128)(2,1)} %collective-permute-done.14.refs_2_), channel_id=1, source_target_pairs={{8,16},{16,24},{9,17},{17,25},{10,18},{18,26},{11,19},{19,27},{12,... | collective-permute-start | bytes 7077896 | tf_op jit(solution)/shard_map/ppermute | solution.py:583
  309.2 63.8 %collective-permute-start.17 = (bf16[256,4608]{1,0:T(8,128)(2,1)}, bf16[256,4608]{1,0:T(8,128)(2,1)S(1)}, u32[]{:S(2)}, u32[]{:S(2)}) collective-permute-start(bf16[256,4608]{1,0:T(8,128)(2,1)} %collective-permute-done.15.refs_3_), channel_id=1, source_target_pairs={{16,8},{8,0},{17,9},{9,1},{18,10},{10,2},{19,11},{11,3},{20,12},{1... | collective-permute-start | bytes 7077896 | tf_op jit(solution)/shard_map/ppermute | solution.py:583
  314.0 55.0 %collective-permute-start.18 = (bf16[256,3840]{1,0:T(8,128)(2,1)S(1)}, bf16[256,3840]{1,0:T(8,128)(2,1)S(1)}, u32[]{:S(2)}, u32[]{:S(2)}) collective-permute-start(bf16[256,3840]{1,0:T(8,128)(2,1)S(1)} %get-tuple-element.179), channel_id=1, source_target_pairs={{0,8},{1,9},{2,10},{3,11},{4,12},{5,13},{6,14},{7,15}} | collective-permute-start | bytes 5898248 | tf_op jit(solution)/shard_map/ppermute | solution.py:603
  373.0 49.4 %collective-permute-start.20 = (bf16[256,4608]{1,0:T(8,128)(2,1)S(1)}, bf16[256,4608]{1,0:T(8,128)(2,1)S(1)}, u32[]{:S(2)}, u32[]{:S(2)}) collective-permute-start(bf16[256,4608]{1,0:T(8,128)(2,1)S(1)} %collective-permute-done.16.refs_4_), channel_id=1, source_target_pairs={{16,24},{17,25},{18,26},{19,27},{20,28},{21,29},{22,30},{23,31}} | collective-permute-start | bytes 7077896 | tf_op jit(solution)/shard_map/ppermute | solution.py:583
  373.8 53.2 %collective-permute-start.21 = (bf16[256,4608]{1,0:T(8,128)(2,1)S(1)}, bf16[256,4608]{1,0:T(8,128)(2,1)S(1)}, u32[]{:S(2)}, u32[]{:S(2)}) collective-permute-start(bf16[256,4608]{1,0:T(8,128)(2,1)S(1)} %collective-permute-done.17.refs_5_), channel_id=1, source_target_pairs={{8,0},{9,1},{10,2},{11,3},{12,4},{13,5},{14,6},{15,7}} | collective-permute-start | bytes 7077896 | tf_op jit(solution)/shard_map/ppermute | solution.py:583
  377.1 45.3 %collective-permute-start.22 = (bf16[256,3840]{1,0:T(8,128)(2,1)S(1)}, bf16[256,3840]{1,0:T(8,128)(2,1)S(1)}, u32[]{:S(2)}, u32[]{:S(2)}) collective-permute-start(bf16[256,3840]{1,0:T(8,128)(2,1)S(1)} %get-tuple-element.177), channel_id=1, source_target_pairs={{0,8},{8,16},{1,9},{9,17},{2,10},{10,18},{3,11},{11,19},{4,12},{12... | collective-permute-start | bytes 5898248 | tf_op jit(solution)/shard_map/ppermute | solution.py:603
  428.4 44.3 %collective-permute-start.24 = (bf16[256,3840]{1,0:T(8,128)(2,1)S(1)}, bf16[256,3840]{1,0:T(8,128)(2,1)}, u32[]{:S(2)}, u32[]{:S(2)}) collective-permute-start(bf16[256,3840]{1,0:T(8,128)(2,1)S(1)} %get-tuple-element.106), channel_id=1, source_target_pairs={{0,8},{8,16},{16,24},{1,9},{9,17},{17,25},{2,10},{10,18},{18,26},{... | collective-permute-start | bytes 5898248 | tf_op jit(solution)/shard_map/ppermute | solution.py:603
  431.1 43.8 %collective-permute-start.25 = (bf16[256,3840]{1,0:T(8,128)(2,1)S(1)}, bf16[256,3840]{1,0:T(8,128)(2,1)}, u32[]{:S(2)}, u32[]{:S(2)}) collective-permute-start(bf16[256,3840]{1,0:T(8,128)(2,1)S(1)} %get-tuple-element.107), channel_id=1, source_target_pairs={{24,16},{16,8},{8,0},{25,17},{17,9},{9,1},{26,18},{18,10},{10,2},{... | collective-permute-start | bytes 5898248 | tf_op jit(solution)/shard_map/ppermute | solution.py:603
  474.9 36.8 %all-to-all-start.2 = ((bf16[8,160,1024]{2,1,0:T(8,128)(2,1)}), bf16[8,160,1024]{2,1,0:T(8,128)(2,1)}, u32[]{:S(2)}, u32[]{:S(2)}) async-start(bf16[8,160,1024]{2,1,0:T(8,128)(2,1)} %bitcast.199), calls=%async_computation.2 | async-start | bytes 5242880 | tf_op jit(solution)/shard_map/all_to_all | solution.py:753
  479.4 254.1 %reduce-scatter.2.cloned.1.call-start = ((), (), s32[]{:S(2)}) async-start(), calls=%async_computation.6 | async-start | bytes 11796480 | tf_op jit(solution)/shard_map/reduce_scatter | solution.py:883
  519.9 68.9 %all-to-all-start.3 = ((bf16[8,160,1024]{2,1,0:T(8,128)(2,1)}), bf16[8,160,1024]{2,1,0:T(8,128)(2,1)}, u32[]{:S(2)}, u32[]{:S(2)}) async-start(bf16[8,160,1024]{2,1,0:T(8,128)(2,1)} %bitcast.48), calls=%async_computation.3 | async-start | bytes 5242880 | tf_op jit(solution)/shard_map/all_to_all | solution.py:753
  622.0 28.4 %collective-permute-start.29 = (bf16[2,2,144,1024]{3,2,0,1:T(8,128)(2,1)S(1)}, bf16[2,2,144,1024]{3,2,0,1:T(8,128)(2,1)S(1)}, u32[]{:S(2)}, u32[]{:S(2)}) collective-permute-start(bf16[2,2,144,1024]{3,2,0,1:T(8,128)(2,1)S(1)} %select_bitcast_fusion), channel_id=1, source_target_pairs={{0,4},{1,5},{2,6},{3,7},{4,0},{5,1},{6,2},{7,3},{8,12},{9,13},{10,... | collective-permute-start | bytes 3538952 | tf_op jit(solution)/shard_map/ppermute | solution.py:612
  624.3 28.6 %collective-permute-start.27 = (bf16[2,2,144,1024]{3,2,0,1:T(8,128)(2,1)S(1)}, bf16[2,2,144,1024]{3,2,0,1:T(8,128)(2,1)S(1)}, u32[]{:S(2)}, u32[]{:S(2)}) collective-permute-start(bf16[2,2,144,1024]{3,2,0,1:T(8,128)(2,1)S(1)} %select_bitcast_fusion.1), channel_id=1, source_target_pairs={{0,2},{1,3},{2,0},{3,1},{4,6},{5,7},{6,4},{7,5},{8,10},{9,11},{10,... | collective-permute-start | bytes 3538952 | tf_op jit(solution)/shard_map/ppermute | solution.py:612
  626.0 59.1 %collective-permute-start.31 = (bf16[512,1024]{1,0:T(8,128)(2,1)S(1)}, bf16[512,1024]{1,0:T(8,128)(2,1)S(1)}, u32[]{:S(2)}, u32[]{:S(2)}) collective-permute-start(bf16[512,1024]{1,0:T(8,128)(2,1)S(1)} %slice.547), channel_id=1, source_target_pairs={{8,0},{16,8},{24,16},{9,1},{17,9},{25,17},{10,2},{18,10},{26,18},{... | collective-permute-start | bytes 3145736 | tf_op jit(solution)/shard_map/ppermute | solution.py:30
  (91 other events, 819.7 us)
Sparse Core Ops, SparseCore 0:
  19.0 60.9 all-gather.5
Sparse Core Ops, SparseCore 1:
  105.3 150.1 all-gather.3
  504.2 182.1 reduce-scatter.1

commit v4 on v3

--- a/solution.py
+++ b/solution.py
@@ -17,7 +17,7 @@
 NEGATIVE = -1e30
 LANES = 128
 CHUNK = 256
-FF_TILE = 256
+FF_TILE = 512
 ROW_TILE = 256
 VMEM_LIMIT = 58 * 2**20
 BF16 = jnp.bfloat16
@@ -84,41 +84,26 @@
     )(padded)
 
 
-def unband_kernel(band_ref, dist_ref):
+def sum_band(band_ref):
     blocks = WINDOW // LANES
     size = (blocks + 2) * LANES
     row = lax.broadcasted_iota(jnp.int32, (8, 1), 0)
     edge = jnp.zeros((8, LANES), F32)
-    for head in range(band_ref.shape[0]):
-        total = None
-        for group in range(LANES // 8):
-            pieces = [edge]
-            for a in range(blocks, -1, -1):
-                first = a * LANES + group * 8
-                pieces.append(band_ref[head, first : first + 8, :])
-            wide = jnp.concatenate(pieces, axis=1)
-            if group:
-                wide = pltpu.roll(wide, size - 8 * group, 1)
-            total = wide if total is None else total + wide
-        dist = jnp.zeros_like(total)
-        for r in range(8):
-            turned = pltpu.roll(total, size - r, 1) if r else total
-            dist = dist + jnp.where(row == r, turned, 0.0)
-        dist_ref[head : head + 1, :] = jnp.sum(dist, axis=0, keepdims=True)[:, LANES : LANES + WINDOW]
-
-
-def sum_band(band_grad):
-    group = 8
-    return pl.pallas_call(
-        unband_kernel,
-        grid=(HEADS // group,),
-        in_specs=[pl.BlockSpec((group, WINDOW + LANES, LANES), lambda h: (h, 0, 0))],
-        out_specs=pl.BlockSpec((group, WINDOW), lambda h: (h, 0)),
-        out_shape=jax.ShapeDtypeStruct((HEADS, WINDOW), F32),
-        compiler_params=params(),
-        cost_estimate=brief(),
-        name="bias_band_sums",
-    )(band_grad)
+    total = None
+    for group in range(LANES // 8):
+        pieces = [edge]
+        for a in range(blocks, -1, -1):
+            first = a * LANES + group * 8
+            pieces.append(band_ref[first : first + 8, :])
+        wide = jnp.concatenate(pieces, axis=1)
+        if group:
+            wide = pltpu.roll(wide, size - 8 * group, 1)
+        total = wide if total is None else total + wide
+    dist = jnp.zeros_like(total)
+    for r in range(8):
+        turned = pltpu.roll(total, size - r, 1) if r else total
+        dist = dist + jnp.where(row == r, turned, 0.0)
+    return jnp.sum(dist, axis=0, keepdims=True)[:, LANES : LANES + WINDOW]
 
 
 def head_lanes(head):
@@ -206,14 +191,53 @@
     )(queries, keys, values, query_doc, key_doc, band)
 
 
+def probs_kernel(q_ref, k_ref, qdoc_ref, kdoc_ref, band_ref, lse_ref, probs_ref):
+    for chunk in range(q_ref.shape[0] // CHUNK):
+        start = chunk * CHUNK
+        for head in range(2):
+            scores = masked_scores(head, start, q_ref, k_ref, qdoc_ref, kdoc_ref)
+            band = band_ref[head]
+            lse = lse_ref[0, head : head + 1, pl.ds(start, CHUNK)]
+            parts = []
+            for s, (first, rows) in enumerate(sub_blocks()):
+                lanes = slice(s * LANES, (s + 1) * LANES)
+                parts.append(jnp.exp(scores[first : first + rows, lanes] + band - lse[:, lanes]).astype(BF16))
+            probs_ref[head, chunk] = spread(parts)
+
+
+def make_probs(queries, keys, query_doc, key_doc, band, lse):
+    rows, width = queries.shape
+    keys_rows = keys.shape[0]
+    pairs = HEADS // 2
+    wide = 2 * HEAD_DIM
+    span, chunks = WINDOW + CHUNK, rows // CHUNK
+    return pl.pallas_call(
+        probs_kernel,
+        grid=(pairs,),
+        in_specs=[
+            pl.BlockSpec((rows, wide), lambda p: (0, p)),
+            pl.BlockSpec((keys_rows, wide), lambda p: (0, p)),
+            pl.BlockSpec((rows, wide), lambda p: (0, 0)),
+            pl.BlockSpec((keys_rows, wide), lambda p: (0, 0)),
+            pl.BlockSpec((2, WINDOW + LANES, LANES), lambda p: (p, 0, 0)),
+            pl.BlockSpec((1, 2, rows), lambda p: (p, 0, 0)),
+        ],
+        out_specs=pl.BlockSpec((2, chunks, span, CHUNK), lambda p: (p, 0, 0, 0)),
+        out_shape=jax.ShapeDtypeStruct((HEADS, chunks, span, CHUNK), BF16),
+        compiler_params=params(),
+        cost_estimate=brief(),
+        name="probs",
+    )(queries, keys, query_doc, key_doc, band, lse)
+
+
 def attend_back_kernel(
-    q_ref, k_ref, v_ref, g_ref, o_ref, lse_ref, qdoc_ref, kdoc_ref, band_ref,
-    dq_ref, dk_ref, dv_ref, dband_ref, dk_sum, dv_sum,
+    q_ref, k_ref, v_ref, g_ref, o_ref, probs_ref, dq_ref, dk_ref, dv_ref, dist_ref, dk_sum, dv_sum, dband
 ):
     span = WINDOW + CHUNK
     dk_sum[...] = jnp.zeros_like(dk_sum)
     dv_sum[...] = jnp.zeros_like(dv_sum)
-    for start in range(0, q_ref.shape[0], CHUNK):
+    for chunk in range(q_ref.shape[0] // CHUNK):
+        start = chunk * CHUNK
         q_rows, k_rows = pl.ds(start, CHUNK), pl.ds(start, span)
         k_turned = k_ref[k_rows, :].T
         product = (g_ref[q_rows, :].astype(F32) * o_ref[q_rows, :].astype(F32)).T
@@ -221,43 +245,40 @@
         for head in range(2):
             mine = head_lanes(head)
             zero = jnp.zeros((), BF16)
-            scores = masked_scores(head, start, q_ref, k_ref, qdoc_ref, kdoc_ref)
             g_part = jnp.where(mine, g_ref[q_rows, :], zero)
             q_part = jnp.where(mine, q_ref[q_rows, :], zero)
             prob_grad = dot_last(v_ref[k_rows, :], g_part)
             delta = jnp.sum(product[head * HEAD_DIM : (head + 1) * HEAD_DIM], axis=0, keepdims=True)
-            lse = lse_ref[0, head : head + 1, q_rows]
-            band = band_ref[head]
-            prob_low, grad_low, grad_sum = [], [], None
+            grad_low, grad_sum = [], None
             for s, (first, rows) in enumerate(sub_blocks()):
                 lanes = slice(s * LANES, (s + 1) * LANES)
-                probs = jnp.exp(scores[first : first + rows, lanes] + band - lse[:, lanes])
+                probs = probs_ref[head, chunk, first : first + rows, lanes].astype(F32)
                 grad = probs * (prob_grad[first : first + rows, lanes] - delta[:, lanes])
-                prob_low.append(probs.astype(BF16))
                 grad_low.append(grad.astype(BF16))
                 grad_sum = grad if grad_sum is None else grad_sum + grad
-            if start == 0:
-                dband_ref[head] = grad_sum
+            if chunk == 0:
+                dband[head] = grad_sum
             else:
-                dband_ref[head] = dband_ref[head] + grad_sum
+                dband[head] = dband[head] + grad_sum
             grads = spread(grad_low)
             dk_sum[k_rows, :] += dot(grads, q_part)
-            dv_sum[k_rows, :] += dot(spread(prob_low), g_part)
+            dv_sum[k_rows, :] += dot(probs_ref[head, chunk], g_part)
             dq_parts.append(dot(k_turned[head * HEAD_DIM : (head + 1) * HEAD_DIM], grads))
         turned = jnp.concatenate(dq_parts, axis=0).T
         dq_ref[q_rows, :] = (turned * HEAD_DIM ** (-0.5)).astype(BF16)
     dk_ref[...] = dk_sum[...].astype(BF16)
     dv_ref[...] = dv_sum[...].astype(BF16)
-
-
-def attend_back(queries, keys, values, grad, out, lse, query_doc, key_doc, band):
+    for head in range(2):
+        dist_ref[0, head : head + 1, :] = sum_band(dband.at[head])
+
+
+def attend_back(queries, keys, values, grad, out, probs):
     rows, width = queries.shape
     keys_rows = keys.shape[0]
     pairs = HEADS // 2
     wide = 2 * HEAD_DIM
     q_spec = pl.BlockSpec((rows, wide), lambda p: (0, p))
     k_spec = pl.BlockSpec((keys_rows, wide), lambda p: (0, p))
-    band_spec = pl.BlockSpec((2, WINDOW + LANES, LANES), lambda p: (p, 0, 0))
     return pl.pallas_call(
         attend_back_kernel,
         grid=(pairs,),
@@ -267,23 +288,26 @@
             k_spec,
             q_spec,
             q_spec,
-            pl.BlockSpec((1, 2, rows), lambda p: (p, 0, 0)),
-            pl.BlockSpec((rows, wide), lambda p: (0, 0)),
-            pl.BlockSpec((keys_rows, wide), lambda p: (0, 0)),
-            band_spec,
-        ],
-        out_specs=[q_spec, k_spec, k_spec, band_spec],
+            pl.BlockSpec((2,) + probs.shape[1:], lambda p: (p, 0, 0, 0)),
+        ],
+        out_specs=[q_spec, k_spec, k_spec, pl.BlockSpec((1, 2, WINDOW), lambda p: (p, 0, 0))],
         out_shape=[
             jax.ShapeDtypeStruct((rows, width), BF16),
             jax.ShapeDtypeStruct((keys_rows, width), BF16),
             jax.ShapeDtypeStruct((keys_rows, width), BF16),
-            jax.ShapeDtypeStruct((HEADS, WINDOW + LANES, LANES), F32),
-        ],
-        scratch_shapes=[pltpu.VMEM((keys_rows, wide), F32), pltpu.VMEM((keys_rows, wide), F32)],
+            jax.ShapeDtypeStruct((pairs, 2, WINDOW), F32),
+        ],
+        scratch_shapes=[
+            pltpu.VMEM((keys_rows, wide), F32),
+            pltpu.VMEM((keys_rows, wide), F32),
+            pltpu.VMEM((2, WINDOW + LANES, LANES), F32),
+        ],
         compiler_params=params(),
-        cost_estimate=pl.CostEstimate(flops=20 * rows * WINDOW * width * 2, bytes_accessed=2**20, transcendentals=0),
+        cost_estimate=pl.CostEstimate(
+            flops=20 * rows * WINDOW * width * 2, bytes_accessed=2**20, transcendentals=0
+        ),
         name="attend_back",
-    )(queries, keys, values, grad, out, lse, query_doc, key_doc, band)
+    )(queries, keys, values, grad, out, probs)
 
 
 def down_blocks(units, width, count):
@@ -376,9 +400,9 @@
             from_columns = slice(2 * units + column, 2 * units + column + wide)
             down_s[to_row : to_row + high, to_column : to_column + wide] = chunk_ref[row : row + high, from_columns]
 
-    for t in range(units // FF_TILE):
-        at = slice(t * FF_TILE, (t + 1) * FF_TILE)
-        up_at = slice(units + t * FF_TILE, units + (t + 1) * FF_TILE)
+    for start in range(0, units, FF_TILE):
+        stop = min(start + FF_TILE, units)
+        at, up_at = slice(start, stop), slice(units + start, units + stop)
         gate_pre = dot(x, chunk_ref[:, at])
         up_pre = dot(x, chunk_ref[:, up_at])
         hidden_grad = dot_last(low_ref[...], down_s[at, :])
@@ -511,11 +535,14 @@
             total = dot(hidden_turned[...], low_ref[...]).astype(BF16)
             first = place * tile
             for (row, column), (from_row, from_column), (high, wide) in down_blocks(units, width, count):
-                part = total[from_row : from_row + high]
                 if column == 0:
-                    grad_ref[row : row + high, :] = part
-                elif from_column <= first < from_column + wide:
-                    rest[row : row + high, first - from_column : first - from_column + tile] = part
+                    grad_ref[row : row + high, :] = total[from_row : from_row + high]
+                    continue
+                low, top = max(first, from_column), min(first + tile, from_column + wide)
+                if low < top:
+                    rest[row : row + high, low - from_column : top - from_column] = total[
+                        from_row : from_row + high, low - first : top - first
+                    ]
 
     for place in range(rest.shape[1] // tile):
 
@@ -526,13 +553,14 @@
 
 def expert_weights(units, count, x, low, dboth, hidden, long=False):
     rows, width = x.shape
-    tile = 256
-    extra = units - width
+    tile = 512
+    extra_steps = -(-(units - width) // tile)
     both_steps, down_steps = 2 * units // tile, width // tile
     whole = lambda i: (0, 0)
+    work = pl.CostEstimate(flops=6 * rows * width * units, bytes_accessed=2**20, transcendentals=0)
     return pl.pallas_call(
         functools.partial(expert_weights_kernel, units, count),
-        grid=(both_steps + down_steps + extra // tile,),
+        grid=(both_steps + down_steps + extra_steps,),
         in_specs=[
             pl.BlockSpec((rows, width), whole),
             pl.BlockSpec((rows, tile), lambda i: (0, jnp.clip(i - both_steps, 0, down_steps - 1))),
@@ -544,12 +572,59 @@
         scratch_shapes=[
             pltpu.VMEM((width, rows), BF16),
             pltpu.VMEM((units, rows), BF16),
-            pltpu.VMEM((width, extra), BF16),
+            pltpu.VMEM((width, extra_steps * tile), BF16),
         ],
         compiler_params=params(),
-        cost_estimate=pl.CostEstimate(flops=(6 * rows * width * units) if long else 2**20, bytes_accessed=2**20, transcendentals=0),
+        cost_estimate=work if long else brief(),
         name="expert_weights",
     )(x, low, dboth, hidden)
+
+
+def expert_sums_kernel(sizes, count, own_ref, up_ref, down_ref, last_ref, gate_out, up_out, down_out):
+    held, width = own_ref.shape[0], down_out.shape[1]
+    extras = [size - held for size in sizes]
+    tile = min(extras)
+    for first in range(0, held, tile):
+        rows = slice(first, first + tile)
+        totals = (
+            own_ref[rows, :].astype(F32) + up_ref[rows, :].astype(F32) + down_ref[rows, :].astype(F32),
+            last_ref[rows, :].astype(F32),
+        )
+        for out, part in ((gate_out, 0), (up_out, 1)):
+            pieces = []
+            for z in range(count):
+                for size, total in zip(sizes, totals):
+                    at = part * size * count + z * size
+                    pieces.append(total[:, at : at + size])
+            out[rows, :] = jnp.concatenate(pieces, axis=1)
+        start = 0
+        for size, extra, total in zip(sizes, extras, totals):
+            wide = width * extra // held
+            at = 2 * size * count
+            down_out[start + first : start + first + tile, :] = total[:, at : at + width]
+            to, columns = start + held + first % extra, first // extra * wide
+            down_out[to : to + tile, columns : columns + wide] = total[:, at + width :]
+            start += size
+
+
+def expert_sums(sizes, count, own, up, down, last):
+    held = own.shape[0]
+    units = sum(sizes)
+    struct = jax.ShapeDtypeStruct
+    width = held * count
+    return pl.pallas_call(
+        functools.partial(expert_sums_kernel, sizes, count),
+        in_specs=[pl.BlockSpec(memory_space=pltpu.VMEM)] * 4,
+        out_specs=[pl.BlockSpec(memory_space=pltpu.VMEM)] * 3,
+        out_shape=[
+            struct((held, units * count), F32),
+            struct((held, units * count), F32),
+            struct((units, width), F32),
+        ],
+        compiler_params=params(),
+        cost_estimate=brief(),
+        name="expert_sums",
+    )(own, up, down, last)
 
 
 def ctx_moves(distance):
@@ -628,15 +703,17 @@
     return bits[1:], bits[:0:-1]
 
 
-def spread_exp(column):
+def spread_exp(column, then):
     count = column.shape[0]
-    halves = []
-    for half, order in zip((column[: count // 2], column[count // 2 :]), routes_exp()):
-        half = half[None]
-        for bit in order:
-            other = swap_exp(half, bit)
-            half = jnp.where(bit_set(bit), jnp.concatenate([other, half]), jnp.concatenate([half, other]))
-        halves.append(half)
+    halves = [column[None, : count // 2], column[None, count // 2 :]]
+    for step, bits in enumerate(zip(*routes_exp())):
+        others = [swap_exp(half, bit) for half, bit in zip(halves, bits)]
+        if step == 0:
+            others = then(others)
+        for place, (half, other, bit) in enumerate(zip(halves, others, bits)):
+            halves[place] = jnp.where(
+                bit_set(bit), jnp.concatenate([other, half]), jnp.concatenate([half, other])
+            )
     return halves
 
 
@@ -660,9 +737,9 @@
     return jnp.concatenate([half[:, :, first : first + rows].reshape(-1, width) for half in done])
 
 
-def scatter_exp(keep, send):
+def scatter_exp(keep, other):
     count, bits = lax.axis_size("ctx"), exp_bits()
-    chip = (keep.astype(F32) + swap_exp(send, 1).astype(F32)).astype(BF16)
+    chip = (keep.astype(F32) + other.astype(F32)).astype(BF16)
     chip = chip.reshape((count, -1) + chip.shape[1:])
     sums = []
     for half, order in zip((chip[: count // 2], chip[count // 2 :]), routes_exp()):
@@ -680,11 +757,71 @@
     return jnp.concatenate(sums)
 
 
-def scatter_ctx(parts):
-    sent = (None, None)
-    for hop in range(1, lax.axis_size("ctx")):
-        sent = scatter_hop(*scatter_add(parts, hop, *sent), hop)
-    return scatter_end(parts, *sent)
+def normed_grad_kernel(
+    halo_steps, x_ref, q_ref, k_ref, v_ref, wq_ref, wk_ref, wv_ref, halo_ref, own_ref, gain_ref, total
+):
+    step = pl.program_id(0)
+    total[...] = dot_last(k_ref[...], wk_ref[...]) + dot_last(v_ref[...], wv_ref[...])
+
+    @pl.when(step >= halo_steps)
+    def _():
+        total[...] += dot_last(q_ref[...], wq_ref[...])
+        own_ref[...] = total[...]
+
+    @pl.when(step < halo_steps)
+    def _():
+        halo_ref[...] = total[...].astype(BF16)
+
+    x = x_ref[...].astype(F32)
+    unit = x * lax.rsqrt(jnp.mean(x * x, axis=1, keepdims=True) + EPSILON)
+    update = jnp.sum((total[...] * unit).reshape(-1, 8, x.shape[1]), axis=0)
+
+    @pl.when(step == 0)
+    def _():
+        gain_ref[...] = update
+
+    @pl.when(step > 0)
+    def _():
+        gain_ref[...] += update
+
+
+def normed_grad_of(inputs_all, query_grad, key_grad, value_grad, full_query, full_key, full_value):
+    all_rows, width = key_grad.shape
+    own = query_grad.shape[0]
+    tile = 256
+    halo_steps = (all_rows - own) // tile
+    row = lambda i: (i, 0)
+    late = lambda i: (jnp.maximum(i - halo_steps, 0), 0)
+    whole = lambda i: (0, 0)
+    block = (tile, width)
+    weight = pl.BlockSpec((width, width), whole, pipeline_mode=pl.Buffered(1))
+    return pl.pallas_call(
+        functools.partial(normed_grad_kernel, halo_steps),
+        grid=(all_rows // tile,),
+        in_specs=[
+            pl.BlockSpec(block, row),
+            pl.BlockSpec(block, late),
+            pl.BlockSpec(block, row),
+            pl.BlockSpec(block, row),
+            weight,
+            weight,
+            weight,
+        ],
+        out_specs=[
+            pl.BlockSpec(block, lambda i: (jnp.minimum(i, halo_steps - 1), 0)),
+            pl.BlockSpec(block, late),
+            pl.BlockSpec((8, width), whole),
+        ],
+        out_shape=[
+            jax.ShapeDtypeStruct((all_rows - own, width), BF16),
+            jax.ShapeDtypeStruct((own, width), F32),
+            jax.ShapeDtypeStruct((8, width), F32),
+        ],
+        scratch_shapes=[pltpu.VMEM(block, F32)],
+        compiler_params=params(),
+        cost_estimate=brief(),
+        name="normed_grad",
+    )(inputs_all, query_grad, key_grad, value_grad, full_query, full_key, full_value)
 
 
 def slab_kernel(part, x_ref, q_ref, k_ref, v_ref, o_ref, g_ref, tail_ref, keep_ref, send_ref, x_turned, o_turned, total):
@@ -820,14 +957,19 @@
     column, halo[0], early, packed[0] = together(column, halo[0], early, packed[0])
     for _ in range(1, reach):
         halo.insert(0, shift_ctx(halo[0], 1))
-    packed[0], halo[0] = together(packed[0], halo[0])
-    chunk0 = lax.all_gather(packed[0], "ctx", axis=0, tiled=True)
     onehot_bucket = (bucket_of[None, :] == jnp.arange(BUCKETS, dtype=jnp.int32)[:, None]).astype(BF16)
     band = make_band(dot(table, onehot_bucket))
-    *halves, band = together(*spread_exp(column), band)
+
+    def then(others):
+        *others, halo[0], packed[0] = together(*others, halo[0], packed[0])
+        return others
+
+    *halves, band = together(*spread_exp(column, then), band)
+    chunk0 = lax.all_gather(packed[0], "ctx", axis=0, tiled=True)
     dense = spread_core(halves)
     full_query, full_key, full_value, full_out = (join_weights(dense, i * part, part) for i in range(4))
-    inputs_all = jnp.concatenate(halo, axis=0).astype(F32)
+    tokens_all = jnp.concatenate(halo, axis=0)
+    inputs_all = tokens_all.astype(F32)
     inputs = own_tokens.astype(F32)
 
     ends = jnp.cumsum(doc_lengths[0])
@@ -857,20 +999,20 @@
     router_turned = jnp.pad(full_router.T, ((0, LANES - experts), (0, 0)))
     extras = (early, router_turned)
     units0, units1 = (size * ctx_count for size in sizes)
-    arrived, packed[1] = together(arrived, packed[1])
-    up = down = packed[1]
-    pieces = [up]
+    arrived, packed[1], chunk0 = together(arrived, packed[1], chunk0)
+    up, down = gather_hop(packed[1], packed[1], 1)
     hidden, dboth, carried, _ = run_expert(True, False, units0, ctx_count, arrived, [chunk0], extras, None)
     grad0 = expert_weights(units0, ctx_count, arrived, carried[0], dboth, hidden)
-    sent = (None, None)
+    pieces, sent = [packed[1]], (None, None)
+    probs = make_probs(queries, keys, query_doc, key_doc, band, lse)
     for hop in range(1, ctx_count):
-        up, down = gather_hop(up, down, hop)
         if hop == 1:
             up, down, grad0 = together(up, down, grad0)
             parts0 = grad0.reshape(ctx_count, held, -1)
         else:
+            up, down = gather_hop(up, down, hop)
             sent = scatter_hop(*scatter_add(parts0, hop - 1, *sent), hop - 1)
-            up, down, *sent = together(up, down, *sent)
+            up, down, probs, *sent = together(up, down, probs, *sent)
         pieces += [up, down]
     arrived, *sent = together(arrived, *scatter_add(parts0, ctx_count - 1, *sent))
     sent = scatter_hop(*sent, ctx_count - 1)
@@ -892,18 +1034,18 @@
     attended_grad = dot_last(branch_grad, full_out).astype(BF16)
     made, attended_grad = together(made, attended_grad)
     made = exchange(made.reshape(experts, capacity, width)).reshape(-1, width)
-    query_grad, key_grad, value_grad, band_grad = attend_back(
-        queries, keys, values, attended_grad, attended, lse, query_doc, key_doc, band
+    query_grad, key_grad, value_grad, dist_grad = attend_back(
+        queries, keys, values, attended_grad, attended, probs
     )
     bias_grad = jnp.dot(
-        sum_band(band_grad), onehot_bucket.T.astype(F32), precision=lax.Precision.HIGHEST
+        dist_grad.reshape(HEADS, WINDOW), onehot_bucket.T.astype(F32), precision=lax.Precision.HIGHEST
     )
 
-    normed_grad_all = dot_last(key_grad, full_key) + dot_last(value_grad, full_value)
-    own_grad = normed_grad_all[reach * rows :] + dot_last(query_grad, full_query)
-    halo_grad = normed_grad_all[: reach * rows]
-    _, first_pull = jax.vjp(norm_rows, inputs_all, full_gain_attn)
-    gain_attn_grad = first_pull(jnp.concatenate([halo_grad, own_grad], axis=0))[1]
+    halo_grad, own_grad, gain_attn_grad = normed_grad_of(
+        tokens_all, query_grad, key_grad, value_grad, full_query, full_key, full_value
+    )
+    gain_attn_grad = jnp.sum(gain_attn_grad, axis=0)
+
     tail = jnp.concatenate(
         [
             router_grad[:, :experts].reshape(devices, -1),
@@ -917,36 +1059,24 @@
     query_grad, made = together(query_grad, made)
     output = (middle + dot_rows(routes, made)).astype(BF16)
     keep, send = make_slabs(normed_all, query_grad, key_grad, value_grad, attended, branch_grad, tail)
-    parts = scatter_exp(keep, send)
-
-    returning = None
-    for stride in range(reach, 0, -1):
-        piece = halo_grad[(reach - stride) * rows : (reach - stride + 1) * rows]
-        if returning is not None:
-            parts, returning, *sent = together(parts, returning, *sent)
-            piece = piece + returning.astype(F32)
-        returning = shift_ctx(piece.astype(BF16), -1)
-    sums = scatter_ctx(parts)
+    other = swap_exp(send, 1)
+    parts = scatter_exp(keep, other)
+    pieces = [halo_grad[place * rows : (place + 1) * rows] for place in range(reach)]
+    returning = shift_ctx(pieces[0], -1)
+    for piece in pieces[1:]:
+        parts, returning = together(parts, returning)
+        returning = shift_ctx((piece.astype(F32) + returning.astype(F32)).astype(BF16), -1)
+    own0 = lax.dynamic_index_in_dim(parts0, ctx_index, 0, keepdims=False)
+    expert_grads = expert_sums(sizes, ctx_count, own0, *sent, total1)
+    sent = (None, None)
+    for hop in range(1, ctx_count):
+        sent = scatter_add(parts, hop, *sent)
+        sent = scatter_hop(*sent, hop)
+        if hop == 1:
+            *sent, grad_gate, grad_up, grad_down = together(*sent, *expert_grads)
+    sums = scatter_end(parts, *sent)
     _, own_pull = jax.vjp(norm_rows, inputs, full_gain_attn)
     input_grad = middle_grad + own_pull(own_grad + returning.astype(F32))[0]
-    scattered = [scatter_end(parts0, *sent), total1.astype(F32)]
-    gate_parts, up_parts, down_parts = [], [], []
-    for size, total in zip(sizes, scattered):
-        units = size * ctx_count
-        gate_parts.append(total[:, :units])
-        up_parts.append(total[:, units : 2 * units])
-        down_parts.append(unpack_down(total[:, 2 * units :], size, width))
-
-    def in_order(parts):
-        shares = [part[:, z * (part.shape[1] // ctx_count) : (z + 1) * (part.shape[1] // ctx_count)]
-                  for z in range(ctx_count) for part in parts]
-        return jnp.concatenate(shares, axis=1)[None]
-
-    expert_grads = (
-        in_order(gate_parts),
-        in_order(up_parts),
-        jnp.concatenate(down_parts, axis=0)[None],
-    )
     tail = sums[4 * part]
     at = part * experts
     return (
@@ -960,9 +1090,9 @@
         tail[at : at + part],
         tail[at + part : at + 2 * part],
         tail[at + 2 * part : at + 2 * part + bias_part],
-        expert_grads[0],
-        expert_grads[1],
-        expert_grads[2],
+        grad_gate[None],
+        grad_up[None],
+        grad_down[None],
     )
 
 

time: 767 us -> 728 us (0.949)
  waiting for transfers between devices: 248 us -> 223 us
  Pallas kernels: 211 us -> 232 us
  matrix products: 51 us -> 35.2 us
  local copies, waits for them, and re-layouts: 64.1 us -> 48.5 us
    pallas_call x1 -> x3, Pallas kernels: 7.85 us -> 40.3 us  [the longest x1 16.9 us: make_probs(): pl.pallas_call(probs_kernel, grid=(pairs,), in_specs=[pl.BlockSpec((rows,...]
    ppermute x12, waiting for transfers between devices: 99.5 us -> 72 us  [scatter_hop(): return (lax.ppermute(up, 'ctx', route), lax.ppermute(down, 'ctx', back))]
    all_to_all x4, waiting for transfers between devices: 27.3 us -> 45.1 us  [exchange(): lax.all_to_all(blocks, 'exp', split_axis=0, concat_axis=0, tiled=True)]
    dot_general x4 -> x1, matrix products: 19.6 us -> 2.31 us  [dot_last(): lax.dot_general(left, right, (((1,), (1,)), ((), ())), preferred_element_...]
    all_gather x1, waiting for transfers between devices: 26 us -> 10.3 us  [body(): chunk0 = lax.all_gather(packed[0], 'ctx', axis=0, tiled=True)]
    concatenate x2 -> x0, local copies, waits for them, and re-layouts: 8.07 us -> none  [in_order(): return jnp.concatenate(shares, axis=1)[None]]
    ppermute x6, waiting for transfers between devices: 8.58 us -> 0.82 us  [gather_hop(): return (lax.ppermute(up, 'ctx', route), lax.ppermute(down, 'ctx', back))]
    unnamed x148 -> x118, local copies, waits for them, and re-layouts: 22.6 us -> 19 us
  transfers between devices with their start and end apart: 46 -> 46, of which waited for: 24 -> 25; matrix products, arithmetic and copies ran while one was open for 19% -> 19% of each run, Pallas kernels for 28% -> 30%
where the time goes in v4:
time: 728 us; the launch traced here: 719 us
  Pallas kernels  232 us (32%)
  waiting for transfers between devices  223 us (31%)
  starting transfers between devices  103 us (14%)
  other arithmetic  62 us (9%)
  local copies, waits for them, and re-layouts  48.5 us (7%)
  matrix products  35.2 us (5%)
  between operations  15.2 us (2%)
    pallas_call x2, Pallas kernels, run_expert(): pl.pallas_call(functools.partial(expert_kernel, first, last, units, count...  73.7 us
    ppermute x12, waiting for transfers between devices, scatter_hop(): return (lax.ppermute(up, 'ctx', route), lax.ppermute(down, 'ctx', back))  72 us
    ppermute x11, waiting for transfers between devices, swap_exp(): lax.ppermute(block, 'exp', [(i, i ^ bit) for i in range(lax.axis_size('ex...  61.8 us
    all_to_all x4, waiting for transfers between devices, exchange(): lax.all_to_all(blocks, 'exp', split_axis=0, concat_axis=0, tiled=True)  45.1 us
    pallas_call x2, Pallas kernels, expert_weights(): pl.pallas_call(functools.partial(expert_weights_kernel, units, count), gr...  37.4 us
    ppermute x12, starting transfers between devices, scatter_hop(): return (lax.ppermute(up, 'ctx', route), lax.ppermute(down, 'ctx', back))  33.7 us
    ppermute x10, waiting for transfers between devices, shift_ctx(): return lax.ppermute(block, 'ctx', route)  32.6 us
    pallas_call x1, Pallas kernels, attend(): pl.pallas_call(attend_kernel, grid=(pairs,), in_specs=[pl.BlockSpec((rows...  28.9 us
  transfers between devices with their start and end apart: 46, of which 25 were waited for; matrix products, arithmetic and copies ran while one was open for 19% of the time, Pallas kernels for 30%

profile of v4, /device:TPU:0, one launch (start us, length us, event | category | flops | bytes accessed | tf_op | source)
XLA Modules:
  0.0 719.4 jit_solution(11273325327977100104)
XLA Ops:
  80.4 8.3 %collective-permute-done.8 = bf16[1,2,128,1024]{3,2,1,0:T(8,128)(2,1)S(1)} collective-permute-done((bf16[1,2,128,1024]{3,2,1,0:T(8,128)(2,1)S(1)}, bf16[1,2,128,1024]{3,2,1,0:T(8,128)(2,1)S(1)}, u32[]{:S(2)}, u32[]{:S(2)}) %collective-permute-start.8) | collective-permute-done | bytes 524320 | tf_op jit(solution)/shard_map/ppermute | solution.py:687
  106.7 7.3 %bias_band.1.band_ref = f32[16,1152,128]{2,1,0:T(8,128)} custom-call(f32[16,1280]{1,0:T(8,128)} %pad_maximum_fusion.9.bias_ref), custom_call_target="tpu_custom_call" | custom-call | flops 1048576 | bytes 1048576 | tf_op jit(solution)/shard_map/bias_band/pallas_call | solution.py:75
  114.0 8.6 %collective-permute-done.11 = bf16[2,2,128,1024]{3,2,1,0:T(8,128)(2,1)S(1)} collective-permute-done((bf16[2,2,128,1024]{3,2,1,0:T(8,128)(2,1)}, bf16[2,2,128,1024]{3,2,1,0:T(8,128)(2,1)S(1)}, u32[]{:S(2)}, u32[]{:S(2)}) %collective-permute-start.11) | collective-permute-done | bytes 1048608 | tf_op jit(solution)/shard_map/ppermute | solution.py:687
  157.1 28.9 %attend.1 = (bf16[512,1024]{1,0:T(8,128)(2,1)}, f32[8,2,512]{2,1,0:T(2,128)}) custom-call(bf16[512,1024]{1,0:T(8,128)(2,1)} %fusion.21.q_ref, bf16[1536,1024]{1,0:T(8,128)(2,1)} %convolution_convert_fusion.3.k_ref, bf16[1536,1024]{1,0:T(8,128)(2,1)} %convolution_convert_fusion.2.v_ref, bf16[512,128]{1,0:T(8,128)(2,1)} %compare_convert_fusion.qdoc_ref, ...), custom_call_target="tpu_custom_call" | custom-call | flops 1048576 | bytes 1048576 | tf_op jit(solution)/shard_map/attend/pallas_call | solution.py:169
  209.3 18.3 %all-to-all-done.1 = bf16[8,160,1024]{2,1,0:T(8,128)(2,1)S(1)} async-done(((bf16[8,160,1024]{2,1,0:T(8,128)(2,1)}), bf16[8,160,1024]{2,1,0:T(8,128)(2,1)S(1)}, u32[]{:S(2)}, u32[]{:S(2)}) %all-to-all-start.1) | async-done | bytes 2621472 | tf_op jit(solution)/shard_map/all_to_all | solution.py:890
  227.6 10.3 %all-gather.4.cloned.1.call-done.refs_1_ = bf16[1024,3840]{1,0:T(8,128)(2,1)} async-done(((bf16[256,3840]{1,0:T(8,128)(2,1)}), bf16[1024,3840]{1,0:T(8,128)(2,1)}) %all-gather.4.cloned.1.call-update) | async-done | bytes 7864336 | tf_op jit(solution)/shard_map/all_gather | solution.py:968
  239.3 6.0 collective-permute-start.14
  246.4 32.7 %expert.2 = (bf16[1280,1280]{1,0:T(8,128)(2,1)}, bf16[1280,2560]{1,0:T(8,128)(2,1)}, bf16[1280,1024]{1,0:T(8,128)(2,1)}, f32[1280,128]{1,0:T(8,128)}, f32[1280,1024]{1,0:T(8,128)}, /*index=5*/f32[1280,1024]{1,0:T(8,128)}) custom-call(bf16[1280,1024]{1,0:T(8,128)(2,1)} %bitcast.171, bf16[1024,3840]{1,0:T(8,128)(2,1)} %all-gather.4.cloned.1.call-done.refs_1_, ...), custom_call_target="tpu_custom_call" | custom-call | flops 1048576 | bytes 1048576 | tf_op jit(solution)/shard_map/expert/pallas_call | solution.py:484
  279.1 17.4 %expert_weights.2 = bf16[1024,3840]{1,0:T(8,128)(2,1)} custom-call(bf16[1280,1024]{1,0:T(8,128)(2,1)} %bitcast.172, bf16[1280,1024]{1,0:T(8,128)(2,1)} %get-tuple-element.148.low_ref.refs_11_, bf16[1280,2560]{1,0:T(8,128)(2,1)} %get-tuple-element.102.dboth_ref, bf16[1280,1280]{1,0:T(8,128)(2,1)} %get-tuple-element.103.hidden_ref), custom_call_target="tpu_custom_call" | custom-call | flops 1048576 | bytes 1048576 | tf_op jit(solution)/shard_map/expert_weights/pallas_call | solution.py:561
  306.1 6.3 collective-permute-start.18
  312.4 16.9 %probs.1.probs_ref = bf16[16,2,1280,256]{3,2,1,0:T(8,128)(2,1)} custom-call(bf16[512,1024]{1,0:T(8,128)(2,1)} %fusion.21.q_ref, bf16[1536,1024]{1,0:T(8,128)(2,1)} %convolution_convert_fusion.3.k_ref, bf16[512,128]{1,0:T(8,128)(2,1)} %compare_convert_fusion.qdoc_ref, bf16[1536,128]{1,0:T(8,128)(2,1)} %select_convert_fusion.kdoc_ref, ...), custom_call_target="tpu_custom_call" | custom-call | flops 1048576 | bytes 1048576 | tf_op jit(solution)/shard_map/probs/pallas_call | solution.py:214
  329.3 23.3 %collective-permute-done.18 = bf16[256,3840]{1,0:T(8,128)(2,1)} collective-permute-done((bf16[256,3840]{1,0:T(8,128)(2,1)}, bf16[256,3840]{1,0:T(8,128)(2,1)}, u32[]{:S(2)}, u32[]{:S(2)}) %collective-permute-start.18) | collective-permute-done | bytes 1966112 | tf_op jit(solution)/shard_map/ppermute | solution.py:678
  365.9 40.0 %collective-permute-done.22 = bf16[256,3840]{1,0:T(8,128)(2,1)S(1)} collective-permute-done((bf16[256,3840]{1,0:T(8,128)(2,1)S(1)}, bf16[256,3840]{1,0:T(8,128)(2,1)S(1)}, u32[]{:S(2)}, u32[]{:S(2)}) %collective-permute-start.22) | collective-permute-done | bytes 1966112 | tf_op jit(solution)/shard_map/ppermute | solution.py:678
  413.9 41.0 %expert.3 = (bf16[1280,1536]{1,0:T(8,128)(2,1)}, bf16[1280,3072]{1,0:T(8,128)(2,1)}, bf16[1280,1024]{1,0:T(8,128)(2,1)}, bf16[1280,1024]{1,0:T(8,128)(2,1)}, f32[1024,128]{1,0:T(8,128)}) custom-call(bf16[1280,1024]{1,0:T(8,128)(2,1)} %bitcast.173, bf16[256,4608]{1,0:T(8,128)(2,1)} %maximum_dynamic-update-slice_fusion.refs_1_, ...), custom_call_target="tpu_custom_call" | custom-call | flops 1048576 | bytes 1048576 | tf_op jit(solution)/shard_map/expert/pallas_call | solution.py:484
  456.2 20.0 %expert_weights.3 = bf16[1024,4608]{1,0:T(8,128)(2,1)} custom-call(bf16[1280,1024]{1,0:T(8,128)(2,1)} %bitcast.174, bf16[1280,1024]{1,0:T(8,128)(2,1)} %get-tuple-element.148.low_ref.refs_11_, bf16[1280,3072]{1,0:T(8,128)(2,1)} %get-tuple-element.149.dboth_ref, bf16[1280,1536]{1,0:T(8,128)(2,1)} %get-tuple-element.150.hidden_ref), custom_call_target="tpu_custom_call" | custom-call | flops 12079595520 | bytes 1048576 | tf_op jit(solution)/shard_map/expert_weights/pallas_call | solution.py:561
  487.6 25.6 %all-to-all-done.2 = bf16[8,160,1024]{2,1,0:T(8,128)(2,1)} async-done(((bf16[8,160,1024]{2,1,0:T(8,128)(2,1)}), bf16[8,160,1024]{2,1,0:T(8,128)(2,1)}, u32[]{:S(2)}, u32[]{:S(2)}) %all-to-all-start.2) | async-done | bytes 2621472 | tf_op jit(solution)/shard_map/all_to_all | solution.py:890
  527.2 25.7 %attend_back.1 = (bf16[512,1024]{1,0:T(8,128)(2,1)}, bf16[1536,1024]{1,0:T(8,128)(2,1)}, bf16[1536,1024]{1,0:T(8,128)(2,1)}, f32[8,2,1024]{2,1,0:T(2,128)}) custom-call(bf16[512,1024]{1,0:T(8,128)(2,1)} %fusion.21.q_ref, bf16[1536,1024]{1,0:T(8,128)(2,1)} %convolution_convert_fusion.3.k_ref, bf16[1536,1024]{1,0:T(8,128)(2,1)} %convolution_convert_fusion.2.v_ref, ...), custom_call_target="tpu_custom_call" | custom-call | flops 21474836480 | bytes 1048576 | tf_op jit(solution)/shard_map/attend_back/pallas_call | solution.py:282
  554.0 15.8 %normed_grad.1 = (bf16[1024,1024]{1,0:T(8,128)(2,1)}, f32[512,1024]{1,0:T(8,128)}, f32[8,1024]{1,0:T(8,128)}) custom-call(bf16[1536,1024]{1,0:T(8,128)(2,1)} %copy-done.3, bf16[512,1024]{1,0:T(8,128)(2,1)} %get-tuple-element.138.q_ref, bf16[1536,1024]{1,0:T(8,128)(2,1)} %get-tuple-element.134.k_ref, bf16[1536,1024]{1,0:T(8,128)(2,1)} %get-tuple-element.135.v_ref, ...), custom_call_target="tpu_custom_call" | custom-call | flops 1048576 | bytes 1048576 | tf_op jit(solution)/shard_map/normed_grad/pallas_call | solution.py:798
  572.0 19.1 %slabs.1 = (bf16[16,144,1024]{2,1,0:T(8,128)(2,1)}, bf16[16,144,1024]{2,1,0:T(8,128)(2,1)}) custom-call(bf16[1536,1024]{1,0:T(8,128)(2,1)} %copy-done.5, bf16[512,1024]{1,0:T(8,128)(2,1)} %get-tuple-element.138.q_ref, bf16[1536,1024]{1,0:T(8,128)(2,1)} %get-tuple-element.134.k_ref, bf16[1536,1024]{1,0:T(8,128)(2,1)} %get-tuple-element.135.v_ref, ...), custom_call_target="tpu_custom_call" | custom-call | flops 1048576 | bytes 1048576 | tf_op jit(solution)/shard_map/slabs/pallas_call | solution.py:864
  591.8 7.7 %collective-permute-done.26 = bf16[16,144,1024]{2,1,0:T(8,128)(2,1)S(1)} collective-permute-done((bf16[16,144,1024]{2,1,0:T(8,128)(2,1)}, bf16[16,144,1024]{2,1,0:T(8,128)(2,1)S(1)}, u32[]{:S(2)}, u32[]{:S(2)}) %collective-permute-start.26) | collective-permute-done | bytes 4718624 | tf_op jit(solution)/shard_map/ppermute | solution.py:687
  610.7 23.1 %collective-permute-done.29 = bf16[2,2,144,1024]{3,2,0,1:T(8,128)(2,1)S(1)} collective-permute-done((bf16[2,2,144,1024]{3,2,0,1:T(8,128)(2,1)S(1)}, bf16[2,2,144,1024]{3,2,0,1:T(8,128)(2,1)S(1)}, u32[]{:S(2)}, u32[]{:S(2)}) %collective-permute-start.29) | collective-permute-done | bytes 1179680 | tf_op jit(solution)/shard_map/ppermute | solution.py:687
  638.7 10.8 %collective-permute-done.30 = bf16[2,144,1024]{2,1,0:T(8,128)(2,1)S(1)} collective-permute-done((bf16[2,144,1024]{2,1,0:T(8,128)(2,1)S(1)}, bf16[2,144,1024]{2,1,0:T(8,128)(2,1)S(1)}, u32[]{:S(2)}, u32[]{:S(2)}) %collective-permute-start.30) | collective-permute-done | bytes 589856 | tf_op jit(solution)/shard_map/ppermute | solution.py:687
  652.1 8.4 %collective-permute-done.31 = bf16[512,1024]{1,0:T(8,128)(2,1)S(1)} collective-permute-done((bf16[512,1024]{1,0:T(8,128)(2,1)S(1)}, bf16[512,1024]{1,0:T(8,128)(2,1)S(1)}, u32[]{:S(2)}, u32[]{:S(2)}) %collective-permute-start.31) | collective-permute-done | bytes 1048608 | tf_op jit(solution)/shard_map/ppermute | solution.py:30
  669.5 7.5 %expert_sums.1 = (f32[256,2816]{1,0:T(8,128)}, f32[256,2816]{1,0:T(8,128)}, f32[704,1024]{1,0:T(8,128)}) custom-call(bf16[256,3840]{1,0:T(8,128)(2,1)} %get-tuple-element.204.own_ref, bf16[256,3840]{1,0:T(8,128)(2,1)} %copy-done.34, bf16[256,3840]{1,0:T(8,128)(2,1)} %collective-permute-done.25.down_ref, ...), custom_call_target="tpu_custom_call" | custom-call | flops 1048576 | bytes 1048576 | tf_op jit(solution)/shard_map/expert_sums/pallas_call | solution.py:615
  (323 shorter events, 275.1 us)
Async XLA Ops:
  7.2 97.4 %all-gather.6.cloned.1.call-start = ((), (), s32[]{:S(2)}) async-start(), calls=%async_computation.7 | async-start | bytes 1081344 | tf_op jit(solution)/shard_map/all_gather | solution.py:949
  8.9 37.1 %collective-permute-start = (bf16[1,128,1024]{2,1,0:T(8,128)(2,1)}, bf16[1,128,1024]{2,1,0:T(8,128)(2,1)}, u32[]{:S(2)}, u32[]{:S(2)}) collective-permute-start(bf16[1,128,1024]{2,1,0:T(8,128)(2,1)} %maximum_bitcast_fusion.2), channel_id=1, source_target_pairs={{0,8},{8,16},{16,24},{1,9},{9,17},{17,25},{2,10},{10,18},{18,26},{... | collective-permute-start | bytes 786440 | tf_op jit(solution)/shard_map/ppermute | solution.py:30
  14.5 33.3 %collective-permute-start.1 = (bf16[1,128,1024]{2,1,0:T(8,128)(2,1)}, bf16[1,128,1024]{2,1,0:T(8,128)(2,1)}, u32[]{:S(2)}, u32[]{:S(2)}) collective-permute-start(bf16[1,128,1024]{2,1,0:T(8,128)(2,1)} %maximum_bitcast_fusion.2), channel_id=1, source_target_pairs={{8,0},{16,8},{24,16},{9,1},{17,9},{25,17},{10,2},{18,10},{26,18},{... | collective-permute-start | bytes 786440 | tf_op jit(solution)/shard_map/ppermute | solution.py:30
  18.1 53.3 %collective-permute-start.6 = (bf16[512,1024]{1,0:T(8,128)(2,1)}, bf16[512,1024]{1,0:T(8,128)(2,1)}, u32[]{:S(2)}, u32[]{:S(2)}) collective-permute-start(bf16[512,1024]{1,0:T(8,128)(2,1)} %bitcast.179), channel_id=1, source_target_pairs={{0,8},{8,16},{16,24},{1,9},{9,17},{17,25},{2,10},{10,18},{18,26},{... | collective-permute-start | bytes 3145736 | tf_op jit(solution)/shard_map/ppermute | solution.py:30
  30.2 42.3 %all-to-all-start = ((bf16[8,160,1152]{2,1,0:T(8,128)(2,1)}), bf16[8,160,1152]{2,1,0:T(8,128)(2,1)S(1)}, u32[]{:S(2)}, u32[]{:S(2)}) async-start(bf16[8,160,1152]{2,1,0:T(8,128)(2,1)} %bitcast.198), calls=%async_computation | async-start | bytes 5898240 | tf_op jit(solution)/shard_map/all_to_all | solution.py:890
  34.0 204.0 %all-gather.4.cloned.1.call-start = ((), (), s32[]{:S(2)}) async-start(), calls=%async_computation.5 | async-start | bytes 9830400 | tf_op jit(solution)/shard_map/all_gather | solution.py:968
  191.8 35.8 %all-to-all-start.1 = ((bf16[8,160,1024]{2,1,0:T(8,128)(2,1)}), bf16[8,160,1024]{2,1,0:T(8,128)(2,1)S(1)}, u32[]{:S(2)}, u32[]{:S(2)}) async-start(bf16[8,160,1024]{2,1,0:T(8,128)(2,1)} %bitcast.201), calls=%async_computation.1 | async-start | bytes 5242880 | tf_op jit(solution)/shard_map/all_to_all | solution.py:890
  195.4 474.1 %reduce-scatter.2.cloned.1.call-start = ((), (), s32[]{:S(2)}) async-start(), calls=%async_computation.6 | async-start | bytes 11796480 | tf_op jit(solution)/shard_map/reduce_scatter | solution.py:1025
  238.0 58.6 %collective-permute-start.15 = (bf16[256,4608]{1,0:T(8,128)(2,1)}, bf16[256,4608]{1,0:T(8,128)(2,1)}, u32[]{:S(2)}, u32[]{:S(2)}) collective-permute-start(bf16[256,4608]{1,0:T(8,128)(2,1)} %maximum_dynamic-update-slice_fusion.refs_1_), channel_id=1, source_target_pairs={{24,16},{16,8},{8,0},{25,17},{17,9},{9,1},{26,18},{18,10},{10,2},{... | collective-permute-start | bytes 7077896 | tf_op jit(solution)/shard_map/ppermute | solution.py:658
  239.3 57.3 %collective-permute-start.14 = (bf16[256,4608]{1,0:T(8,128)(2,1)}, bf16[256,4608]{1,0:T(8,128)(2,1)}, u32[]{:S(2)}, u32[]{:S(2)}) collective-permute-start(bf16[256,4608]{1,0:T(8,128)(2,1)} %maximum_dynamic-update-slice_fusion.refs_1_), channel_id=1, source_target_pairs={{0,8},{8,16},{16,24},{1,9},{9,17},{17,25},{2,10},{10,18},{18,26},{... | collective-permute-start | bytes 7077896 | tf_op jit(solution)/shard_map/ppermute | solution.py:658
  296.5 56.1 %collective-permute-start.16 = (bf16[256,4608]{1,0:T(8,128)(2,1)}, bf16[256,4608]{1,0:T(8,128)(2,1)S(1)}, u32[]{:S(2)}, u32[]{:S(2)}) collective-permute-start(bf16[256,4608]{1,0:T(8,128)(2,1)} %collective-permute-done.14.refs_2_), channel_id=1, source_target_pairs={{8,16},{16,24},{9,17},{17,25},{10,18},{18,26},{11,19},{19,27},{12,... | collective-permute-start | bytes 7077896 | tf_op jit(solution)/shard_map/ppermute | solution.py:658
  297.4 55.3 %collective-permute-start.17 = (bf16[256,4608]{1,0:T(8,128)(2,1)}, bf16[256,4608]{1,0:T(8,128)(2,1)S(1)}, u32[]{:S(2)}, u32[]{:S(2)}) collective-permute-start(bf16[256,4608]{1,0:T(8,128)(2,1)} %collective-permute-done.15.refs_3_), channel_id=1, source_target_pairs={{16,8},{8,0},{17,9},{9,1},{18,10},{10,2},{19,11},{11,3},{20,12},{1... | collective-permute-start | bytes 7077896 | tf_op jit(solution)/shard_map/ppermute | solution.py:658
  306.1 46.5 %collective-permute-start.18 = (bf16[256,3840]{1,0:T(8,128)(2,1)}, bf16[256,3840]{1,0:T(8,128)(2,1)}, u32[]{:S(2)}, u32[]{:S(2)}) collective-permute-start(bf16[256,3840]{1,0:T(8,128)(2,1)} %get-tuple-element.206), channel_id=1, source_target_pairs={{0,8},{1,9},{2,10},{3,11},{4,12},{5,13},{6,14},{7,15}} | collective-permute-start | bytes 5898248 | tf_op jit(solution)/shard_map/ppermute | solution.py:678
  352.6 53.2 %collective-permute-start.20 = (bf16[256,4608]{1,0:T(8,128)(2,1)S(1)}, bf16[256,4608]{1,0:T(8,128)(2,1)S(1)}, u32[]{:S(2)}, u32[]{:S(2)}) collective-permute-start(bf16[256,4608]{1,0:T(8,128)(2,1)S(1)} %collective-permute-done.16.refs_4_), channel_id=1, source_target_pairs={{16,24},{17,25},{18,26},{19,27},{20,28},{21,29},{22,30},{23,31}} | collective-permute-start | bytes 7077896 | tf_op jit(solution)/shard_map/ppermute | solution.py:658
  353.4 53.2 %collective-permute-start.21 = (bf16[256,4608]{1,0:T(8,128)(2,1)S(1)}, bf16[256,4608]{1,0:T(8,128)(2,1)S(1)}, u32[]{:S(2)}, u32[]{:S(2)}) collective-permute-start(bf16[256,4608]{1,0:T(8,128)(2,1)S(1)} %collective-permute-done.17.refs_5_), channel_id=1, source_target_pairs={{8,0},{9,1},{10,2},{11,3},{12,4},{13,5},{14,6},{15,7}} | collective-permute-start | bytes 7077896 | tf_op jit(solution)/shard_map/ppermute | solution.py:658
  360.5 45.3 %collective-permute-start.22 = (bf16[256,3840]{1,0:T(8,128)(2,1)S(1)}, bf16[256,3840]{1,0:T(8,128)(2,1)S(1)}, u32[]{:S(2)}, u32[]{:S(2)}) collective-permute-start(bf16[256,3840]{1,0:T(8,128)(2,1)S(1)} %get-tuple-element.210), channel_id=1, source_target_pairs={{0,8},{8,16},{1,9},{9,17},{2,10},{10,18},{3,11},{11,19},{4,12},{12... | collective-permute-start | bytes 5898248 | tf_op jit(solution)/shard_map/ppermute | solution.py:678
  408.1 46.9 %collective-permute-start.24 = (bf16[256,3840]{1,0:T(8,128)(2,1)S(1)}, bf16[256,3840]{1,0:T(8,128)(2,1)S(1)}, u32[]{:S(2)}, u32[]{:S(2)}) collective-permute-start(bf16[256,3840]{1,0:T(8,128)(2,1)S(1)} %get-tuple-element.125), channel_id=1, source_target_pairs={{0,8},{8,16},{16,24},{1,9},{9,17},{17,25},{2,10},{10,18},{18,26},{... | collective-permute-start | bytes 5898248 | tf_op jit(solution)/shard_map/ppermute | solution.py:678
  412.6 43.6 %collective-permute-start.25 = (bf16[256,3840]{1,0:T(8,128)(2,1)S(1)}, bf16[256,3840]{1,0:T(8,128)(2,1)}, u32[]{:S(2)}, u32[]{:S(2)}) collective-permute-start(bf16[256,3840]{1,0:T(8,128)(2,1)S(1)} %get-tuple-element.126), channel_id=1, source_target_pairs={{24,16},{16,8},{8,0},{25,17},{17,9},{9,1},{26,18},{18,10},{10,2},{... | collective-permute-start | bytes 5898248 | tf_op jit(solution)/shard_map/ppermute | solution.py:678
  476.2 37.0 %all-to-all-start.2 = ((bf16[8,160,1024]{2,1,0:T(8,128)(2,1)}), bf16[8,160,1024]{2,1,0:T(8,128)(2,1)}, u32[]{:S(2)}, u32[]{:S(2)}) async-start(bf16[8,160,1024]{2,1,0:T(8,128)(2,1)} %bitcast.200), calls=%async_computation.2 | async-start | bytes 5242880 | tf_op jit(solution)/shard_map/all_to_all | solution.py:890
  522.8 49.2 %all-to-all-start.3 = ((bf16[8,160,1024]{2,1,0:T(8,128)(2,1)}), bf16[8,160,1024]{2,1,0:T(8,128)(2,1)}, u32[]{:S(2)}, u32[]{:S(2)}) async-start(bf16[8,160,1024]{2,1,0:T(8,128)(2,1)} %bitcast.199), calls=%async_computation.3 | async-start | bytes 5242880 | tf_op jit(solution)/shard_map/all_to_all | solution.py:890
  605.4 28.3 %collective-permute-start.29 = (bf16[2,2,144,1024]{3,2,0,1:T(8,128)(2,1)S(1)}, bf16[2,2,144,1024]{3,2,0,1:T(8,128)(2,1)S(1)}, u32[]{:S(2)}, u32[]{:S(2)}) collective-permute-start(bf16[2,2,144,1024]{3,2,0,1:T(8,128)(2,1)S(1)} %select_bitcast_fusion), channel_id=1, source_target_pairs={{0,4},{1,5},{2,6},{3,7},{4,0},{5,1},{6,2},{7,3},{8,12},{9,13},{10,... | collective-permute-start | bytes 3538952 | tf_op jit(solution)/shard_map/ppermute | solution.py:687
  607.7 28.6 %collective-permute-start.27 = (bf16[2,2,144,1024]{3,2,0,1:T(8,128)(2,1)S(1)}, bf16[2,2,144,1024]{3,2,0,1:T(8,128)(2,1)S(1)}, u32[]{:S(2)}, u32[]{:S(2)}) collective-permute-start(bf16[2,2,144,1024]{3,2,0,1:T(8,128)(2,1)S(1)} %select_bitcast_fusion.1), channel_id=1, source_target_pairs={{0,2},{1,3},{2,0},{3,1},{4,6},{5,7},{6,4},{7,5},{8,10},{9,11},{10,... | collective-permute-start | bytes 3538952 | tf_op jit(solution)/shard_map/ppermute | solution.py:687
  609.4 51.1 %collective-permute-start.31 = (bf16[512,1024]{1,0:T(8,128)(2,1)S(1)}, bf16[512,1024]{1,0:T(8,128)(2,1)S(1)}, u32[]{:S(2)}, u32[]{:S(2)}) collective-permute-start(bf16[512,1024]{1,0:T(8,128)(2,1)S(1)} %slice.279), channel_id=1, source_target_pairs={{8,0},{16,8},{24,16},{9,1},{17,9},{25,17},{10,2},{18,10},{26,18},{... | collective-permute-start | bytes 3145736 | tf_op jit(solution)/shard_map/ppermute | solution.py:30
  668.2 27.1 %collective-permute-start.32 = (bf16[512,1024]{1,0:T(8,128)(2,1)}, bf16[512,1024]{1,0:T(8,128)(2,1)}, u32[]{:S(2)}, u32[]{:S(2)}) collective-permute-start(bf16[512,1024]{1,0:T(8,128)(2,1)} %add_convert_fusion.1), channel_id=1, source_target_pairs={{8,0},{16,8},{24,16},{9,1},{17,9},{25,17},{10,2},{18,10},{26,18},{... | collective-permute-start | bytes 3145736 | tf_op jit(solution)/shard_map/ppermute | solution.py:30
  (75 other events, 789.3 us)
Sparse Core Ops, SparseCore 0:
  18.2 60.8 all-gather.5
  96.6 141.3 all-gather.3
  476.3 183.2 reduce-scatter.1

commit v5 on v4

--- a/solution.py
+++ b/solution.py
@@ -665,6 +665,8 @@
         return lax.dynamic_index_in_dim(parts, jnp.clip(at, 0, count - 1), 0, keepdims=False).astype(F32)
 
     distance = count - hop
+    if hop == 1:
+        return parts[count - 1].astype(BF16), parts[0].astype(BF16)
     mine_up, mine_down = part(index + distance), part(index - distance)
     if up is not None:
         mine_up, mine_down = mine_up + up.astype(F32), mine_down + down.astype(F32)
@@ -1022,6 +1024,7 @@
     low, made, back, _ = carried
     hidden, dboth, low, made, back, *sent = together(hidden, dboth, low, made, back, *sent)
     grad1 = expert_weights(units1, ctx_count, arrived, low, dboth, hidden, True)
+    back, grad1 = together(back, grad1)
     total1 = lax.psum_scatter(grad1, "ctx", scatter_dimension=0, tiled=True)
     back = exchange(back.reshape(experts, capacity, width)).reshape(-1, width)
 
@@ -1064,7 +1067,7 @@
     pieces = [halo_grad[place * rows : (place + 1) * rows] for place in range(reach)]
     returning = shift_ctx(pieces[0], -1)
     for piece in pieces[1:]:
-        parts, returning = together(parts, returning)
+        parts, returning, output = together(parts, returning, output)
         returning = shift_ctx((piece.astype(F32) + returning.astype(F32)).astype(BF16), -1)
     own0 = lax.dynamic_index_in_dim(parts0, ctx_index, 0, keepdims=False)
     expert_grads = expert_sums(sizes, ctx_count, own0, *sent, total1)

time: 728 us -> 730 us (level)
  transfers between devices with their start and end apart: 46 -> 46, of which waited for: 25 -> 26; matrix products, arithmetic and copies ran while one was open for 19% -> 19% of each run, Pallas kernels for 30% -> 29%
where the time goes in v5:
time: 730 us; the launch traced here: 722 us
  Pallas kernels  233 us (32%)
  waiting for transfers between devices  221 us (30%)
  starting transfers between devices  105 us (14%)
  other arithmetic  61.8 us (8%)
  local copies, waits for them, and re-layouts  50.3 us (7%)
  matrix products  35.1 us (5%)
  between operations  15.2 us (2%)
    ppermute x12, waiting for transfers between devices, scatter_hop(): return (lax.ppermute(up, 'ctx', route), lax.ppermute(down, 'ctx', back))  77.2 us
    pallas_call x2, Pallas kernels, run_expert(): pl.pallas_call(functools.partial(expert_kernel, first, last, units, count...  73.8 us
    ppermute x11, waiting for transfers between devices, swap_exp(): lax.ppermute(block, 'exp', [(i, i ^ bit) for i in range(lax.axis_size('ex...  57.6 us
    all_to_all x4, waiting for transfers between devices, exchange(): lax.all_to_all(blocks, 'exp', split_axis=0, concat_axis=0, tiled=True)  45.1 us
    pallas_call x2, Pallas kernels, expert_weights(): pl.pallas_call(functools.partial(expert_weights_kernel, units, count), gr...  37.4 us
    ppermute x12, starting transfers between devices, scatter_hop(): return (lax.ppermute(up, 'ctx', route), lax.ppermute(down, 'ctx', back))  35.6 us
    ppermute x10, waiting for transfers between devices, shift_ctx(): return lax.ppermute(block, 'ctx', route)  29.4 us
    pallas_call x1, Pallas kernels, attend(): pl.pallas_call(attend_kernel, grid=(pairs,), in_specs=[pl.BlockSpec((rows...  28.9 us
  transfers between devices with their start and end apart: 46, of which 26 were waited for; matrix products, arithmetic and copies ran while one was open for 19% of the time, Pallas kernels for 29%

profile of v5, /device:TPU:0, one launch (start us, length us, event | category | flops | bytes accessed | tf_op | source)
XLA Modules:
  0.0 721.5 jit_solution(18245092910599782065)
XLA Ops:
  80.4 8.4 %collective-permute-done.8 = bf16[1,2,128,1024]{3,2,1,0:T(8,128)(2,1)S(1)} collective-permute-done((bf16[1,2,128,1024]{3,2,1,0:T(8,128)(2,1)S(1)}, bf16[1,2,128,1024]{3,2,1,0:T(8,128)(2,1)S(1)}, u32[]{:S(2)}, u32[]{:S(2)}) %collective-permute-start.8) | collective-permute-done | bytes 524320 | tf_op jit(solution)/shard_map/ppermute | solution.py:689
  106.7 7.3 %bias_band.1.band_ref = f32[16,1152,128]{2,1,0:T(8,128)} custom-call(f32[16,1280]{1,0:T(8,128)} %pad_maximum_fusion.9.bias_ref), custom_call_target="tpu_custom_call" | custom-call | flops 1048576 | bytes 1048576 | tf_op jit(solution)/shard_map/bias_band/pallas_call | solution.py:75
  114.0 8.6 %collective-permute-done.11 = bf16[2,2,128,1024]{3,2,1,0:T(8,128)(2,1)S(1)} collective-permute-done((bf16[2,2,128,1024]{3,2,1,0:T(8,128)(2,1)}, bf16[2,2,128,1024]{3,2,1,0:T(8,128)(2,1)S(1)}, u32[]{:S(2)}, u32[]{:S(2)}) %collective-permute-start.11) | collective-permute-done | bytes 1048608 | tf_op jit(solution)/shard_map/ppermute | solution.py:689
  157.1 28.9 %attend.1 = (bf16[512,1024]{1,0:T(8,128)(2,1)}, f32[8,2,512]{2,1,0:T(2,128)}) custom-call(bf16[512,1024]{1,0:T(8,128)(2,1)} %fusion.21.q_ref, bf16[1536,1024]{1,0:T(8,128)(2,1)} %convolution_convert_fusion.3.k_ref, bf16[1536,1024]{1,0:T(8,128)(2,1)} %convolution_convert_fusion.2.v_ref, bf16[512,128]{1,0:T(8,128)(2,1)} %compare_convert_fusion.qdoc_ref, ...), custom_call_target="tpu_custom_call" | custom-call | flops 1048576 | bytes 1048576 | tf_op jit(solution)/shard_map/attend/pallas_call | solution.py:169
  209.3 18.3 %all-to-all-done.1 = bf16[8,160,1024]{2,1,0:T(8,128)(2,1)S(1)} async-done(((bf16[8,160,1024]{2,1,0:T(8,128)(2,1)}), bf16[8,160,1024]{2,1,0:T(8,128)(2,1)S(1)}, u32[]{:S(2)}, u32[]{:S(2)}) %all-to-all-start.1) | async-done | bytes 2621472 | tf_op jit(solution)/shard_map/all_to_all | solution.py:892
  227.6 10.4 %all-gather.4.cloned.1.call-done.refs_1_ = bf16[1024,3840]{1,0:T(8,128)(2,1)} async-done(((bf16[256,3840]{1,0:T(8,128)(2,1)}), bf16[1024,3840]{1,0:T(8,128)(2,1)}) %all-gather.4.cloned.1.call-update) | async-done | bytes 7864336 | tf_op jit(solution)/shard_map/all_gather | solution.py:970
  246.5 32.7 %expert.2 = (bf16[1280,1280]{1,0:T(8,128)(2,1)}, bf16[1280,2560]{1,0:T(8,128)(2,1)}, bf16[1280,1024]{1,0:T(8,128)(2,1)}, f32[1280,128]{1,0:T(8,128)}, f32[1280,1024]{1,0:T(8,128)}, /*index=5*/f32[1280,1024]{1,0:T(8,128)}) custom-call(bf16[1280,1024]{1,0:T(8,128)(2,1)} %bitcast.166, bf16[1024,3840]{1,0:T(8,128)(2,1)} %all-gather.4.cloned.1.call-done.refs_1_, ...), custom_call_target="tpu_custom_call" | custom-call | flops 1048576 | bytes 1048576 | tf_op jit(solution)/shard_map/expert/pallas_call | solution.py:484
  279.2 17.4 %expert_weights.2 = bf16[1024,3840]{1,0:T(8,128)(2,1)} custom-call(bf16[1280,1024]{1,0:T(8,128)(2,1)} %bitcast.167, bf16[1280,1024]{1,0:T(8,128)(2,1)} %get-tuple-element.132.low_ref.refs_11_, bf16[1280,2560]{1,0:T(8,128)(2,1)} %get-tuple-element.105.dboth_ref, bf16[1280,1280]{1,0:T(8,128)(2,1)} %get-tuple-element.106.hidden_ref), custom_call_target="tpu_custom_call" | custom-call | flops 1048576 | bytes 1048576 | tf_op jit(solution)/shard_map/expert_weights/pallas_call | solution.py:561
  305.0 6.2 collective-permute-start.18
  311.2 16.9 %probs.1.probs_ref = bf16[16,2,1280,256]{3,2,1,0:T(8,128)(2,1)} custom-call(bf16[512,1024]{1,0:T(8,128)(2,1)} %fusion.21.q_ref, bf16[1536,1024]{1,0:T(8,128)(2,1)} %convolution_convert_fusion.3.k_ref, bf16[512,128]{1,0:T(8,128)(2,1)} %compare_convert_fusion.qdoc_ref, bf16[1536,128]{1,0:T(8,128)(2,1)} %select_convert_fusion.kdoc_ref, ...), custom_call_target="tpu_custom_call" | custom-call | flops 1048576 | bytes 1048576 | tf_op jit(solution)/shard_map/probs/pallas_call | solution.py:214
  328.1 23.3 %collective-permute-done.18 = bf16[256,3840]{1,0:T(8,128)(2,1)} collective-permute-done((bf16[256,3840]{1,0:T(8,128)(2,1)}, bf16[256,3840]{1,0:T(8,128)(2,1)}, u32[]{:S(2)}, u32[]{:S(2)}) %collective-permute-start.18) | collective-permute-done | bytes 1966112 | tf_op jit(solution)/shard_map/ppermute | solution.py:680
  365.6 40.2 %collective-permute-done.22 = bf16[256,3840]{1,0:T(8,128)(2,1)S(1)} collective-permute-done((bf16[256,3840]{1,0:T(8,128)(2,1)S(1)}, bf16[256,3840]{1,0:T(8,128)(2,1)S(1)}, u32[]{:S(2)}, u32[]{:S(2)}) %collective-permute-start.22) | collective-permute-done | bytes 1966112 | tf_op jit(solution)/shard_map/ppermute | solution.py:680
  413.7 41.1 %expert.3 = (bf16[1280,1536]{1,0:T(8,128)(2,1)}, bf16[1280,3072]{1,0:T(8,128)(2,1)}, bf16[1280,1024]{1,0:T(8,128)(2,1)}, bf16[1280,1024]{1,0:T(8,128)(2,1)}, f32[1024,128]{1,0:T(8,128)}) custom-call(bf16[1280,1024]{1,0:T(8,128)(2,1)} %bitcast.168, bf16[256,4608]{1,0:T(8,128)(2,1)} %maximum_dynamic-update-slice_fusion.refs_1_, ...), custom_call_target="tpu_custom_call" | custom-call | flops 1048576 | bytes 1048576 | tf_op jit(solution)/shard_map/expert/pallas_call | solution.py:484
  456.3 20.0 %expert_weights.3 = bf16[1024,4608]{1,0:T(8,128)(2,1)} custom-call(bf16[1280,1024]{1,0:T(8,128)(2,1)} %bitcast.169, bf16[1280,1024]{1,0:T(8,128)(2,1)} %get-tuple-element.132.low_ref.refs_11_, bf16[1280,3072]{1,0:T(8,128)(2,1)} %get-tuple-element.133.dboth_ref, bf16[1280,1536]{1,0:T(8,128)(2,1)} %get-tuple-element.134.hidden_ref), custom_call_target="tpu_custom_call" | custom-call | flops 12079595520 | bytes 1048576 | tf_op jit(solution)/shard_map/expert_weights/pallas_call | solution.py:561
  487.7 25.6 %all-to-all-done.2 = bf16[8,160,1024]{2,1,0:T(8,128)(2,1)} async-done(((bf16[8,160,1024]{2,1,0:T(8,128)(2,1)}), bf16[8,160,1024]{2,1,0:T(8,128)(2,1)}, u32[]{:S(2)}, u32[]{:S(2)}) %all-to-all-start.2) | async-done | bytes 2621472 | tf_op jit(solution)/shard_map/all_to_all | solution.py:892
  527.2 25.7 %attend_back.1 = (bf16[512,1024]{1,0:T(8,128)(2,1)}, bf16[1536,1024]{1,0:T(8,128)(2,1)}, bf16[1536,1024]{1,0:T(8,128)(2,1)}, f32[8,2,1024]{2,1,0:T(2,128)}) custom-call(bf16[512,1024]{1,0:T(8,128)(2,1)} %fusion.21.q_ref, bf16[1536,1024]{1,0:T(8,128)(2,1)} %convolution_convert_fusion.3.k_ref, bf16[1536,1024]{1,0:T(8,128)(2,1)} %convolution_convert_fusion.2.v_ref, ...), custom_call_target="tpu_custom_call" | custom-call | flops 21474836480 | bytes 1048576 | tf_op jit(solution)/shard_map/attend_back/pallas_call | solution.py:282
  554.1 15.9 %normed_grad.1 = (bf16[1024,1024]{1,0:T(8,128)(2,1)}, f32[512,1024]{1,0:T(8,128)}, f32[8,1024]{1,0:T(8,128)}) custom-call(bf16[1536,1024]{1,0:T(8,128)(2,1)} %copy-done.3, bf16[512,1024]{1,0:T(8,128)(2,1)} %get-tuple-element.140.q_ref, bf16[1536,1024]{1,0:T(8,128)(2,1)} %get-tuple-element.141.k_ref, bf16[1536,1024]{1,0:T(8,128)(2,1)} %get-tuple-element.142.v_ref, ...), custom_call_target="tpu_custom_call" | custom-call | flops 1048576 | bytes 1048576 | tf_op jit(solution)/shard_map/normed_grad/pallas_call | solution.py:800
  572.1 19.1 %slabs.1 = (bf16[16,144,1024]{2,1,0:T(8,128)(2,1)}, bf16[16,144,1024]{2,1,0:T(8,128)(2,1)}) custom-call(bf16[1536,1024]{1,0:T(8,128)(2,1)} %copy-done.5, bf16[512,1024]{1,0:T(8,128)(2,1)} %get-tuple-element.140.q_ref, bf16[1536,1024]{1,0:T(8,128)(2,1)} %get-tuple-element.141.k_ref, bf16[1536,1024]{1,0:T(8,128)(2,1)} %get-tuple-element.142.v_ref, ...), custom_call_target="tpu_custom_call" | custom-call | flops 1048576 | bytes 1048576 | tf_op jit(solution)/shard_map/slabs/pallas_call | solution.py:866
  591.8 7.7 %collective-permute-done.26 = bf16[16,144,1024]{2,1,0:T(8,128)(2,1)S(1)} collective-permute-done((bf16[16,144,1024]{2,1,0:T(8,128)(2,1)}, bf16[16,144,1024]{2,1,0:T(8,128)(2,1)S(1)}, u32[]{:S(2)}, u32[]{:S(2)}) %collective-permute-start.26) | collective-permute-done | bytes 4718624 | tf_op jit(solution)/shard_map/ppermute | solution.py:689
  610.6 23.1 %collective-permute-done.29 = bf16[2,2,144,1024]{3,2,0,1:T(8,128)(2,1)S(1)} collective-permute-done((bf16[2,2,144,1024]{3,2,0,1:T(8,128)(2,1)S(1)}, bf16[2,2,144,1024]{3,2,0,1:T(8,128)(2,1)S(1)}, u32[]{:S(2)}, u32[]{:S(2)}) %collective-permute-start.29) | collective-permute-done | bytes 1179680 | tf_op jit(solution)/shard_map/ppermute | solution.py:689
  643.1 6.5 collective-permute-done.30
  652.1 8.3 %collective-permute-done.31 = bf16[512,1024]{1,0:T(8,128)(2,1)S(1)} collective-permute-done((bf16[512,1024]{1,0:T(8,128)(2,1)S(1)}, bf16[512,1024]{1,0:T(8,128)(2,1)S(1)}, u32[]{:S(2)}, u32[]{:S(2)}) %collective-permute-start.31) | collective-permute-done | bytes 1048608 | tf_op jit(solution)/shard_map/ppermute | solution.py:30
  672.4 7.6 %expert_sums.1 = (f32[256,2816]{1,0:T(8,128)}, f32[256,2816]{1,0:T(8,128)}, f32[704,1024]{1,0:T(8,128)}) custom-call(bf16[256,3840]{1,0:T(8,128)(2,1)} %dynamic-slice_bitcast_fusion.own_ref, bf16[256,3840]{1,0:T(8,128)(2,1)} %copy-done.34, bf16[256,3840]{1,0:T(8,128)(2,1)} %collective-permute-done.25.down_ref, ...), custom_call_target="tpu_custom_call" | custom-call | flops 1048576 | bytes 1048576 | tf_op jit(solution)/shard_map/expert_sums/pallas_call | solution.py:615
  705.8 6.1 collective-permute-done.38
  (324 shorter events, 281.1 us)
Async XLA Ops:
  7.2 97.4 %all-gather.6.cloned.1.call-start = ((), (), s32[]{:S(2)}) async-start(), calls=%async_computation.7 | async-start | bytes 1081344 | tf_op jit(solution)/shard_map/all_gather | solution.py:951
  8.9 37.1 %collective-permute-start = (bf16[1,128,1024]{2,1,0:T(8,128)(2,1)}, bf16[1,128,1024]{2,1,0:T(8,128)(2,1)}, u32[]{:S(2)}, u32[]{:S(2)}) collective-permute-start(bf16[1,128,1024]{2,1,0:T(8,128)(2,1)} %maximum_bitcast_fusion.2), channel_id=1, source_target_pairs={{0,8},{8,16},{16,24},{1,9},{9,17},{17,25},{2,10},{10,18},{18,26},{... | collective-permute-start | bytes 786440 | tf_op jit(solution)/shard_map/ppermute | solution.py:30
  14.5 33.4 %collective-permute-start.1 = (bf16[1,128,1024]{2,1,0:T(8,128)(2,1)}, bf16[1,128,1024]{2,1,0:T(8,128)(2,1)}, u32[]{:S(2)}, u32[]{:S(2)}) collective-permute-start(bf16[1,128,1024]{2,1,0:T(8,128)(2,1)} %maximum_bitcast_fusion.2), channel_id=1, source_target_pairs={{8,0},{16,8},{24,16},{9,1},{17,9},{25,17},{10,2},{18,10},{26,18},{... | collective-permute-start | bytes 786440 | tf_op jit(solution)/shard_map/ppermute | solution.py:30
  18.1 53.3 %collective-permute-start.6 = (bf16[512,1024]{1,0:T(8,128)(2,1)}, bf16[512,1024]{1,0:T(8,128)(2,1)}, u32[]{:S(2)}, u32[]{:S(2)}) collective-permute-start(bf16[512,1024]{1,0:T(8,128)(2,1)} %bitcast.174), channel_id=1, source_target_pairs={{0,8},{8,16},{16,24},{1,9},{9,17},{17,25},{2,10},{10,18},{18,26},{... | collective-permute-start | bytes 3145736 | tf_op jit(solution)/shard_map/ppermute | solution.py:30
  30.2 42.3 %all-to-all-start = ((bf16[8,160,1152]{2,1,0:T(8,128)(2,1)}), bf16[8,160,1152]{2,1,0:T(8,128)(2,1)S(1)}, u32[]{:S(2)}, u32[]{:S(2)}) async-start(bf16[8,160,1152]{2,1,0:T(8,128)(2,1)} %bitcast.193), calls=%async_computation | async-start | bytes 5898240 | tf_op jit(solution)/shard_map/all_to_all | solution.py:892
  33.9 204.0 %all-gather.4.cloned.1.call-start = ((), (), s32[]{:S(2)}) async-start(), calls=%async_computation.5 | async-start | bytes 9830400 | tf_op jit(solution)/shard_map/all_gather | solution.py:970
  191.8 35.8 %all-to-all-start.1 = ((bf16[8,160,1024]{2,1,0:T(8,128)(2,1)}), bf16[8,160,1024]{2,1,0:T(8,128)(2,1)S(1)}, u32[]{:S(2)}, u32[]{:S(2)}) async-start(bf16[8,160,1024]{2,1,0:T(8,128)(2,1)} %bitcast.196), calls=%async_computation.1 | async-start | bytes 5242880 | tf_op jit(solution)/shard_map/all_to_all | solution.py:892
  195.4 476.9 %reduce-scatter.2.cloned.1.call-start = ((), (), s32[]{:S(2)}) async-start(), calls=%async_computation.6 | async-start | bytes 11796480 | tf_op jit(solution)/shard_map/reduce_scatter | solution.py:1028
  238.0 58.6 %collective-permute-start.15 = (bf16[256,4608]{1,0:T(8,128)(2,1)}, bf16[256,4608]{1,0:T(8,128)(2,1)}, u32[]{:S(2)}, u32[]{:S(2)}) collective-permute-start(bf16[256,4608]{1,0:T(8,128)(2,1)} %maximum_dynamic-update-slice_fusion.refs_1_), channel_id=1, source_target_pairs={{24,16},{16,8},{8,0},{25,17},{17,9},{9,1},{26,18},{18,10},{10,2},{... | collective-permute-start | bytes 7077896 | tf_op jit(solution)/shard_map/ppermute | solution.py:658
  239.3 57.3 %collective-permute-start.14 = (bf16[256,4608]{1,0:T(8,128)(2,1)}, bf16[256,4608]{1,0:T(8,128)(2,1)}, u32[]{:S(2)}, u32[]{:S(2)}) collective-permute-start(bf16[256,4608]{1,0:T(8,128)(2,1)} %maximum_dynamic-update-slice_fusion.refs_1_), channel_id=1, source_target_pairs={{0,8},{8,16},{16,24},{1,9},{9,17},{17,25},{2,10},{10,18},{18,26},{... | collective-permute-start | bytes 7077896 | tf_op jit(solution)/shard_map/ppermute | solution.py:658
  296.6 54.8 %collective-permute-start.16 = (bf16[256,4608]{1,0:T(8,128)(2,1)}, bf16[256,4608]{1,0:T(8,128)(2,1)S(1)}, u32[]{:S(2)}, u32[]{:S(2)}) collective-permute-start(bf16[256,4608]{1,0:T(8,128)(2,1)} %collective-permute-done.14.refs_2_), channel_id=1, source_target_pairs={{8,16},{16,24},{9,17},{17,25},{10,18},{18,26},{11,19},{19,27},{12,... | collective-permute-start | bytes 7077896 | tf_op jit(solution)/shard_map/ppermute | solution.py:658
  297.4 54.9 %collective-permute-start.17 = (bf16[256,4608]{1,0:T(8,128)(2,1)}, bf16[256,4608]{1,0:T(8,128)(2,1)S(1)}, u32[]{:S(2)}, u32[]{:S(2)}) collective-permute-start(bf16[256,4608]{1,0:T(8,128)(2,1)} %collective-permute-done.15.refs_3_), channel_id=1, source_target_pairs={{16,8},{8,0},{17,9},{9,1},{18,10},{10,2},{19,11},{11,3},{20,12},{1... | collective-permute-start | bytes 7077896 | tf_op jit(solution)/shard_map/ppermute | solution.py:658
  305.0 46.5 %collective-permute-start.18 = (bf16[256,3840]{1,0:T(8,128)(2,1)}, bf16[256,3840]{1,0:T(8,128)(2,1)}, u32[]{:S(2)}, u32[]{:S(2)}) collective-permute-start(bf16[256,3840]{1,0:T(8,128)(2,1)} %get-tuple-element.215), channel_id=1, source_target_pairs={{0,8},{1,9},{2,10},{3,11},{4,12},{5,13},{6,14},{7,15}} | collective-permute-start | bytes 5898248 | tf_op jit(solution)/shard_map/ppermute | solution.py:680
  352.3 53.4 %collective-permute-start.20 = (bf16[256,4608]{1,0:T(8,128)(2,1)S(1)}, bf16[256,4608]{1,0:T(8,128)(2,1)S(1)}, u32[]{:S(2)}, u32[]{:S(2)}) collective-permute-start(bf16[256,4608]{1,0:T(8,128)(2,1)S(1)} %collective-permute-done.16.refs_4_), channel_id=1, source_target_pairs={{16,24},{17,25},{18,26},{19,27},{20,28},{21,29},{22,30},{23,31}} | collective-permute-start | bytes 7077896 | tf_op jit(solution)/shard_map/ppermute | solution.py:658
  353.1 53.4 %collective-permute-start.21 = (bf16[256,4608]{1,0:T(8,128)(2,1)S(1)}, bf16[256,4608]{1,0:T(8,128)(2,1)S(1)}, u32[]{:S(2)}, u32[]{:S(2)}) collective-permute-start(bf16[256,4608]{1,0:T(8,128)(2,1)S(1)} %collective-permute-done.17.refs_5_), channel_id=1, source_target_pairs={{8,0},{9,1},{10,2},{11,3},{12,4},{13,5},{14,6},{15,7}} | collective-permute-start | bytes 7077896 | tf_op jit(solution)/shard_map/ppermute | solution.py:658
  360.2 45.5 %collective-permute-start.22 = (bf16[256,3840]{1,0:T(8,128)(2,1)S(1)}, bf16[256,3840]{1,0:T(8,128)(2,1)S(1)}, u32[]{:S(2)}, u32[]{:S(2)}) collective-permute-start(bf16[256,3840]{1,0:T(8,128)(2,1)S(1)} %get-tuple-element.213), channel_id=1, source_target_pairs={{0,8},{8,16},{1,9},{9,17},{2,10},{10,18},{3,11},{11,19},{4,12},{12... | collective-permute-start | bytes 5898248 | tf_op jit(solution)/shard_map/ppermute | solution.py:680
  407.9 46.9 %collective-permute-start.24 = (bf16[256,3840]{1,0:T(8,128)(2,1)S(1)}, bf16[256,3840]{1,0:T(8,128)(2,1)S(1)}, u32[]{:S(2)}, u32[]{:S(2)}) collective-permute-start(bf16[256,3840]{1,0:T(8,128)(2,1)S(1)} %get-tuple-element.128), channel_id=1, source_target_pairs={{0,8},{8,16},{16,24},{1,9},{9,17},{17,25},{2,10},{10,18},{18,26},{... | collective-permute-start | bytes 5898248 | tf_op jit(solution)/shard_map/ppermute | solution.py:680
  412.4 43.8 %collective-permute-start.25 = (bf16[256,3840]{1,0:T(8,128)(2,1)S(1)}, bf16[256,3840]{1,0:T(8,128)(2,1)}, u32[]{:S(2)}, u32[]{:S(2)}) collective-permute-start(bf16[256,3840]{1,0:T(8,128)(2,1)S(1)} %get-tuple-element.129), channel_id=1, source_target_pairs={{24,16},{16,8},{8,0},{25,17},{17,9},{9,1},{26,18},{18,10},{10,2},{... | collective-permute-start | bytes 5898248 | tf_op jit(solution)/shard_map/ppermute | solution.py:680
  476.3 37.0 %all-to-all-start.2 = ((bf16[8,160,1024]{2,1,0:T(8,128)(2,1)}), bf16[8,160,1024]{2,1,0:T(8,128)(2,1)}, u32[]{:S(2)}, u32[]{:S(2)}) async-start(bf16[8,160,1024]{2,1,0:T(8,128)(2,1)} %bitcast.195), calls=%async_computation.2 | async-start | bytes 5242880 | tf_op jit(solution)/shard_map/all_to_all | solution.py:892
  522.8 49.3 %all-to-all-start.3 = ((bf16[8,160,1024]{2,1,0:T(8,128)(2,1)}), bf16[8,160,1024]{2,1,0:T(8,128)(2,1)}, u32[]{:S(2)}, u32[]{:S(2)}) async-start(bf16[8,160,1024]{2,1,0:T(8,128)(2,1)} %bitcast.194), calls=%async_computation.3 | async-start | bytes 5242880 | tf_op jit(solution)/shard_map/all_to_all | solution.py:892
  605.4 28.3 %collective-permute-start.29 = (bf16[2,2,144,1024]{3,2,0,1:T(8,128)(2,1)S(1)}, bf16[2,2,144,1024]{3,2,0,1:T(8,128)(2,1)S(1)}, u32[]{:S(2)}, u32[]{:S(2)}) collective-permute-start(bf16[2,2,144,1024]{3,2,0,1:T(8,128)(2,1)S(1)} %select_bitcast_fusion), channel_id=1, source_target_pairs={{0,4},{1,5},{2,6},{3,7},{4,0},{5,1},{6,2},{7,3},{8,12},{9,13},{10,... | collective-permute-start | bytes 3538952 | tf_op jit(solution)/shard_map/ppermute | solution.py:689
  607.7 28.6 %collective-permute-start.27 = (bf16[2,2,144,1024]{3,2,0,1:T(8,128)(2,1)S(1)}, bf16[2,2,144,1024]{3,2,0,1:T(8,128)(2,1)S(1)}, u32[]{:S(2)}, u32[]{:S(2)}) collective-permute-start(bf16[2,2,144,1024]{3,2,0,1:T(8,128)(2,1)S(1)} %select_bitcast_fusion.1), channel_id=1, source_target_pairs={{0,2},{1,3},{2,0},{3,1},{4,6},{5,7},{6,4},{7,5},{8,10},{9,11},{10,... | collective-permute-start | bytes 3538952 | tf_op jit(solution)/shard_map/ppermute | solution.py:689
  609.3 51.1 %collective-permute-start.31 = (bf16[512,1024]{1,0:T(8,128)(2,1)S(1)}, bf16[512,1024]{1,0:T(8,128)(2,1)S(1)}, u32[]{:S(2)}, u32[]{:S(2)}) collective-permute-start(bf16[512,1024]{1,0:T(8,128)(2,1)S(1)} %slice.294), channel_id=1, source_target_pairs={{8,0},{16,8},{24,16},{9,1},{17,9},{25,17},{10,2},{18,10},{26,18},{... | collective-permute-start | bytes 3145736 | tf_op jit(solution)/shard_map/ppermute | solution.py:30
  668.1 27.1 %collective-permute-start.32 = (bf16[512,1024]{1,0:T(8,128)(2,1)}, bf16[512,1024]{1,0:T(8,128)(2,1)}, u32[]{:S(2)}, u32[]{:S(2)}) collective-permute-start(bf16[512,1024]{1,0:T(8,128)(2,1)} %add_convert_fusion.1), channel_id=1, source_target_pairs={{8,0},{16,8},{24,16},{9,1},{17,9},{25,17},{10,2},{18,10},{26,18},{... | collective-permute-start | bytes 3145736 | tf_op jit(solution)/shard_map/ppermute | solution.py:30
  (75 other events, 807.7 us)
Sparse Core Ops, SparseCore 0:
  18.2 60.9 all-gather.5
  96.6 141.3 all-gather.3
  476.4 183.1 reduce-scatter.1

commit v6 on v5

--- a/solution.py
+++ b/solution.py
@@ -1075,7 +1075,7 @@
     for hop in range(1, ctx_count):
         sent = scatter_add(parts, hop, *sent)
         sent = scatter_hop(*sent, hop)
-        if hop == 1:
+        if hop == min(2, ctx_count - 1):
             *sent, grad_gate, grad_up, grad_down = together(*sent, *expert_grads)
     sums = scatter_end(parts, *sent)
     _, own_pull = jax.vjp(norm_rows, inputs, full_gain_attn)

time: 730 us -> 740 us (1.014)
  starting transfers between devices: 105 us -> 119 us
    ppermute x12, starting transfers between devices: 35.6 us -> 49.4 us  [scatter_hop(): return (lax.ppermute(up, 'ctx', route), lax.ppermute(down, 'ctx', back))]
    unnamed x118 -> x120, local copies, waits for them, and re-layouts: 19 us -> 19.3 us
  transfers between devices with their start and end apart: 46 -> 46, of which waited for: 26 -> 25; matrix products, arithmetic and copies ran while one was open for 19% -> 18% of each run, Pallas kernels for 29% -> 29%
where the time goes in v6:
time: 740 us; the launch traced here: 732 us
  Pallas kernels  233 us (31%)
  waiting for transfers between devices  220 us (30%)
  starting transfers between devices  119 us (16%)
  other arithmetic  59.9 us (8%)
  local copies, waits for them, and re-layouts  49.7 us (7%)
  matrix products  35.2 us (5%)
  between operations  15.2 us (2%)
    pallas_call x2, Pallas kernels, run_expert(): pl.pallas_call(functools.partial(expert_kernel, first, last, units, count...  73.7 us
    ppermute x12, waiting for transfers between devices, scatter_hop(): return (lax.ppermute(up, 'ctx', route), lax.ppermute(down, 'ctx', back))  71.4 us
    ppermute x11, waiting for transfers between devices, swap_exp(): lax.ppermute(block, 'exp', [(i, i ^ bit) for i in range(lax.axis_size('ex...  57.5 us
    ppermute x12, starting transfers between devices, scatter_hop(): return (lax.ppermute(up, 'ctx', route), lax.ppermute(down, 'ctx', back))  49.4 us
    all_to_all x4, waiting for transfers between devices, exchange(): lax.all_to_all(blocks, 'exp', split_axis=0, concat_axis=0, tiled=True)  45.1 us
    pallas_call x2, Pallas kernels, expert_weights(): pl.pallas_call(functools.partial(expert_weights_kernel, units, count), gr...  37.4 us
    ppermute x10, waiting for transfers between devices, shift_ctx(): return lax.ppermute(block, 'ctx', route)  34.2 us
    pallas_call x1, Pallas kernels, attend(): pl.pallas_call(attend_kernel, grid=(pairs,), in_specs=[pl.BlockSpec((rows...  28.9 us
  transfers between devices with their start and end apart: 46, of which 25 were waited for; matrix products, arithmetic and copies ran while one was open for 18% of the time, Pallas kernels for 29%

profile of v6, /device:TPU:0, one launch (start us, length us, event | category | flops | bytes accessed | tf_op | source)
XLA Modules:
  0.0 732.0 jit_solution(14340518196887996825)
XLA Ops:
  80.4 8.3 %collective-permute-done.8 = bf16[1,2,128,1024]{3,2,1,0:T(8,128)(2,1)S(1)} collective-permute-done((bf16[1,2,128,1024]{3,2,1,0:T(8,128)(2,1)S(1)}, bf16[1,2,128,1024]{3,2,1,0:T(8,128)(2,1)S(1)}, u32[]{:S(2)}, u32[]{:S(2)}) %collective-permute-start.8) | collective-permute-done | bytes 524320 | tf_op jit(solution)/shard_map/ppermute | solution.py:689
  106.7 7.3 bias_band.1.band_ref
  114.0 8.6 %collective-permute-done.11 = bf16[2,2,128,1024]{3,2,1,0:T(8,128)(2,1)S(1)} collective-permute-done((bf16[2,2,128,1024]{3,2,1,0:T(8,128)(2,1)}, bf16[2,2,128,1024]{3,2,1,0:T(8,128)(2,1)S(1)}, u32[]{:S(2)}, u32[]{:S(2)}) %collective-permute-start.11) | collective-permute-done | bytes 1048608 | tf_op jit(solution)/shard_map/ppermute | solution.py:689
  157.1 28.9 %attend.1 = (bf16[512,1024]{1,0:T(8,128)(2,1)}, f32[8,2,512]{2,1,0:T(2,128)}) custom-call(bf16[512,1024]{1,0:T(8,128)(2,1)} %fusion.21.q_ref, bf16[1536,1024]{1,0:T(8,128)(2,1)} %convolution_convert_fusion.3.k_ref, bf16[1536,1024]{1,0:T(8,128)(2,1)} %convolution_convert_fusion.2.v_ref, bf16[512,128]{1,0:T(8,128)(2,1)} %compare_convert_fusion.qdoc_ref, ...), custom_call_target="tpu_custom_call" | custom-call | flops 1048576 | bytes 1048576 | tf_op jit(solution)/shard_map/attend/pallas_call | solution.py:169
  209.2 18.4 %all-to-all-done.1 = bf16[8,160,1024]{2,1,0:T(8,128)(2,1)S(1)} async-done(((bf16[8,160,1024]{2,1,0:T(8,128)(2,1)}), bf16[8,160,1024]{2,1,0:T(8,128)(2,1)S(1)}, u32[]{:S(2)}, u32[]{:S(2)}) %all-to-all-start.1) | async-done | bytes 2621472 | tf_op jit(solution)/shard_map/all_to_all | solution.py:892
  227.6 10.3 %all-gather.4.cloned.1.call-done.refs_1_ = bf16[1024,3840]{1,0:T(8,128)(2,1)} async-done(((bf16[256,3840]{1,0:T(8,128)(2,1)}), bf16[1024,3840]{1,0:T(8,128)(2,1)}) %all-gather.4.cloned.1.call-update) | async-done | bytes 7864336 | tf_op jit(solution)/shard_map/all_gather | solution.py:970
  246.5 32.7 %expert.2 = (bf16[1280,1280]{1,0:T(8,128)(2,1)}, bf16[1280,2560]{1,0:T(8,128)(2,1)}, bf16[1280,1024]{1,0:T(8,128)(2,1)}, f32[1280,128]{1,0:T(8,128)}, f32[1280,1024]{1,0:T(8,128)}, /*index=5*/f32[1280,1024]{1,0:T(8,128)}) custom-call(bf16[1280,1024]{1,0:T(8,128)(2,1)} %bitcast.166, bf16[1024,3840]{1,0:T(8,128)(2,1)} %all-gather.4.cloned.1.call-done.refs_1_, ...), custom_call_target="tpu_custom_call" | custom-call | flops 1048576 | bytes 1048576 | tf_op jit(solution)/shard_map/expert/pallas_call | solution.py:484
  279.1 17.4 %expert_weights.2 = bf16[1024,3840]{1,0:T(8,128)(2,1)} custom-call(bf16[1280,1024]{1,0:T(8,128)(2,1)} %bitcast.167, bf16[1280,1024]{1,0:T(8,128)(2,1)} %get-tuple-element.132.low_ref.refs_11_, bf16[1280,2560]{1,0:T(8,128)(2,1)} %get-tuple-element.105.dboth_ref, bf16[1280,1280]{1,0:T(8,128)(2,1)} %get-tuple-element.106.hidden_ref), custom_call_target="tpu_custom_call" | custom-call | flops 1048576 | bytes 1048576 | tf_op jit(solution)/shard_map/expert_weights/pallas_call | solution.py:561
  311.1 16.9 %probs.1.probs_ref = bf16[16,2,1280,256]{3,2,1,0:T(8,128)(2,1)} custom-call(bf16[512,1024]{1,0:T(8,128)(2,1)} %fusion.21.q_ref, bf16[1536,1024]{1,0:T(8,128)(2,1)} %convolution_convert_fusion.3.k_ref, bf16[512,128]{1,0:T(8,128)(2,1)} %compare_convert_fusion.qdoc_ref, bf16[1536,128]{1,0:T(8,128)(2,1)} %select_convert_fusion.kdoc_ref, ...), custom_call_target="tpu_custom_call" | custom-call | flops 1048576 | bytes 1048576 | tf_op jit(solution)/shard_map/probs/pallas_call | solution.py:214
  328.1 23.3 %collective-permute-done.18 = bf16[256,3840]{1,0:T(8,128)(2,1)} collective-permute-done((bf16[256,3840]{1,0:T(8,128)(2,1)}, bf16[256,3840]{1,0:T(8,128)(2,1)}, u32[]{:S(2)}, u32[]{:S(2)}) %collective-permute-start.18) | collective-permute-done | bytes 1966112 | tf_op jit(solution)/shard_map/ppermute | solution.py:680
  365.5 40.1 %collective-permute-done.22 = bf16[256,3840]{1,0:T(8,128)(2,1)S(1)} collective-permute-done((bf16[256,3840]{1,0:T(8,128)(2,1)S(1)}, bf16[256,3840]{1,0:T(8,128)(2,1)S(1)}, u32[]{:S(2)}, u32[]{:S(2)}) %collective-permute-start.22) | collective-permute-done | bytes 1966112 | tf_op jit(solution)/shard_map/ppermute | solution.py:680
  413.6 41.1 %expert.3 = (bf16[1280,1536]{1,0:T(8,128)(2,1)}, bf16[1280,3072]{1,0:T(8,128)(2,1)}, bf16[1280,1024]{1,0:T(8,128)(2,1)}, bf16[1280,1024]{1,0:T(8,128)(2,1)}, f32[1024,128]{1,0:T(8,128)}) custom-call(bf16[1280,1024]{1,0:T(8,128)(2,1)} %bitcast.168, bf16[256,4608]{1,0:T(8,128)(2,1)} %maximum_dynamic-update-slice_fusion.refs_1_, ...), custom_call_target="tpu_custom_call" | custom-call | flops 1048576 | bytes 1048576 | tf_op jit(solution)/shard_map/expert/pallas_call | solution.py:484
  456.1 20.0 %expert_weights.3 = bf16[1024,4608]{1,0:T(8,128)(2,1)} custom-call(bf16[1280,1024]{1,0:T(8,128)(2,1)} %bitcast.169, bf16[1280,1024]{1,0:T(8,128)(2,1)} %get-tuple-element.132.low_ref.refs_11_, bf16[1280,3072]{1,0:T(8,128)(2,1)} %get-tuple-element.133.dboth_ref, bf16[1280,1536]{1,0:T(8,128)(2,1)} %get-tuple-element.134.hidden_ref), custom_call_target="tpu_custom_call" | custom-call | flops 12079595520 | bytes 1048576 | tf_op jit(solution)/shard_map/expert_weights/pallas_call | solution.py:561
  487.6 25.6 %all-to-all-done.2 = bf16[8,160,1024]{2,1,0:T(8,128)(2,1)} async-done(((bf16[8,160,1024]{2,1,0:T(8,128)(2,1)}), bf16[8,160,1024]{2,1,0:T(8,128)(2,1)}, u32[]{:S(2)}, u32[]{:S(2)}) %all-to-all-start.2) | async-done | bytes 2621472 | tf_op jit(solution)/shard_map/all_to_all | solution.py:892
  527.2 25.7 %attend_back.1 = (bf16[512,1024]{1,0:T(8,128)(2,1)}, bf16[1536,1024]{1,0:T(8,128)(2,1)}, bf16[1536,1024]{1,0:T(8,128)(2,1)}, f32[8,2,1024]{2,1,0:T(2,128)}) custom-call(bf16[512,1024]{1,0:T(8,128)(2,1)} %fusion.21.q_ref, bf16[1536,1024]{1,0:T(8,128)(2,1)} %convolution_convert_fusion.3.k_ref, bf16[1536,1024]{1,0:T(8,128)(2,1)} %convolution_convert_fusion.2.v_ref, ...), custom_call_target="tpu_custom_call" | custom-call | flops 21474836480 | bytes 1048576 | tf_op jit(solution)/shard_map/attend_back/pallas_call | solution.py:282
  554.0 15.9 %normed_grad.1 = (bf16[1024,1024]{1,0:T(8,128)(2,1)}, f32[512,1024]{1,0:T(8,128)}, f32[8,1024]{1,0:T(8,128)}) custom-call(bf16[1536,1024]{1,0:T(8,128)(2,1)} %copy-done.3, bf16[512,1024]{1,0:T(8,128)(2,1)} %get-tuple-element.140.q_ref, bf16[1536,1024]{1,0:T(8,128)(2,1)} %get-tuple-element.141.k_ref, bf16[1536,1024]{1,0:T(8,128)(2,1)} %get-tuple-element.142.v_ref, ...), custom_call_target="tpu_custom_call" | custom-call | flops 1048576 | bytes 1048576 | tf_op jit(solution)/shard_map/normed_grad/pallas_call | solution.py:800
  572.0 19.1 %slabs.1 = (bf16[16,144,1024]{2,1,0:T(8,128)(2,1)}, bf16[16,144,1024]{2,1,0:T(8,128)(2,1)}) custom-call(bf16[1536,1024]{1,0:T(8,128)(2,1)} %copy-done.5, bf16[512,1024]{1,0:T(8,128)(2,1)} %get-tuple-element.140.q_ref, bf16[1536,1024]{1,0:T(8,128)(2,1)} %get-tuple-element.141.k_ref, bf16[1536,1024]{1,0:T(8,128)(2,1)} %get-tuple-element.142.v_ref, ...), custom_call_target="tpu_custom_call" | custom-call | flops 1048576 | bytes 1048576 | tf_op jit(solution)/shard_map/slabs/pallas_call | solution.py:866
  591.8 7.7 %collective-permute-done.26 = bf16[16,144,1024]{2,1,0:T(8,128)(2,1)S(1)} collective-permute-done((bf16[16,144,1024]{2,1,0:T(8,128)(2,1)}, bf16[16,144,1024]{2,1,0:T(8,128)(2,1)S(1)}, u32[]{:S(2)}, u32[]{:S(2)}) %collective-permute-start.26) | collective-permute-done | bytes 4718624 | tf_op jit(solution)/shard_map/ppermute | solution.py:689
  610.6 23.1 %collective-permute-done.29 = bf16[2,2,144,1024]{3,2,0,1:T(8,128)(2,1)S(1)} collective-permute-done((bf16[2,2,144,1024]{3,2,0,1:T(8,128)(2,1)S(1)}, bf16[2,2,144,1024]{3,2,0,1:T(8,128)(2,1)S(1)}, u32[]{:S(2)}, u32[]{:S(2)}) %collective-permute-start.29) | collective-permute-done | bytes 1179680 | tf_op jit(solution)/shard_map/ppermute | solution.py:689
  643.0 6.5 collective-permute-done.30
  652.1 8.3 %collective-permute-done.31 = bf16[512,1024]{1,0:T(8,128)(2,1)S(1)} collective-permute-done((bf16[512,1024]{1,0:T(8,128)(2,1)S(1)}, bf16[512,1024]{1,0:T(8,128)(2,1)S(1)}, u32[]{:S(2)}, u32[]{:S(2)}) %collective-permute-start.31) | collective-permute-done | bytes 1048608 | tf_op jit(solution)/shard_map/ppermute | solution.py:30
  681.3 6.4 collective-permute-done.32
  688.8 7.6 %expert_sums.1 = (f32[256,2816]{1,0:T(8,128)}, f32[256,2816]{1,0:T(8,128)}, f32[704,1024]{1,0:T(8,128)}) custom-call(bf16[256,3840]{1,0:T(8,128)(2,1)} %dynamic-slice_bitcast_fusion.own_ref, bf16[256,3840]{1,0:T(8,128)(2,1)} %copy-done.35, bf16[256,3840]{1,0:T(8,128)(2,1)} %collective-permute-done.25.down_ref, ...), custom_call_target="tpu_custom_call" | custom-call | flops 1048576 | bytes 1048576 | tf_op jit(solution)/shard_map/expert_sums/pallas_call | solution.py:615
  697.7 16.0 %collective-permute-start.37 = (bf16[144,1024]{1,0:T(8,128)(2,1)S(1)}, bf16[144,1024]{1,0:T(8,128)(2,1)S(1)}, u32[]{:S(2)}, u32[]{:S(2)}) collective-permute-start(bf16[144,1024]{1,0:T(8,128)(2,1)S(1)} %get-tuple-element.242), channel_id=1, source_target_pairs={{0,8},{8,16},{16,24},{1,9},{9,17},{17,25},{2,10},{10,18},{18,26},{... | collective-permute-start | bytes 884744 | tf_op jit(solution)/shard_map/ppermute | solution.py:680
  (325 shorter events, 281.6 us)
Async XLA Ops:
  7.2 97.4 %all-gather.6.cloned.1.call-start = ((), (), s32[]{:S(2)}) async-start(), calls=%async_computation.7 | async-start | bytes 1081344 | tf_op jit(solution)/shard_map/all_gather | solution.py:951
  8.9 37.1 %collective-permute-start = (bf16[1,128,1024]{2,1,0:T(8,128)(2,1)}, bf16[1,128,1024]{2,1,0:T(8,128)(2,1)}, u32[]{:S(2)}, u32[]{:S(2)}) collective-permute-start(bf16[1,128,1024]{2,1,0:T(8,128)(2,1)} %maximum_bitcast_fusion.2), channel_id=1, source_target_pairs={{0,8},{8,16},{16,24},{1,9},{9,17},{17,25},{2,10},{10,18},{18,26},{... | collective-permute-start | bytes 786440 | tf_op jit(solution)/shard_map/ppermute | solution.py:30
  14.5 33.3 %collective-permute-start.1 = (bf16[1,128,1024]{2,1,0:T(8,128)(2,1)}, bf16[1,128,1024]{2,1,0:T(8,128)(2,1)}, u32[]{:S(2)}, u32[]{:S(2)}) collective-permute-start(bf16[1,128,1024]{2,1,0:T(8,128)(2,1)} %maximum_bitcast_fusion.2), channel_id=1, source_target_pairs={{8,0},{16,8},{24,16},{9,1},{17,9},{25,17},{10,2},{18,10},{26,18},{... | collective-permute-start | bytes 786440 | tf_op jit(solution)/shard_map/ppermute | solution.py:30
  18.1 53.3 %collective-permute-start.6 = (bf16[512,1024]{1,0:T(8,128)(2,1)}, bf16[512,1024]{1,0:T(8,128)(2,1)}, u32[]{:S(2)}, u32[]{:S(2)}) collective-permute-start(bf16[512,1024]{1,0:T(8,128)(2,1)} %bitcast.174), channel_id=1, source_target_pairs={{0,8},{8,16},{16,24},{1,9},{9,17},{17,25},{2,10},{10,18},{18,26},{... | collective-permute-start | bytes 3145736 | tf_op jit(solution)/shard_map/ppermute | solution.py:30
  30.2 42.3 %all-to-all-start = ((bf16[8,160,1152]{2,1,0:T(8,128)(2,1)}), bf16[8,160,1152]{2,1,0:T(8,128)(2,1)S(1)}, u32[]{:S(2)}, u32[]{:S(2)}) async-start(bf16[8,160,1152]{2,1,0:T(8,128)(2,1)} %bitcast.193), calls=%async_computation | async-start | bytes 5898240 | tf_op jit(solution)/shard_map/all_to_all | solution.py:892
  33.9 204.0 %all-gather.4.cloned.1.call-start = ((), (), s32[]{:S(2)}) async-start(), calls=%async_computation.5 | async-start | bytes 9830400 | tf_op jit(solution)/shard_map/all_gather | solution.py:970
  191.8 35.8 %all-to-all-start.1 = ((bf16[8,160,1024]{2,1,0:T(8,128)(2,1)}), bf16[8,160,1024]{2,1,0:T(8,128)(2,1)S(1)}, u32[]{:S(2)}, u32[]{:S(2)}) async-start(bf16[8,160,1024]{2,1,0:T(8,128)(2,1)} %bitcast.196), calls=%async_computation.1 | async-start | bytes 5242880 | tf_op jit(solution)/shard_map/all_to_all | solution.py:892
  195.4 493.3 %reduce-scatter.2.cloned.1.call-start = ((), (), s32[]{:S(2)}) async-start(), calls=%async_computation.6 | async-start | bytes 11796480 | tf_op jit(solution)/shard_map/reduce_scatter | solution.py:1028
  238.0 58.6 %collective-permute-start.15 = (bf16[256,4608]{1,0:T(8,128)(2,1)}, bf16[256,4608]{1,0:T(8,128)(2,1)}, u32[]{:S(2)}, u32[]{:S(2)}) collective-permute-start(bf16[256,4608]{1,0:T(8,128)(2,1)} %maximum_dynamic-update-slice_fusion.refs_1_), channel_id=1, source_target_pairs={{24,16},{16,8},{8,0},{25,17},{17,9},{9,1},{26,18},{18,10},{10,2},{... | collective-permute-start | bytes 7077896 | tf_op jit(solution)/shard_map/ppermute | solution.py:658
  239.2 57.3 %collective-permute-start.14 = (bf16[256,4608]{1,0:T(8,128)(2,1)}, bf16[256,4608]{1,0:T(8,128)(2,1)}, u32[]{:S(2)}, u32[]{:S(2)}) collective-permute-start(bf16[256,4608]{1,0:T(8,128)(2,1)} %maximum_dynamic-update-slice_fusion.refs_1_), channel_id=1, source_target_pairs={{0,8},{8,16},{16,24},{1,9},{9,17},{17,25},{2,10},{10,18},{18,26},{... | collective-permute-start | bytes 7077896 | tf_op jit(solution)/shard_map/ppermute | solution.py:658
  296.5 54.8 %collective-permute-start.16 = (bf16[256,4608]{1,0:T(8,128)(2,1)}, bf16[256,4608]{1,0:T(8,128)(2,1)S(1)}, u32[]{:S(2)}, u32[]{:S(2)}) collective-permute-start(bf16[256,4608]{1,0:T(8,128)(2,1)} %collective-permute-done.14.refs_2_), channel_id=1, source_target_pairs={{8,16},{16,24},{9,17},{17,25},{10,18},{18,26},{11,19},{19,27},{12,... | collective-permute-start | bytes 7077896 | tf_op jit(solution)/shard_map/ppermute | solution.py:658
  297.4 54.9 %collective-permute-start.17 = (bf16[256,4608]{1,0:T(8,128)(2,1)}, bf16[256,4608]{1,0:T(8,128)(2,1)S(1)}, u32[]{:S(2)}, u32[]{:S(2)}) collective-permute-start(bf16[256,4608]{1,0:T(8,128)(2,1)} %collective-permute-done.15.refs_3_), channel_id=1, source_target_pairs={{16,8},{8,0},{17,9},{9,1},{18,10},{10,2},{19,11},{11,3},{20,12},{1... | collective-permute-start | bytes 7077896 | tf_op jit(solution)/shard_map/ppermute | solution.py:658
  304.9 46.4 %collective-permute-start.18 = (bf16[256,3840]{1,0:T(8,128)(2,1)}, bf16[256,3840]{1,0:T(8,128)(2,1)}, u32[]{:S(2)}, u32[]{:S(2)}) collective-permute-start(bf16[256,3840]{1,0:T(8,128)(2,1)} %get-tuple-element.215), channel_id=1, source_target_pairs={{0,8},{1,9},{2,10},{3,11},{4,12},{5,13},{6,14},{7,15}} | collective-permute-start | bytes 5898248 | tf_op jit(solution)/shard_map/ppermute | solution.py:680
  352.2 53.4 %collective-permute-start.20 = (bf16[256,4608]{1,0:T(8,128)(2,1)S(1)}, bf16[256,4608]{1,0:T(8,128)(2,1)S(1)}, u32[]{:S(2)}, u32[]{:S(2)}) collective-permute-start(bf16[256,4608]{1,0:T(8,128)(2,1)S(1)} %collective-permute-done.16.refs_4_), channel_id=1, source_target_pairs={{16,24},{17,25},{18,26},{19,27},{20,28},{21,29},{22,30},{23,31}} | collective-permute-start | bytes 7077896 | tf_op jit(solution)/shard_map/ppermute | solution.py:658
  353.0 53.4 %collective-permute-start.21 = (bf16[256,4608]{1,0:T(8,128)(2,1)S(1)}, bf16[256,4608]{1,0:T(8,128)(2,1)S(1)}, u32[]{:S(2)}, u32[]{:S(2)}) collective-permute-start(bf16[256,4608]{1,0:T(8,128)(2,1)S(1)} %collective-permute-done.17.refs_5_), channel_id=1, source_target_pairs={{8,0},{9,1},{10,2},{11,3},{12,4},{13,5},{14,6},{15,7}} | collective-permute-start | bytes 7077896 | tf_op jit(solution)/shard_map/ppermute | solution.py:658
  360.1 45.5 %collective-permute-start.22 = (bf16[256,3840]{1,0:T(8,128)(2,1)S(1)}, bf16[256,3840]{1,0:T(8,128)(2,1)S(1)}, u32[]{:S(2)}, u32[]{:S(2)}) collective-permute-start(bf16[256,3840]{1,0:T(8,128)(2,1)S(1)} %get-tuple-element.213), channel_id=1, source_target_pairs={{0,8},{8,16},{1,9},{9,17},{2,10},{10,18},{3,11},{11,19},{4,12},{12... | collective-permute-start | bytes 5898248 | tf_op jit(solution)/shard_map/ppermute | solution.py:680
  407.8 46.9 %collective-permute-start.24 = (bf16[256,3840]{1,0:T(8,128)(2,1)S(1)}, bf16[256,3840]{1,0:T(8,128)(2,1)S(1)}, u32[]{:S(2)}, u32[]{:S(2)}) collective-permute-start(bf16[256,3840]{1,0:T(8,128)(2,1)S(1)} %get-tuple-element.128), channel_id=1, source_target_pairs={{0,8},{8,16},{16,24},{1,9},{9,17},{17,25},{2,10},{10,18},{18,26},{... | collective-permute-start | bytes 5898248 | tf_op jit(solution)/shard_map/ppermute | solution.py:680
  412.3 43.8 %collective-permute-start.25 = (bf16[256,3840]{1,0:T(8,128)(2,1)S(1)}, bf16[256,3840]{1,0:T(8,128)(2,1)}, u32[]{:S(2)}, u32[]{:S(2)}) collective-permute-start(bf16[256,3840]{1,0:T(8,128)(2,1)S(1)} %get-tuple-element.129), channel_id=1, source_target_pairs={{24,16},{16,8},{8,0},{25,17},{17,9},{9,1},{26,18},{18,10},{10,2},{... | collective-permute-start | bytes 5898248 | tf_op jit(solution)/shard_map/ppermute | solution.py:680
  476.2 37.0 %all-to-all-start.2 = ((bf16[8,160,1024]{2,1,0:T(8,128)(2,1)}), bf16[8,160,1024]{2,1,0:T(8,128)(2,1)}, u32[]{:S(2)}, u32[]{:S(2)}) async-start(bf16[8,160,1024]{2,1,0:T(8,128)(2,1)} %bitcast.195), calls=%async_computation.2 | async-start | bytes 5242880 | tf_op jit(solution)/shard_map/all_to_all | solution.py:892
  522.8 49.3 %all-to-all-start.3 = ((bf16[8,160,1024]{2,1,0:T(8,128)(2,1)}), bf16[8,160,1024]{2,1,0:T(8,128)(2,1)}, u32[]{:S(2)}, u32[]{:S(2)}) async-start(bf16[8,160,1024]{2,1,0:T(8,128)(2,1)} %bitcast.194), calls=%async_computation.3 | async-start | bytes 5242880 | tf_op jit(solution)/shard_map/all_to_all | solution.py:892
  605.4 28.3 %collective-permute-start.29 = (bf16[2,2,144,1024]{3,2,0,1:T(8,128)(2,1)S(1)}, bf16[2,2,144,1024]{3,2,0,1:T(8,128)(2,1)S(1)}, u32[]{:S(2)}, u32[]{:S(2)}) collective-permute-start(bf16[2,2,144,1024]{3,2,0,1:T(8,128)(2,1)S(1)} %select_bitcast_fusion), channel_id=1, source_target_pairs={{0,4},{1,5},{2,6},{3,7},{4,0},{5,1},{6,2},{7,3},{8,12},{9,13},{10,... | collective-permute-start | bytes 3538952 | tf_op jit(solution)/shard_map/ppermute | solution.py:689
  607.7 28.6 %collective-permute-start.27 = (bf16[2,2,144,1024]{3,2,0,1:T(8,128)(2,1)S(1)}, bf16[2,2,144,1024]{3,2,0,1:T(8,128)(2,1)S(1)}, u32[]{:S(2)}, u32[]{:S(2)}) collective-permute-start(bf16[2,2,144,1024]{3,2,0,1:T(8,128)(2,1)S(1)} %select_bitcast_fusion.1), channel_id=1, source_target_pairs={{0,2},{1,3},{2,0},{3,1},{4,6},{5,7},{6,4},{7,5},{8,10},{9,11},{10,... | collective-permute-start | bytes 3538952 | tf_op jit(solution)/shard_map/ppermute | solution.py:689
  609.3 51.0 %collective-permute-start.31 = (bf16[512,1024]{1,0:T(8,128)(2,1)S(1)}, bf16[512,1024]{1,0:T(8,128)(2,1)S(1)}, u32[]{:S(2)}, u32[]{:S(2)}) collective-permute-start(bf16[512,1024]{1,0:T(8,128)(2,1)S(1)} %slice.294), channel_id=1, source_target_pairs={{8,0},{16,8},{24,16},{9,1},{17,9},{25,17},{10,2},{18,10},{26,18},{... | collective-permute-start | bytes 3145736 | tf_op jit(solution)/shard_map/ppermute | solution.py:30
  660.8 26.9 %collective-permute-start.32 = (bf16[512,1024]{1,0:T(8,128)(2,1)S(1)}, bf16[512,1024]{1,0:T(8,128)(2,1)S(1)}, u32[]{:S(2)}, u32[]{:S(2)}) collective-permute-start(bf16[512,1024]{1,0:T(8,128)(2,1)S(1)} %add_convert_fusion.1), channel_id=1, source_target_pairs={{8,0},{16,8},{24,16},{9,1},{17,9},{25,17},{10,2},{18,10},{26,18},{... | collective-permute-start | bytes 3145736 | tf_op jit(solution)/shard_map/ppermute | solution.py:30
  (76 other events, 877.8 us)
Sparse Core Ops, SparseCore 0:
  18.2 60.9 all-gather.5
  96.6 141.3 all-gather.3
  476.3 183.1 reduce-scatter.1

commit v7 on v4

--- a/solution.py
+++ b/solution.py
@@ -1005,6 +1005,7 @@
     grad0 = expert_weights(units0, ctx_count, arrived, carried[0], dboth, hidden)
     pieces, sent = [packed[1]], (None, None)
     probs = make_probs(queries, keys, query_doc, key_doc, band, lse)
+    own0 = lax.dynamic_index_in_dim(grad0.reshape(ctx_count, held, -1), ctx_index, 0, keepdims=False)
     for hop in range(1, ctx_count):
         if hop == 1:
             up, down, grad0 = together(up, down, grad0)
@@ -1012,7 +1013,7 @@
         else:
             up, down = gather_hop(up, down, hop)
             sent = scatter_hop(*scatter_add(parts0, hop - 1, *sent), hop - 1)
-            up, down, probs, *sent = together(up, down, probs, *sent)
+            up, down, probs, own0, *sent = together(up, down, probs, own0, *sent)
         pieces += [up, down]
     arrived, *sent = together(arrived, *scatter_add(parts0, ctx_count - 1, *sent))
     sent = scatter_hop(*sent, ctx_count - 1)
@@ -1032,11 +1033,11 @@
     middle_grad = upstream + middle_norm_grad
     branch_grad = middle_grad.astype(BF16)
     attended_grad = dot_last(branch_grad, full_out).astype(BF16)
-    made, attended_grad = together(made, attended_grad)
-    made = exchange(made.reshape(experts, capacity, width)).reshape(-1, width)
     query_grad, key_grad, value_grad, dist_grad = attend_back(
         queries, keys, values, attended_grad, attended, probs
     )
+    made, query_grad = together(made, query_grad)
+    made = exchange(made.reshape(experts, capacity, width)).reshape(-1, width)
     bias_grad = jnp.dot(
         dist_grad.reshape(HEADS, WINDOW), onehot_bucket.T.astype(F32), precision=lax.Precision.HIGHEST
     )
@@ -1056,7 +1057,6 @@
         axis=1,
     ).astype(BF16)
     tail = jnp.pad(tail[:, None, :], ((0, 0), (0, 15), (0, width - tail.shape[1])))
-    query_grad, made = together(query_grad, made)
     output = (middle + dot_rows(routes, made)).astype(BF16)
     keep, send = make_slabs(normed_all, query_grad, key_grad, value_grad, attended, branch_grad, tail)
     other = swap_exp(send, 1)
@@ -1064,9 +1064,8 @@
     pieces = [halo_grad[place * rows : (place + 1) * rows] for place in range(reach)]
     returning = shift_ctx(pieces[0], -1)
     for piece in pieces[1:]:
-        parts, returning = together(parts, returning)
+        parts, returning, output = together(parts, returning, output)
         returning = shift_ctx((piece.astype(F32) + returning.astype(F32)).astype(BF16), -1)
-    own0 = lax.dynamic_index_in_dim(parts0, ctx_index, 0, keepdims=False)
     expert_grads = expert_sums(sizes, ctx_count, own0, *sent, total1)
     sent = (None, None)
     for hop in range(1, ctx_count):

time: 728 us -> 736 us (1.011)
    ppermute x11, waiting for transfers between devices: 61.8 us -> 71.8 us  [swap_exp(): lax.ppermute(block, 'exp', [(i, i ^ bit) for i in range(lax.axis_size('ex...]
    ppermute x10, waiting for transfers between devices: 32.6 us -> 23.9 us  [shift_ctx(): return lax.ppermute(block, 'ctx', route)]
    unnamed x118 -> x124, local copies, waits for them, and re-layouts: 19 us -> 20.9 us
  transfers between devices with their start and end apart: 46 -> 46, of which waited for: 25 -> 25; matrix products, arithmetic and copies ran while one was open for 19% -> 19% of each run, Pallas kernels for 30% -> 29%
where the time goes in v7:
time: 736 us; the launch traced here: 728 us
  Pallas kernels  233 us (32%)
  waiting for transfers between devices  227 us (31%)
  starting transfers between devices  99 us (13%)
  other arithmetic  65.6 us (9%)
  local copies, waits for them, and re-layouts  52.6 us (7%)
  matrix products  35.8 us (5%)
  between operations  15.1 us (2%)
    pallas_call x2, Pallas kernels, run_expert(): pl.pallas_call(functools.partial(expert_kernel, first, last, units, count...  73.9 us
    ppermute x12, waiting for transfers between devices, scatter_hop(): return (lax.ppermute(up, 'ctx', route), lax.ppermute(down, 'ctx', back))  73.4 us
    ppermute x11, waiting for transfers between devices, swap_exp(): lax.ppermute(block, 'exp', [(i, i ^ bit) for i in range(lax.axis_size('ex...  71.8 us
    all_to_all x4, waiting for transfers between devices, exchange(): lax.all_to_all(blocks, 'exp', split_axis=0, concat_axis=0, tiled=True)  45.1 us
    pallas_call x2, Pallas kernels, expert_weights(): pl.pallas_call(functools.partial(expert_weights_kernel, units, count), gr...  37.4 us
    ppermute x12, starting transfers between devices, scatter_hop(): return (lax.ppermute(up, 'ctx', route), lax.ppermute(down, 'ctx', back))  33.9 us
    pallas_call x1, Pallas kernels, attend(): pl.pallas_call(attend_kernel, grid=(pairs,), in_specs=[pl.BlockSpec((rows...  28.9 us
    ppermute x10, starting transfers between devices, shift_ctx(): return lax.ppermute(block, 'ctx', route)  27.4 us
  transfers between devices with their start and end apart: 46, of which 25 were waited for; matrix products, arithmetic and copies ran while one was open for 19% of the time, Pallas kernels for 29%

profile of v7, /device:TPU:0, one launch (start us, length us, event | category | flops | bytes accessed | tf_op | source)
XLA Modules:
  0.0 728.1 jit_solution(16512830933664757667)
XLA Ops:
  80.4 8.4 %collective-permute-done.8 = bf16[1,2,128,1024]{3,2,1,0:T(8,128)(2,1)S(1)} collective-permute-done((bf16[1,2,128,1024]{3,2,1,0:T(8,128)(2,1)S(1)}, bf16[1,2,128,1024]{3,2,1,0:T(8,128)(2,1)S(1)}, u32[]{:S(2)}, u32[]{:S(2)}) %collective-permute-start.8) | collective-permute-done | bytes 524320 | tf_op jit(solution)/shard_map/ppermute | solution.py:687
  106.7 7.0 bias_band.1.band_ref
  113.7 8.9 %collective-permute-done.11 = bf16[2,2,128,1024]{3,2,1,0:T(8,128)(2,1)S(1)} collective-permute-done((bf16[2,2,128,1024]{3,2,1,0:T(8,128)(2,1)}, bf16[2,2,128,1024]{3,2,1,0:T(8,128)(2,1)S(1)}, u32[]{:S(2)}, u32[]{:S(2)}) %collective-permute-start.11) | collective-permute-done | bytes 1048608 | tf_op jit(solution)/shard_map/ppermute | solution.py:687
  157.1 28.9 %attend.1 = (bf16[512,1024]{1,0:T(8,128)(2,1)}, f32[8,2,512]{2,1,0:T(2,128)}) custom-call(bf16[512,1024]{1,0:T(8,128)(2,1)} %fusion.23.q_ref, bf16[1536,1024]{1,0:T(8,128)(2,1)} %convolution_convert_fusion.3.k_ref, bf16[1536,1024]{1,0:T(8,128)(2,1)} %convolution_convert_fusion.2.v_ref, bf16[512,128]{1,0:T(8,128)(2,1)} %compare_convert_fusion.qdoc_ref, ...), custom_call_target="tpu_custom_call" | custom-call | flops 1048576 | bytes 1048576 | tf_op jit(solution)/shard_map/attend/pallas_call | solution.py:169
  209.3 18.3 %all-to-all-done.1 = bf16[8,160,1024]{2,1,0:T(8,128)(2,1)S(1)} async-done(((bf16[8,160,1024]{2,1,0:T(8,128)(2,1)}), bf16[8,160,1024]{2,1,0:T(8,128)(2,1)S(1)}, u32[]{:S(2)}, u32[]{:S(2)}) %all-to-all-start.1) | async-done | bytes 2621472 | tf_op jit(solution)/shard_map/all_to_all | solution.py:890
  227.7 10.4 %all-gather.4.cloned.1.call-done.refs_1_ = bf16[1024,3840]{1,0:T(8,128)(2,1)} async-done(((bf16[256,3840]{1,0:T(8,128)(2,1)}), bf16[1024,3840]{1,0:T(8,128)(2,1)}) %all-gather.4.cloned.1.call-update) | async-done | bytes 7864336 | tf_op jit(solution)/shard_map/all_gather | solution.py:968
  239.3 5.9 collective-permute-start.14
  246.5 32.9 %expert.2 = (bf16[1280,1280]{1,0:T(8,128)(2,1)}, bf16[1280,2560]{1,0:T(8,128)(2,1)}, bf16[1280,1024]{1,0:T(8,128)(2,1)}, f32[1280,128]{1,0:T(8,128)}, f32[1280,1024]{1,0:T(8,128)}, /*index=5*/f32[1280,1024]{1,0:T(8,128)}) custom-call(bf16[1280,1024]{1,0:T(8,128)(2,1)} %bitcast.176, bf16[1024,3840]{1,0:T(8,128)(2,1)} %all-gather.4.cloned.1.call-done.refs_1_, ...), custom_call_target="tpu_custom_call" | custom-call | flops 1048576 | bytes 1048576 | tf_op jit(solution)/shard_map/expert/pallas_call | solution.py:484
  279.3 17.4 %expert_weights.2 = bf16[1024,3840]{1,0:T(8,128)(2,1)} custom-call(bf16[1280,1024]{1,0:T(8,128)(2,1)} %bitcast.177, bf16[1280,1024]{1,0:T(8,128)(2,1)} %get-tuple-element.150.low_ref.refs_11_, bf16[1280,2560]{1,0:T(8,128)(2,1)} %get-tuple-element.103.dboth_ref, bf16[1280,1280]{1,0:T(8,128)(2,1)} %get-tuple-element.104.hidden_ref), custom_call_target="tpu_custom_call" | custom-call | flops 1048576 | bytes 1048576 | tf_op jit(solution)/shard_map/expert_weights/pallas_call | solution.py:561
  305.2 6.3 collective-permute-start.18
  311.5 16.9 %probs.1.probs_ref = bf16[16,2,1280,256]{3,2,1,0:T(8,128)(2,1)} custom-call(bf16[512,1024]{1,0:T(8,128)(2,1)} %fusion.23.q_ref, bf16[1536,1024]{1,0:T(8,128)(2,1)} %convolution_convert_fusion.3.k_ref, bf16[512,128]{1,0:T(8,128)(2,1)} %compare_convert_fusion.qdoc_ref, bf16[1536,128]{1,0:T(8,128)(2,1)} %select_convert_fusion.kdoc_ref, ...), custom_call_target="tpu_custom_call" | custom-call | flops 1048576 | bytes 1048576 | tf_op jit(solution)/shard_map/probs/pallas_call | solution.py:214
  331.6 20.1 %collective-permute-done.18 = bf16[256,3840]{1,0:T(8,128)(2,1)} collective-permute-done((bf16[256,3840]{1,0:T(8,128)(2,1)}, bf16[256,3840]{1,0:T(8,128)(2,1)}, u32[]{:S(2)}, u32[]{:S(2)}) %collective-permute-start.18) | collective-permute-done | bytes 1966112 | tf_op jit(solution)/shard_map/ppermute | solution.py:678
  365.2 40.1 %collective-permute-done.22 = bf16[256,3840]{1,0:T(8,128)(2,1)S(1)} collective-permute-done((bf16[256,3840]{1,0:T(8,128)(2,1)S(1)}, bf16[256,3840]{1,0:T(8,128)(2,1)S(1)}, u32[]{:S(2)}, u32[]{:S(2)}) %collective-permute-start.22) | collective-permute-done | bytes 1966112 | tf_op jit(solution)/shard_map/ppermute | solution.py:678
  413.4 41.1 %expert.3 = (bf16[1280,1536]{1,0:T(8,128)(2,1)}, bf16[1280,3072]{1,0:T(8,128)(2,1)}, bf16[1280,1024]{1,0:T(8,128)(2,1)}, bf16[1280,1024]{1,0:T(8,128)(2,1)}, f32[1024,128]{1,0:T(8,128)}) custom-call(bf16[1280,1024]{1,0:T(8,128)(2,1)} %bitcast.178, bf16[256,4608]{1,0:T(8,128)(2,1)} %maximum_dynamic-update-slice_fusion.refs_1_, ...), custom_call_target="tpu_custom_call" | custom-call | flops 1048576 | bytes 1048576 | tf_op jit(solution)/shard_map/expert/pallas_call | solution.py:484
  455.9 20.0 %expert_weights.3 = bf16[1024,4608]{1,0:T(8,128)(2,1)} custom-call(bf16[1280,1024]{1,0:T(8,128)(2,1)} %bitcast.179, bf16[1280,1024]{1,0:T(8,128)(2,1)} %get-tuple-element.150.low_ref.refs_11_, bf16[1280,3072]{1,0:T(8,128)(2,1)} %get-tuple-element.151.dboth_ref, bf16[1280,1536]{1,0:T(8,128)(2,1)} %get-tuple-element.152.hidden_ref), custom_call_target="tpu_custom_call" | custom-call | flops 12079595520 | bytes 1048576 | tf_op jit(solution)/shard_map/expert_weights/pallas_call | solution.py:561
  487.4 25.6 %all-to-all-done.2 = bf16[8,160,1024]{2,1,0:T(8,128)(2,1)} async-done(((bf16[8,160,1024]{2,1,0:T(8,128)(2,1)}), bf16[8,160,1024]{2,1,0:T(8,128)(2,1)}, u32[]{:S(2)}, u32[]{:S(2)}) %all-to-all-start.2) | async-done | bytes 2621472 | tf_op jit(solution)/shard_map/all_to_all | solution.py:890
  523.6 25.7 %attend_back.1 = (bf16[512,1024]{1,0:T(8,128)(2,1)}, bf16[1536,1024]{1,0:T(8,128)(2,1)}, bf16[1536,1024]{1,0:T(8,128)(2,1)}, f32[8,2,1024]{2,1,0:T(2,128)}) custom-call(bf16[512,1024]{1,0:T(8,128)(2,1)} %fusion.23.q_ref, bf16[1536,1024]{1,0:T(8,128)(2,1)} %convolution_convert_fusion.3.k_ref, bf16[1536,1024]{1,0:T(8,128)(2,1)} %convolution_convert_fusion.2.v_ref, ...), custom_call_target="tpu_custom_call" | custom-call | flops 21474836480 | bytes 1048576 | tf_op jit(solution)/shard_map/attend_back/pallas_call | solution.py:282
  549.3 16.2 %normed_grad.1 = (bf16[1024,1024]{1,0:T(8,128)(2,1)}, f32[512,1024]{1,0:T(8,128)}, f32[8,1024]{1,0:T(8,128)}) custom-call(bf16[1536,1024]{1,0:T(8,128)(2,1)} %copy-done.2, bf16[512,1024]{1,0:T(8,128)(2,1)} %get-tuple-element.133.q_ref, bf16[1536,1024]{1,0:T(8,128)(2,1)} %get-tuple-element.134.k_ref, bf16[1536,1024]{1,0:T(8,128)(2,1)} %get-tuple-element.135.v_ref, ...), custom_call_target="tpu_custom_call" | custom-call | flops 1048576 | bytes 1048576 | tf_op jit(solution)/shard_map/normed_grad/pallas_call | solution.py:798
  567.9 19.4 %slabs.1 = (bf16[16,144,1024]{2,1,0:T(8,128)(2,1)}, bf16[16,144,1024]{2,1,0:T(8,128)(2,1)}) custom-call(bf16[1536,1024]{1,0:T(8,128)(2,1)} %copy-done.4, bf16[512,1024]{1,0:T(8,128)(2,1)} %get-tuple-element.133.q_ref, bf16[1536,1024]{1,0:T(8,128)(2,1)} %get-tuple-element.134.k_ref, bf16[1536,1024]{1,0:T(8,128)(2,1)} %get-tuple-element.135.v_ref, ...), custom_call_target="tpu_custom_call" | custom-call | flops 1048576 | bytes 1048576 | tf_op jit(solution)/shard_map/slabs/pallas_call | solution.py:864
  595.6 6.2 add_convert_fusion
  607.8 40.5 %collective-permute-done.29 = bf16[2,2,144,1024]{3,2,0,1:T(8,128)(2,1)S(1)} collective-permute-done((bf16[2,2,144,1024]{3,2,0,1:T(8,128)(2,1)S(1)}, bf16[2,2,144,1024]{3,2,0,1:T(8,128)(2,1)S(1)}, u32[]{:S(2)}, u32[]{:S(2)}) %collective-permute-start.29) | collective-permute-done | bytes 1179680 | tf_op jit(solution)/shard_map/ppermute | solution.py:687
  658.3 7.0 collective-permute-done.30
  680.8 7.6 %expert_sums.1 = (f32[256,2816]{1,0:T(8,128)}, f32[256,2816]{1,0:T(8,128)}, f32[704,1024]{1,0:T(8,128)}) custom-call(bf16[256,3840]{1,0:T(8,128)(2,1)} %dynamic-slice_bitcast_fusion.2.own_ref, bf16[256,3840]{1,0:T(8,128)(2,1)} %copy-done.34, bf16[256,3840]{1,0:T(8,128)(2,1)} %collective-permute-done.25.down_ref, ...), custom_call_target="tpu_custom_call" | custom-call | flops 1048576 | bytes 1048576 | tf_op jit(solution)/shard_map/expert_sums/pallas_call | solution.py:615
  712.1 6.4 collective-permute-done.38
  (331 shorter events, 275.7 us)
Async XLA Ops:
  7.2 97.4 %all-gather.6.cloned.1.call-start = ((), (), s32[]{:S(2)}) async-start(), calls=%async_computation.7 | async-start | bytes 1081344 | tf_op jit(solution)/shard_map/all_gather | solution.py:949
  8.9 37.1 %collective-permute-start = (bf16[1,128,1024]{2,1,0:T(8,128)(2,1)}, bf16[1,128,1024]{2,1,0:T(8,128)(2,1)}, u32[]{:S(2)}, u32[]{:S(2)}) collective-permute-start(bf16[1,128,1024]{2,1,0:T(8,128)(2,1)} %maximum_bitcast_fusion.2), channel_id=1, source_target_pairs={{0,8},{8,16},{16,24},{1,9},{9,17},{17,25},{2,10},{10,18},{18,26},{... | collective-permute-start | bytes 786440 | tf_op jit(solution)/shard_map/ppermute | solution.py:30
  14.5 33.3 %collective-permute-start.1 = (bf16[1,128,1024]{2,1,0:T(8,128)(2,1)}, bf16[1,128,1024]{2,1,0:T(8,128)(2,1)}, u32[]{:S(2)}, u32[]{:S(2)}) collective-permute-start(bf16[1,128,1024]{2,1,0:T(8,128)(2,1)} %maximum_bitcast_fusion.2), channel_id=1, source_target_pairs={{8,0},{16,8},{24,16},{9,1},{17,9},{25,17},{10,2},{18,10},{26,18},{... | collective-permute-start | bytes 786440 | tf_op jit(solution)/shard_map/ppermute | solution.py:30
  18.1 53.3 %collective-permute-start.6 = (bf16[512,1024]{1,0:T(8,128)(2,1)}, bf16[512,1024]{1,0:T(8,128)(2,1)}, u32[]{:S(2)}, u32[]{:S(2)}) collective-permute-start(bf16[512,1024]{1,0:T(8,128)(2,1)} %bitcast.184), channel_id=1, source_target_pairs={{0,8},{8,16},{16,24},{1,9},{9,17},{17,25},{2,10},{10,18},{18,26},{... | collective-permute-start | bytes 3145736 | tf_op jit(solution)/shard_map/ppermute | solution.py:30
  30.3 42.3 %all-to-all-start = ((bf16[8,160,1152]{2,1,0:T(8,128)(2,1)}), bf16[8,160,1152]{2,1,0:T(8,128)(2,1)S(1)}, u32[]{:S(2)}, u32[]{:S(2)}) async-start(bf16[8,160,1152]{2,1,0:T(8,128)(2,1)} %bitcast.203), calls=%async_computation | async-start | bytes 5898240 | tf_op jit(solution)/shard_map/all_to_all | solution.py:890
  34.0 204.1 %all-gather.4.cloned.1.call-start = ((), (), s32[]{:S(2)}) async-start(), calls=%async_computation.5 | async-start | bytes 9830400 | tf_op jit(solution)/shard_map/all_gather | solution.py:968
  191.8 35.8 %all-to-all-start.1 = ((bf16[8,160,1024]{2,1,0:T(8,128)(2,1)}), bf16[8,160,1024]{2,1,0:T(8,128)(2,1)S(1)}, u32[]{:S(2)}, u32[]{:S(2)}) async-start(bf16[8,160,1024]{2,1,0:T(8,128)(2,1)} %bitcast.206), calls=%async_computation.1 | async-start | bytes 5242880 | tf_op jit(solution)/shard_map/all_to_all | solution.py:890
  195.5 485.3 %reduce-scatter.2.cloned.1.call-start = ((), (), s32[]{:S(2)}) async-start(), calls=%async_computation.6 | async-start | bytes 11796480 | tf_op jit(solution)/shard_map/reduce_scatter | solution.py:1026
  238.0 58.7 %collective-permute-start.15 = (bf16[256,4608]{1,0:T(8,128)(2,1)}, bf16[256,4608]{1,0:T(8,128)(2,1)}, u32[]{:S(2)}, u32[]{:S(2)}) collective-permute-start(bf16[256,4608]{1,0:T(8,128)(2,1)} %maximum_dynamic-update-slice_fusion.refs_1_), channel_id=1, source_target_pairs={{24,16},{16,8},{8,0},{25,17},{17,9},{9,1},{26,18},{18,10},{10,2},{... | collective-permute-start | bytes 7077896 | tf_op jit(solution)/shard_map/ppermute | solution.py:658
  239.3 57.4 %collective-permute-start.14 = (bf16[256,4608]{1,0:T(8,128)(2,1)}, bf16[256,4608]{1,0:T(8,128)(2,1)}, u32[]{:S(2)}, u32[]{:S(2)}) collective-permute-start(bf16[256,4608]{1,0:T(8,128)(2,1)} %maximum_dynamic-update-slice_fusion.refs_1_), channel_id=1, source_target_pairs={{0,8},{8,16},{16,24},{1,9},{9,17},{17,25},{2,10},{10,18},{18,26},{... | collective-permute-start | bytes 7077896 | tf_op jit(solution)/shard_map/ppermute | solution.py:658
  296.7 55.0 %collective-permute-start.16 = (bf16[256,4608]{1,0:T(8,128)(2,1)}, bf16[256,4608]{1,0:T(8,128)(2,1)S(1)}, u32[]{:S(2)}, u32[]{:S(2)}) collective-permute-start(bf16[256,4608]{1,0:T(8,128)(2,1)} %collective-permute-done.14.refs_2_), channel_id=1, source_target_pairs={{8,16},{16,24},{9,17},{17,25},{10,18},{18,26},{11,19},{19,27},{12,... | collective-permute-start | bytes 7077896 | tf_op jit(solution)/shard_map/ppermute | solution.py:658
  297.6 55.0 %collective-permute-start.17 = (bf16[256,4608]{1,0:T(8,128)(2,1)}, bf16[256,4608]{1,0:T(8,128)(2,1)S(1)}, u32[]{:S(2)}, u32[]{:S(2)}) collective-permute-start(bf16[256,4608]{1,0:T(8,128)(2,1)} %collective-permute-done.15.refs_3_), channel_id=1, source_target_pairs={{16,8},{8,0},{17,9},{9,1},{18,10},{10,2},{19,11},{11,3},{20,12},{1... | collective-permute-start | bytes 7077896 | tf_op jit(solution)/shard_map/ppermute | solution.py:658
  303.2 28.4 %collective-permute-start.19 = (bf16[256,3840]{1,0:T(8,128)(2,1)}, bf16[256,3840]{1,0:T(8,128)(2,1)}, u32[]{:S(2)}, u32[]{:S(2)}) collective-permute-start(bf16[256,3840]{1,0:T(8,128)(2,1)} %get-tuple-element.210), channel_id=1, source_target_pairs={{24,16},{25,17},{26,18},{27,19},{28,20},{29,21},{30,22},{31,23}} | collective-permute-start | bytes 5898248 | tf_op jit(solution)/shard_map/ppermute | solution.py:678
  305.2 46.5 %collective-permute-start.18 = (bf16[256,3840]{1,0:T(8,128)(2,1)}, bf16[256,3840]{1,0:T(8,128)(2,1)}, u32[]{:S(2)}, u32[]{:S(2)}) collective-permute-start(bf16[256,3840]{1,0:T(8,128)(2,1)} %get-tuple-element.211), channel_id=1, source_target_pairs={{0,8},{1,9},{2,10},{3,11},{4,12},{5,13},{6,14},{7,15}} | collective-permute-start | bytes 5898248 | tf_op jit(solution)/shard_map/ppermute | solution.py:678
  352.6 52.8 %collective-permute-start.20 = (bf16[256,4608]{1,0:T(8,128)(2,1)S(1)}, bf16[256,4608]{1,0:T(8,128)(2,1)S(1)}, u32[]{:S(2)}, u32[]{:S(2)}) collective-permute-start(bf16[256,4608]{1,0:T(8,128)(2,1)S(1)} %collective-permute-done.16.refs_4_), channel_id=1, source_target_pairs={{16,24},{17,25},{18,26},{19,27},{20,28},{21,29},{22,30},{23,31}} | collective-permute-start | bytes 7077896 | tf_op jit(solution)/shard_map/ppermute | solution.py:658
  353.4 53.4 %collective-permute-start.21 = (bf16[256,4608]{1,0:T(8,128)(2,1)S(1)}, bf16[256,4608]{1,0:T(8,128)(2,1)S(1)}, u32[]{:S(2)}, u32[]{:S(2)}) collective-permute-start(bf16[256,4608]{1,0:T(8,128)(2,1)S(1)} %collective-permute-done.17.refs_5_), channel_id=1, source_target_pairs={{8,0},{9,1},{10,2},{11,3},{12,4},{13,5},{14,6},{15,7}} | collective-permute-start | bytes 7077896 | tf_op jit(solution)/shard_map/ppermute | solution.py:658
  359.9 45.5 %collective-permute-start.22 = (bf16[256,3840]{1,0:T(8,128)(2,1)S(1)}, bf16[256,3840]{1,0:T(8,128)(2,1)S(1)}, u32[]{:S(2)}, u32[]{:S(2)}) collective-permute-start(bf16[256,3840]{1,0:T(8,128)(2,1)S(1)} %get-tuple-element.209), channel_id=1, source_target_pairs={{0,8},{8,16},{1,9},{9,17},{2,10},{10,18},{3,11},{11,19},{4,12},{12... | collective-permute-start | bytes 5898248 | tf_op jit(solution)/shard_map/ppermute | solution.py:678
  408.1 46.3 %collective-permute-start.24 = (bf16[256,3840]{1,0:T(8,128)(2,1)S(1)}, bf16[256,3840]{1,0:T(8,128)(2,1)S(1)}, u32[]{:S(2)}, u32[]{:S(2)}) collective-permute-start(bf16[256,3840]{1,0:T(8,128)(2,1)S(1)} %get-tuple-element.127), channel_id=1, source_target_pairs={{0,8},{8,16},{16,24},{1,9},{9,17},{17,25},{2,10},{10,18},{18,26},{... | collective-permute-start | bytes 5898248 | tf_op jit(solution)/shard_map/ppermute | solution.py:678
  412.1 43.8 %collective-permute-start.25 = (bf16[256,3840]{1,0:T(8,128)(2,1)S(1)}, bf16[256,3840]{1,0:T(8,128)(2,1)}, u32[]{:S(2)}, u32[]{:S(2)}) collective-permute-start(bf16[256,3840]{1,0:T(8,128)(2,1)S(1)} %get-tuple-element.128), channel_id=1, source_target_pairs={{24,16},{16,8},{8,0},{25,17},{17,9},{9,1},{26,18},{18,10},{10,2},{... | collective-permute-start | bytes 5898248 | tf_op jit(solution)/shard_map/ppermute | solution.py:678
  475.9 37.0 %all-to-all-start.2 = ((bf16[8,160,1024]{2,1,0:T(8,128)(2,1)}), bf16[8,160,1024]{2,1,0:T(8,128)(2,1)}, u32[]{:S(2)}, u32[]{:S(2)}) async-start(bf16[8,160,1024]{2,1,0:T(8,128)(2,1)} %bitcast.205), calls=%async_computation.2 | async-start | bytes 5242880 | tf_op jit(solution)/shard_map/all_to_all | solution.py:890
  587.4 66.0 %all-to-all-start.3 = ((bf16[8,160,1024]{2,1,0:T(8,128)(2,1)}), bf16[8,160,1024]{2,1,0:T(8,128)(2,1)}, u32[]{:S(2)}, u32[]{:S(2)}) async-start(bf16[8,160,1024]{2,1,0:T(8,128)(2,1)} %bitcast.204), calls=%async_computation.3 | async-start | bytes 5242880 | tf_op jit(solution)/shard_map/all_to_all | solution.py:890
  602.9 45.4 %collective-permute-start.29 = (bf16[2,2,144,1024]{3,2,0,1:T(8,128)(2,1)S(1)}, bf16[2,2,144,1024]{3,2,0,1:T(8,128)(2,1)S(1)}, u32[]{:S(2)}, u32[]{:S(2)}) collective-permute-start(bf16[2,2,144,1024]{3,2,0,1:T(8,128)(2,1)S(1)} %select_bitcast_fusion), channel_id=1, source_target_pairs={{0,4},{1,5},{2,6},{3,7},{4,0},{5,1},{6,2},{7,3},{8,12},{9,13},{10,... | collective-permute-start | bytes 3538952 | tf_op jit(solution)/shard_map/ppermute | solution.py:687
  603.8 47.5 %collective-permute-start.27 = (bf16[2,2,144,1024]{3,2,0,1:T(8,128)(2,1)S(1)}, bf16[2,2,144,1024]{3,2,0,1:T(8,128)(2,1)S(1)}, u32[]{:S(2)}, u32[]{:S(2)}) collective-permute-start(bf16[2,2,144,1024]{3,2,0,1:T(8,128)(2,1)S(1)} %select_bitcast_fusion.1), channel_id=1, source_target_pairs={{0,2},{1,3},{2,0},{3,1},{4,6},{5,7},{6,4},{7,5},{8,10},{9,11},{10,... | collective-permute-start | bytes 3538952 | tf_op jit(solution)/shard_map/ppermute | solution.py:687
  606.3 63.6 %collective-permute-start.31 = (bf16[512,1024]{1,0:T(8,128)(2,1)}, bf16[512,1024]{1,0:T(8,128)(2,1)}, u32[]{:S(2)}, u32[]{:S(2)}) collective-permute-start(bf16[512,1024]{1,0:T(8,128)(2,1)} %slice.278), channel_id=1, source_target_pairs={{8,0},{16,8},{24,16},{9,1},{17,9},{25,17},{10,2},{18,10},{26,18},{... | collective-permute-start | bytes 3145736 | tf_op jit(solution)/shard_map/ppermute | solution.py:30
  (78 other events, 941.2 us)
Sparse Core Ops, SparseCore 0:
  18.2 60.8 all-gather.5
  96.6 141.4 all-gather.3
  476.0 185.2 reduce-scatter.1
